TPU v7x, 128 devices: a whole 4x4x4 slice. The times are simulated.
128 devices in a mesh: ctx: 8 (over y_lo, z), head: 16 (over y_hi, x, core).
Axes of the slice: x: 4, y: 4 (y_hi: 2, y_lo: 2; y = y_hi * 2 + y_lo), z: 4, core: 2. Of those that a mesh axis runs over, the one named last changes fastest.
Arguments:
- queries: bfloat16 [4096, 8192], P('ctx', 'head'), may hold values from -108 to 108
- key_heads: bfloat16 [4096, 1024], P('ctx'), may hold values from -4.5 to 4.5
- values: bfloat16 [4096, 1024], P('ctx'), may hold values from -6 to 6
- log_decay: float32 [4096, 64], P('ctx', 'head'), may hold values from -1 to 0, as said below
- write_strength: float32 [4096, 64], P('ctx', 'head'), may hold values from 0.1 to 0.9
- query_map: bfloat16 [64, 128, 128], P('head'), may hold values from -0.5 to 0.5
- key_map: bfloat16 [64, 128, 128], P('head'), may hold values from -0.5 to 0.5
- out_weight: bfloat16 [8192, 8192], P('head'), may hold values from -0.09375 to 0.09375
Outputs:
- mean_square: float32 [], replicated
- query_map_grad: float32 [64, 128, 128], P('head')
- key_map_grad: float32 [64, 128, 128], P('head')
Inputs may be any that keep to these rules, and one draw needn't show every extreme that they name: `log_decay`: log decays are negative.
All inputs are finite; a program needn't handle non-finite values.
Results may differ from a plain program's by a relative error of at most 0.0024.
Values may be sent and summed in bfloat16 or wider, within the bound.
No kernel may reach another device: no remote copies, remote signals or barrier semaphores. Data moves between devices by JAX's collectives and lax.ppermute only.
A program may use at most 192 MiB of HBM per device.

v0:
```python
import math

import jax
import jax.numpy as jnp
from jax import lax
from jax.sharding import PartitionSpec as P

D = 8192
QUERY_HEAD_COUNT = 64
KVH = 8
HD = 128
SPAN = 64


BEST_PRECISION = lax.Precision.HIGHEST


def shifted(shard, axis, by):
    length = lax.axis_size(axis)
    pairs = [(i, i + by) for i in range(length) if 0 <= i + by < length]
    return lax.ppermute(shard, axis, pairs)


def unit_rows(vector):
    return vector / jnp.sqrt(jnp.sum(vector * vector, axis=-1, keepdims=True) + 1e-06)


def span_step(state, inputs):
    query_block, key_block, value_block, gate_block, write_block = inputs
    block_len = query_block.shape[1]
    state_width = state.shape[2]
    cumulative = jnp.cumsum(gate_block, axis=1)
    position = jnp.arange(block_len)
    strict = position[:, None] > position[None, :]
    inclusive = position[:, None] >= position[None, :]
    log_gap = cumulative[:, :, None] - cumulative[:, None, :]
    decay_strict = jnp.where(strict, jnp.exp(jnp.where(strict, log_gap, 0.0)), 0.0)
    decay_inclusive = jnp.where(inclusive, jnp.exp(jnp.where(inclusive, log_gap, 0.0)), 0.0)
    key_gram = jnp.einsum("hid,hjd->hij", key_block, key_block, precision=BEST_PRECISION)
    system = write_block[:, :, None] * decay_strict * key_gram + jnp.eye(
        block_len, dtype=key_block.dtype
    )
    growth = jnp.exp(cumulative)
    right_side = jnp.concatenate(
        [write_block[:, :, None] * value_block, (write_block * growth)[:, :, None] * key_block],
        axis=2,
    )
    solved = jax.scipy.linalg.solve_triangular(system, right_side, lower=True, unit_diagonal=True)
    updates = solved[:, :, :state_width] - jnp.einsum(
        "hcd,hdw->hcw", solved[:, :, state_width:], state, precision=BEST_PRECISION
    )
    query_key = jnp.einsum("hid,hjd->hij", query_block, key_block, precision=BEST_PRECISION)
    outputs = growth[:, :, None] * jnp.einsum(
        "hcd,hdw->hcw", query_block, state, precision=BEST_PRECISION
    )
    outputs = outputs + jnp.einsum(
        "hij,hjw->hiw", decay_inclusive * query_key, updates, precision=BEST_PRECISION
    )
    tail_decay = jnp.exp(cumulative[:, -1:] - cumulative)
    new_state = growth[:, -1][:, None, None] * state + jnp.einsum(
        "hcd,hcw->hdw", key_block * tail_decay[:, :, None], updates, precision=BEST_PRECISION
    )
    return (new_state, outputs)


def run_spans(state, unit_query, unit_key, value_rows, gates, writes, block_len):
    head_count = unit_query.shape[0]
    length = unit_query.shape[1]
    block_count = length // block_len

    def to_blocks(tensor):
        return jnp.moveaxis(
            tensor.reshape((head_count, block_count, block_len) + tensor.shape[2:]), 1, 0
        )

    last_state, outputs = lax.scan(
        span_step,
        state,
        (
            to_blocks(unit_query),
            to_blocks(unit_key),
            to_blocks(value_rows),
            to_blocks(gates),
            to_blocks(writes),
        ),
    )
    outputs = jnp.moveaxis(outputs, 0, 1).reshape(head_count, length, outputs.shape[-1])
    return (last_state, outputs)


def shards(queries, key_heads, values, log_decay, write_strength, query_map, key_map, out_weight):
    row_count = queries.shape[0]
    head_count = query_map.shape[0]
    group_size = QUERY_HEAD_COUNT // KVH
    first_head = lax.axis_index("head") * head_count
    kv_column = first_head // group_size * HD
    key_mine = lax.dynamic_slice_in_dim(key_heads, kv_column, HD, 1)
    value_mine = lax.dynamic_slice_in_dim(values, kv_column, HD, 1)
    query_split = queries.reshape(row_count, head_count, HD).transpose(1, 0, 2)
    query_position = lax.axis_index("ctx") * row_count + jnp.arange(row_count)
    running_max = jnp.full((head_count, row_count), -jnp.inf, jnp.float32)
    running_sum = jnp.zeros((head_count, row_count), jnp.float32)
    weighted = jnp.zeros((head_count, row_count, HD), jnp.float32)
    key_piece = lax.all_gather(key_mine, "ctx", axis=0, tiled=True)
    value_piece = lax.all_gather(value_mine, "ctx", axis=0, tiled=True)
    scores = jnp.einsum(
        "hqd,kd->hqk", query_split, key_piece, preferred_element_type=jnp.float32
    ) / math.sqrt(HD)
    key_position = jnp.arange(key_piece.shape[0])
    allowed = key_position[None, :] <= query_position[:, None]
    scores = jnp.where(allowed[None], scores, -jnp.inf)
    new_max = jnp.max(scores, axis=2)
    safe_max = jnp.where(jnp.isfinite(new_max), new_max, 0.0)
    rescale = jnp.exp(running_max - safe_max)
    weights = jnp.exp(scores - safe_max[:, :, None])
    running_sum = running_sum * rescale + jnp.sum(weights, axis=2)
    weighted = weighted * rescale[:, :, None] + jnp.einsum(
        "hqk,kd->hqd", weights.astype(jnp.bfloat16), value_piece, preferred_element_type=jnp.float32
    )
    running_max, running_sum, weighted = (new_max, running_sum, weighted)
    teacher = (weighted / running_sum[:, :, None]).astype(jnp.bfloat16)
    query_float = query_split.astype(jnp.float32)
    key_float = key_mine.astype(jnp.float32)
    value_float = jnp.broadcast_to(value_mine.astype(jnp.float32), (head_count, row_count, HD))
    gates = log_decay.T
    writes = write_strength.T
    projected_query = jnp.einsum(
        "hrd,hde->hre", query_split, query_map, preferred_element_type=jnp.float32
    )
    projected_key = jnp.einsum("rd,hde->hre", key_mine, key_map, preferred_element_type=jnp.float32)

    def local_pass(state_in, proj_query, proj_key):
        return run_spans(
            state_in, unit_rows(proj_query), unit_rows(proj_key), value_float, gates, writes, SPAN
        )

    unit_query = unit_rows(projected_query)
    unit_key = unit_rows(projected_key)
    identity = jnp.broadcast_to(jnp.eye(HD, dtype=jnp.float32), (head_count, HD, HD))
    zero_state = jnp.zeros((head_count, HD, HD), jnp.float32)
    summary_start = jnp.concatenate([identity, zero_state], axis=2)
    summary_values = jnp.concatenate([jnp.zeros_like(value_float), value_float], axis=2)
    summary, unused_out = run_spans(
        summary_start, unit_query, unit_key, summary_values, gates, writes, SPAN
    )
    carry_map = summary[:, :, :HD]
    carry_add = summary[:, :, HD:]
    state_in = zero_state
    for section in range(lax.axis_size("ctx") - 1):
        state_out = (
            jnp.einsum("hij,hjk->hik", carry_map, state_in, precision=BEST_PRECISION) + carry_add
        )
        state_in = shifted(state_out, "ctx", 1)
    (state_end, student_out), pullback = jax.vjp(
        local_pass, state_in, projected_query, projected_key
    )
    delta_heads = student_out - teacher.astype(jnp.float32)
    weight_float = out_weight.astype(jnp.float32)
    delta_columns = delta_heads.transpose(0, 2, 1).reshape(head_count * HD, row_count)
    columns = weight_float
    difference = lax.psum_scatter(
        jnp.einsum("fc,fr->cr", columns, delta_columns, precision=BEST_PRECISION),
        "head",
        scatter_dimension=0,
        tiled=True,
    )
    square_part = jnp.sum(difference * difference)
    columns = weight_float
    grad_columns = jnp.dot(
        columns, lax.all_gather(difference, "head", axis=0, tiled=True), precision=BEST_PRECISION
    )
    head_grad = grad_columns.reshape(head_count, HD, row_count).transpose(0, 2, 1)
    local_grad, unused_query, unused_key = pullback((jnp.zeros_like(state_end), head_grad))
    back_map = jnp.swapaxes(carry_map, 1, 2)
    state_grad = zero_state
    for section in range(lax.axis_size("ctx") - 1):
        grad_in = (
            jnp.einsum("hij,hjk->hik", back_map, state_grad, precision=BEST_PRECISION) + local_grad
        )
        state_grad = shifted(grad_in, "ctx", -1)
    unused_state, proj_query_grad, proj_key_grad = pullback((state_grad, head_grad))
    query_grad = jnp.einsum("hrd,hre->hde", query_float, proj_query_grad, precision=BEST_PRECISION)
    key_grad = jnp.einsum("rd,hre->hde", key_float, proj_key_grad, precision=BEST_PRECISION)
    normalizer = row_count * lax.axis_size("ctx") * D
    total_square = lax.psum(square_part, ("ctx", "head"))
    query_grad, key_grad = lax.psum((query_grad, key_grad), "ctx")
    return (total_square / normalizer, query_grad, key_grad)


def solution(mesh):
    placed = (
        P("ctx", "head"),
        P("ctx", None),
        P("ctx", None),
        P("ctx", "head"),
        P("ctx", "head"),
        P("head", None, None),
        P("head", None, None),
        P("head", None),
    )
    return jax.shard_map(
        shards,
        mesh=mesh,
        in_specs=placed,
        out_specs=(P(), P("head", None, None), P("head", None, None)),
        check_vma=False,
    )
```

profile of v0, /device:TPU:0, one launch (start us, length us, event | category | flops | bytes accessed | tf_op | source)
XLA Modules:
  0.0 1424.8 jit_solution(2075704569445246741)
XLA Ops:
  16.2 190.3 %while.86 = (s32[]{:T(128)}, f32[4,128,256]{2,1,0:T(8,128)S(1)}, f32[8,4,64]{2,1,0:T(4,128)S(1)}, f32[8,4,64,128]{3,2,1,0:T(8,128)S(1)}, f32[8,4,64]{2,1,0:T(4,1...) while((s32[]{:T(128)}, f32[4,128,256]{2,1,0:T(8,128)S(1)}, f32[8,4,64]{2,1,0:T(4,128)S(1)}, ...), condition=%wide.region_3.4_spmd, body=%wide.region_1.3_spmd.sunk | while | flops 302719296 | bytes 4601025 | solution.py:76
  17.2 19.7 %custom-call.42 = f32[4,1,64,64]{2,3,1,0:T(8,128)S(1)} custom-call(f32[4,1,64,64]{3,2,1,0:T(8,128)S(1)} %fusion.341), custom_call_target="InvertDiagBlocksLowerTriangular" | custom-call | tf_op jit(solution)/shard_map/while/body/eval_jaxpr/jit(_solve_triangular)/vmap()/triangular_solve | solution.py:48
  41.0 19.7 %custom-call.42 = f32[4,1,64,64]{2,3,1,0:T(8,128)S(1)} custom-call(f32[4,1,64,64]{3,2,1,0:T(8,128)S(1)} %fusion.341), custom_call_target="InvertDiagBlocksLowerTriangular" | custom-call | tf_op jit(solution)/shard_map/while/body/eval_jaxpr/jit(_solve_triangular)/vmap()/triangular_solve | solution.py:48
  64.7 19.7 %custom-call.42 = f32[4,1,64,64]{2,3,1,0:T(8,128)S(1)} custom-call(f32[4,1,64,64]{3,2,1,0:T(8,128)S(1)} %fusion.341), custom_call_target="InvertDiagBlocksLowerTriangular" | custom-call | tf_op jit(solution)/shard_map/while/body/eval_jaxpr/jit(_solve_triangular)/vmap()/triangular_solve | solution.py:48
  88.5 19.7 %custom-call.42 = f32[4,1,64,64]{2,3,1,0:T(8,128)S(1)} custom-call(f32[4,1,64,64]{3,2,1,0:T(8,128)S(1)} %fusion.341), custom_call_target="InvertDiagBlocksLowerTriangular" | custom-call | tf_op jit(solution)/shard_map/while/body/eval_jaxpr/jit(_solve_triangular)/vmap()/triangular_solve | solution.py:48
  112.3 19.7 %custom-call.42 = f32[4,1,64,64]{2,3,1,0:T(8,128)S(1)} custom-call(f32[4,1,64,64]{3,2,1,0:T(8,128)S(1)} %fusion.341), custom_call_target="InvertDiagBlocksLowerTriangular" | custom-call | tf_op jit(solution)/shard_map/while/body/eval_jaxpr/jit(_solve_triangular)/vmap()/triangular_solve | solution.py:48
  136.1 19.7 %custom-call.42 = f32[4,1,64,64]{2,3,1,0:T(8,128)S(1)} custom-call(f32[4,1,64,64]{3,2,1,0:T(8,128)S(1)} %fusion.341), custom_call_target="InvertDiagBlocksLowerTriangular" | custom-call | tf_op jit(solution)/shard_map/while/body/eval_jaxpr/jit(_solve_triangular)/vmap()/triangular_solve | solution.py:48
  159.9 19.7 %custom-call.42 = f32[4,1,64,64]{2,3,1,0:T(8,128)S(1)} custom-call(f32[4,1,64,64]{3,2,1,0:T(8,128)S(1)} %fusion.341), custom_call_target="InvertDiagBlocksLowerTriangular" | custom-call | tf_op jit(solution)/shard_map/while/body/eval_jaxpr/jit(_solve_triangular)/vmap()/triangular_solve | solution.py:48
  183.7 19.7 %custom-call.42 = f32[4,1,64,64]{2,3,1,0:T(8,128)S(1)} custom-call(f32[4,1,64,64]{3,2,1,0:T(8,128)S(1)} %fusion.341), custom_call_target="InvertDiagBlocksLowerTriangular" | custom-call | tf_op jit(solution)/shard_map/while/body/eval_jaxpr/jit(_solve_triangular)/vmap()/triangular_solve | solution.py:48
  206.8 3.9 collective-permute-start
  210.8 5.5 collective-permute-done
  216.7 4.4 collective-permute-start.1
  221.1 4.7 collective-permute-done.1
  226.2 4.4 collective-permute-start.2
  230.7 3.8 collective-permute-done.2
  234.8 4.4 collective-permute-start.3
  239.2 3.0 iota_compare_fusion.9
  243.5 4.4 collective-permute-start.4
  249.6 3.7 collective-permute-done.4
  253.8 7.0 collective-permute-start.5
  261.2 6.2 collective-permute-done.5
  267.8 5.8 collective-permute-start.6
  273.7 15.2 %fusion.174 = (f32[4,512]{1,0:T(4,128)S(1)}, f32[4096,4,512]{2,0,1:T(8,128)}) fusion(pred[512,4096]{0,1:T(8,128)(4,1)} %iota_compare_fusion.9, bf16[4096,128]{1,0:T(8,128)(2,1)} %all-gather.4.cloned.1.call-done, bf16[512,512]{1,0:T(8,128)(2,1)} %param.16), kind=kOutput, calls=%fused_computation.250 | convolution fusion | flops 2172647424 | bytes 37232640 | tf_op jit(solution)/shard_map/hqd,kd->hqk/dot_general | solution.py:106
  293.3 245.6 %while.88 = (s32[]{:T(128)}, f32[4,128,128]{2,1,0:T(8,128)S(1)}, f32[8,4,64,128]{3,2,0,1:T(8,128)}, f32[8,4,64,64]{3,2,1,0:T(8,128)}, f32[8,4,64,1]{2,1,3,0:T(4,...) while((s32[]{:T(128)}, f32[4,128,128]{2,1,0:T(8,128)S(1)}, ...), condition=%wide.region_7.8_spmd.clone.clone, body=%wide.region_5.7_spmd.clone.clone.sunk | while | flops 277582656 | bytes 6336841 | solution.py:76
  295.0 19.7 %custom-call.44 = f32[4,1,64,64]{2,3,1,0:T(8,128)S(1)} custom-call(f32[4,1,64,64]{3,2,1,0:T(8,128)S(1)} %add_bitcast_fusion.5), custom_call_target="InvertDiagBlocksLowerTriangular" | custom-call | tf_op jit(solution)/shard_map/jvp()/while/body/eval_jaxpr/jit(_solve_triangular)/vmap()/triangular_solve | solution.py:48
  325.7 19.7 %custom-call.44 = f32[4,1,64,64]{2,3,1,0:T(8,128)S(1)} custom-call(f32[4,1,64,64]{3,2,1,0:T(8,128)S(1)} %add_bitcast_fusion.5), custom_call_target="InvertDiagBlocksLowerTriangular" | custom-call | tf_op jit(solution)/shard_map/jvp()/while/body/eval_jaxpr/jit(_solve_triangular)/vmap()/triangular_solve | solution.py:48
  356.3 19.7 %custom-call.44 = f32[4,1,64,64]{2,3,1,0:T(8,128)S(1)} custom-call(f32[4,1,64,64]{3,2,1,0:T(8,128)S(1)} %add_bitcast_fusion.5), custom_call_target="InvertDiagBlocksLowerTriangular" | custom-call | tf_op jit(solution)/shard_map/jvp()/while/body/eval_jaxpr/jit(_solve_triangular)/vmap()/triangular_solve | solution.py:48
  387.1 19.7 %custom-call.44 = f32[4,1,64,64]{2,3,1,0:T(8,128)S(1)} custom-call(f32[4,1,64,64]{3,2,1,0:T(8,128)S(1)} %add_bitcast_fusion.5), custom_call_target="InvertDiagBlocksLowerTriangular" | custom-call | tf_op jit(solution)/shard_map/jvp()/while/body/eval_jaxpr/jit(_solve_triangular)/vmap()/triangular_solve | solution.py:48
  417.7 19.7 %custom-call.44 = f32[4,1,64,64]{2,3,1,0:T(8,128)S(1)} custom-call(f32[4,1,64,64]{3,2,1,0:T(8,128)S(1)} %add_bitcast_fusion.5), custom_call_target="InvertDiagBlocksLowerTriangular" | custom-call | tf_op jit(solution)/shard_map/jvp()/while/body/eval_jaxpr/jit(_solve_triangular)/vmap()/triangular_solve | solution.py:48
  448.4 19.7 %custom-call.44 = f32[4,1,64,64]{2,3,1,0:T(8,128)S(1)} custom-call(f32[4,1,64,64]{3,2,1,0:T(8,128)S(1)} %add_bitcast_fusion.5), custom_call_target="InvertDiagBlocksLowerTriangular" | custom-call | tf_op jit(solution)/shard_map/jvp()/while/body/eval_jaxpr/jit(_solve_triangular)/vmap()/triangular_solve | solution.py:48
  479.1 19.7 %custom-call.44 = f32[4,1,64,64]{2,3,1,0:T(8,128)S(1)} custom-call(f32[4,1,64,64]{3,2,1,0:T(8,128)S(1)} %add_bitcast_fusion.5), custom_call_target="InvertDiagBlocksLowerTriangular" | custom-call | tf_op jit(solution)/shard_map/jvp()/while/body/eval_jaxpr/jit(_solve_triangular)/vmap()/triangular_solve | solution.py:48
  509.8 19.7 %custom-call.44 = f32[4,1,64,64]{2,3,1,0:T(8,128)S(1)} custom-call(f32[4,1,64,64]{3,2,1,0:T(8,128)S(1)} %add_bitcast_fusion.5), custom_call_target="InvertDiagBlocksLowerTriangular" | custom-call | tf_op jit(solution)/shard_map/jvp()/while/body/eval_jaxpr/jit(_solve_triangular)/vmap()/triangular_solve | solution.py:48
  538.9 2.9 copy.48
  541.8 14.6 %fusion.172 = f32[4,512]{1,0:T(4,128)S(1)} fusion(f32[4096,4,512]{2,0,1:T(8,128)} %get-tuple-element.1380, f32[4,512]{1,0:T(4,128)S(1)} %is-finite_select_fusion, pred[512,4096]{0,1:T(8,128)(4,1)} %iota_compare_fusion.9), kind=kLoop, calls=%fused_computation.248 | loop fusion | flops 33552384 | bytes 35667968 | tf_op jit(solution)/shard_map/reduce_sum | solution.py:116
  556.5 15.8 %divide_convert_fusion = bf16[4,512,128]{1,2,0:T(8,128)(2,1)S(1)} fusion(f32[4096,4,512]{2,0,1:T(8,128)} %get-tuple-element.1380, f32[4,512]{1,0:T(4,128)S(1)} %is-finite_select_fusion, pred[512,4096]{0,1:T(8,128)(4,1)} %iota_compare_fusion.9, bf16[4096,128]{0,1:T(8,128)(2,1)} %all-gather.6.cloned.1.call-done, f32[4,512]{1,0:T(4,128)S(1)} %get-tuple-element.1374, ...), kind=kOutput, calls=%fused_computation.292 | convolution fusion | flops 2181824512 | bytes 37249024 | tf_op jit(solution)/shard_map/hqk,kd->hqd/dot_general | solution.py:117
  572.5 19.1 %convolution_bitcast_fusion = f32[8192,512]{0,1:T(8,128)} fusion(f32[512,512]{1,0:T(8,128)S(1)} %bitcast.482, bf16[512,8192]{1,0:T(8,128)(2,1)} %param.23), kind=kOutput, calls=%fused_computation.253 | convolution fusion | flops 25769803776 | bytes 26214400 | tf_op jit(solution)/shard_map/fc,fr->cr/dot_general | solution.py:162
  591.6 158.2 %reduce-scatter.2.cloned.1.call-done = f32[512,512]{0,1:T(8,128)} async-done(((f32[8192,512]{0,1:T(8,128)}), f32[512,512]{0,1:T(8,128)}) %reduce-scatter.2.cloned.1.call-update) | async-done | bytes 1048592 | tf_op jit(solution)/shard_map/reduce_scatter | solution.py:161
  749.9 110.7 %all-gather.8.cloned.1.call-done = f32[8192,512]{0,1:T(8,128)} async-done(((f32[512,512]{0,1:T(8,128)}), f32[8192,512]{0,1:T(8,128)}) %all-gather.8.cloned.1.call-update) | async-done | bytes 16777232 | tf_op jit(solution)/shard_map/all_gather | solution.py:170
  860.7 17.7 %fusion.226 = f32[512,512]{0,1:T(8,128)S(1)} fusion(f32[8192,512]{0,1:T(8,128)} %all-gather.8.cloned.1.call-done, bf16[512,8192]{1,0:T(8,128)(2,1)} %param.23), kind=kOutput, calls=%fused_computation.345 | convolution fusion | flops 25769803776 | bytes 26214400 | tf_op jit(solution)/shard_map/dot_general | solution.py:169
  881.0 45.7 %while.89 = (s32[]{:T(128)}, f32[4,128,128]{2,1,0:T(8,128)S(1)}, f32[8,4,1,1]{1,3,2,0:T(1,128)S(1)}, f32[8,4,64,128]{3,2,1,0:T(8,128)}, f32[8,4,64,1]{2,1,3,0:T(...) while((s32[]{:T(128)}, f32[4,128,128]{2,1,0:T(8,128)S(1)}, ...), condition=%wide.region_14.15_spmd.clone, body=%wide.region_13.14_spmd.clone.sunk | while | flops 176586752 | bytes 2628795 | solution.py:76
  928.8 8.9 collective-permute-done.7
  939.6 8.3 collective-permute-done.8
  949.7 7.3 collective-permute-done.9
  959.0 8.6 collective-permute-done.10
  969.5 8.2 collective-permute-done.11
  979.6 8.8 collective-permute-done.12
  990.4 9.0 collective-permute-done.13
  1001.5 319.9 %while.87 = (s32[]{:T(128)}, f32[4,128,128]{2,1,0:T(8,128)S(1)}, f32[8,4,64,128]{3,2,1,0:T(8,128)}, f32[8,4,64,128]{3,2,1,0:T(8,128)}, f32[8,4,1,1]{1,3,2,0:T(1,...) while((s32[]{:T(128)}, f32[4,128,128]{2,1,0:T(8,128)S(1)}, ...), condition=%wide.region_16.17_spmd.clone, body=%wide.region_15.16_spmd.clone.sunk | while | flops 541864000 | bytes 8322349 | solution.py:76
  1006.7 19.7 %custom-call.43 = f32[4,1,64,64]{2,3,1,0:T(8,128)S(1)} custom-call(f32[4,1,64,64]{3,2,1,0:T(8,128)S(1)} %add_bitcast_fusion.4), custom_call_target="InvertDiagBlocksLowerTriangular" | custom-call | tf_op jit(solution)/shard_map/transpose(jvp())/while/body/eval_jaxpr/jit(_solve_triangular)/vmap()/triangular_solve | solution.py:48
  1046.7 19.7 %custom-call.43 = f32[4,1,64,64]{2,3,1,0:T(8,128)S(1)} custom-call(f32[4,1,64,64]{3,2,1,0:T(8,128)S(1)} %add_bitcast_fusion.4), custom_call_target="InvertDiagBlocksLowerTriangular" | custom-call | tf_op jit(solution)/shard_map/transpose(jvp())/while/body/eval_jaxpr/jit(_solve_triangular)/vmap()/triangular_solve | solution.py:48
  1086.6 19.7 %custom-call.43 = f32[4,1,64,64]{2,3,1,0:T(8,128)S(1)} custom-call(f32[4,1,64,64]{3,2,1,0:T(8,128)S(1)} %add_bitcast_fusion.4), custom_call_target="InvertDiagBlocksLowerTriangular" | custom-call | tf_op jit(solution)/shard_map/transpose(jvp())/while/body/eval_jaxpr/jit(_solve_triangular)/vmap()/triangular_solve | solution.py:48
  1116.2 2.3 fusion.375
  1126.7 19.7 %custom-call.43 = f32[4,1,64,64]{2,3,1,0:T(8,128)S(1)} custom-call(f32[4,1,64,64]{3,2,1,0:T(8,128)S(1)} %add_bitcast_fusion.4), custom_call_target="InvertDiagBlocksLowerTriangular" | custom-call | tf_op jit(solution)/shard_map/transpose(jvp())/while/body/eval_jaxpr/jit(_solve_triangular)/vmap()/triangular_solve | solution.py:48
  1156.1 2.2 fusion.375
  1166.6 19.7 %custom-call.43 = f32[4,1,64,64]{2,3,1,0:T(8,128)S(1)} custom-call(f32[4,1,64,64]{3,2,1,0:T(8,128)S(1)} %add_bitcast_fusion.4), custom_call_target="InvertDiagBlocksLowerTriangular" | custom-call | tf_op jit(solution)/shard_map/transpose(jvp())/while/body/eval_jaxpr/jit(_solve_triangular)/vmap()/triangular_solve | solution.py:48
  1196.1 2.2 fusion.375
  1206.6 19.7 %custom-call.43 = f32[4,1,64,64]{2,3,1,0:T(8,128)S(1)} custom-call(f32[4,1,64,64]{3,2,1,0:T(8,128)S(1)} %add_bitcast_fusion.4), custom_call_target="InvertDiagBlocksLowerTriangular" | custom-call | tf_op jit(solution)/shard_map/transpose(jvp())/while/body/eval_jaxpr/jit(_solve_triangular)/vmap()/triangular_solve | solution.py:48
  1246.6 19.7 %custom-call.43 = f32[4,1,64,64]{2,3,1,0:T(8,128)S(1)} custom-call(f32[4,1,64,64]{3,2,1,0:T(8,128)S(1)} %add_bitcast_fusion.4), custom_call_target="InvertDiagBlocksLowerTriangular" | custom-call | tf_op jit(solution)/shard_map/transpose(jvp())/while/body/eval_jaxpr/jit(_solve_triangular)/vmap()/triangular_solve | solution.py:48
  1276.0 2.2 fusion.375
  1286.5 19.7 %custom-call.43 = f32[4,1,64,64]{2,3,1,0:T(8,128)S(1)} custom-call(f32[4,1,64,64]{3,2,1,0:T(8,128)S(1)} %add_bitcast_fusion.4), custom_call_target="InvertDiagBlocksLowerTriangular" | custom-call | tf_op jit(solution)/shard_map/transpose(jvp())/while/body/eval_jaxpr/jit(_solve_triangular)/vmap()/triangular_solve | solution.py:48
  1316.1 2.2 fusion.375
  1322.9 2.3 fusion.182
  1333.8 72.1 %psum.21 = f32[]{:T(128)} all-reduce(f32[]{:T(128)} %multiply_reduce_fusion), channel_id=1, replica_groups=mesh['ctx'=8,'head'=16] {'ctx','head'}, use_global_device_ids=true, to_apply=%region_12.13 | all-reduce | flops 1 | bytes 8 | tf_op jit(solution)/shard_map/psum | solution.py:185
  1406.6 6.7 all-reduce.7.cloned.1.call-done
  (632 shorter events, 367.0 us)
Async XLA Ops:
  7.2 1.2 copy-start
  7.2 266.5 %all-gather.4.cloned.1.call-start = ((), (), s32[]{:S(2)}) async-start(), calls=%async_computation.1 | async-start | bytes 1179648 | tf_op jit(solution)/shard_map/all_gather | solution.py:104
  9.1 547.4 %all-gather.6.cloned.1.call-start = ((), (), s32[]{:S(2)}) async-start(), calls=%async_computation.2 | async-start | bytes 1179648 | tf_op jit(solution)/shard_map/all_gather | solution.py:105
  10.2 6.0 copy-start.11
  11.8 1.0 copy-start.3
  206.8 9.5 collective-permute-start
  216.7 9.1 collective-permute-start.1
  226.2 8.3 collective-permute-start.2
  230.6 519.3 %reduce-scatter.2.cloned.1.call-start = ((), (), s32[]{:S(2)}) async-start(), calls=%async_computation.3 | async-start | bytes 17825792 | tf_op jit(solution)/shard_map/reduce_scatter | solution.py:161
  234.8 8.3 collective-permute-start.3
  243.5 9.8 collective-permute-start.4
  249.5 11.6 copy-start.5
  253.8 13.7 collective-permute-start.5
  267.8 21.1 %collective-permute-start.6 = (f32[4,128,128]{2,1,0:T(8,128)S(1)}, f32[4,128,128]{2,1,0:T(8,128)S(1)}, u32[]{:S(2)}, u32[]{:S(2)}) collective-permute-start(f32[4,128,128]{2,1,0:T(8,128)S(1)} %convolution_add_fusion.16), channel_id=1, source_target_pairs={{0,16},{16,32},{32,48},{48,64},{64,80},{80,96},{96,112},{1,17},{17... | collective-permute-start | bytes 786440 | tf_op jit(solution)/shard_map/ppermute | solution.py:21
  538.9 17.5 %copy-start.2 = (f32[8,4,64,128]{3,2,1,0:T(8,128)}, f32[8,4,64,128]{3,2,1,0:T(8,128)S(1)}, u32[]{:S(2)}) copy-start(f32[8,4,64,128]{3,2,1,0:T(8,128)S(1)} %get-tuple-element.2022) | copy-start | bytes 3145732
  556.5 15.8 %copy-start.8 = (f32[4,512,128]{1,2,0:T(8,128)S(1)}, f32[4,512,128]{1,2,0:T(8,128)}, u32[]{:S(2)}) copy-start(f32[4,512,128]{1,2,0:T(8,128)} %copy.48) | copy-start | bytes 3145732
  591.6 269.1 %all-gather.8.cloned.1.call-start = ((), (), s32[]{:S(2)}) async-start(), calls=%async_computation.4 | async-start | bytes 17825792 | tf_op jit(solution)/shard_map/all_gather | solution.py:170
  749.9 663.4 %all-reduce.7.cloned.1.call-start = ((), (), s32[]{:S(2)}) async-start(), calls=%async_computation.5 | async-start | bytes 1048576 | tf_op jit(solution)/shard_map/psum | solution.py:186
  927.3 10.4 collective-permute-start.7
  938.3 9.6 collective-permute-start.8
  948.4 8.6 collective-permute-start.9
  957.7 9.9 collective-permute-start.10
  968.2 9.5 collective-permute-start.11
  978.3 10.1 collective-permute-start.12
  989.0 10.4 collective-permute-start.13
  1321.4 7.3 copy-start.4
  1321.4 7.3 copy-start.9
  1321.4 9.4 copy-start.6
  1321.4 9.4 copy-start.10
  1321.4 11.5 copy-start.7
  1321.5 95.5 %copy-start.1 = (bf16[512,1024]{1,0:T(8,128)(2,1)S(1)}, bf16[512,1024]{1,0:T(8,128)(2,1)}, u32[]{:S(2)}) copy-start(bf16[512,1024]{1,0:T(8,128)(2,1)} %param.17) | copy-start | bytes 3145732
Sparse Core Ops, SparseCore 0:
  10.2 42.3 all-gather.3
  230.7 44.5 all-gather.5
  591.7 158.1 reduce-scatter.1
  752.5 108.1 all-gather.7
  1333.0 80.2 all-reduce.6
where the time goes:
time: 1440 us; the launch traced here: 1420 us
  other arithmetic  547 us (38%)
  waiting for transfers between devices  360 us (25%)
  matrix products  336 us (23%)
  blocking collectives  72.1 us (5%)
  local copies, waits for them, and re-layouts  48.2 us (3%)
  starting transfers between devices  43.8 us (3%)
  between operations  16.5 us (1%)
    another operation x88, other arithmetic, span_step(): jax.scipy.linalg.solve_triangular(system, right_side, lower=True, unit_di...  481 us
    reduce_scatter x1, waiting for transfers between devices, shards(): lax.psum_scatter(jnp.einsum('fc,fr->cr', columns, delta_columns, precisio...  158 us
    all_gather x1, waiting for transfers between devices, shards(): lax.all_gather(difference, 'head', axis=0, tiled=True)  111 us
    ppermute x14, waiting for transfers between devices, shifted(): return lax.ppermute(shard, axis, pairs)  83.7 us
    psum x1, blocking collectives, shards(): total_square = lax.psum(square_part, ('ctx', 'head'))  72.1 us
    dot_general x32, matrix products, span_step(): jnp.einsum('hcd,hdw->hcw', query_block, state, precision=BEST_PRECISION)  51.1 us
    dot_general x40, matrix products, span_step(): jnp.einsum('hcd,hcw->hdw', key_block * tail_decay[:, :, None], updates, p...  49.5 us
    dot_general x40, matrix products, span_step(): jnp.einsum('hcd,hdw->hcw', solved[:, :, state_width:], state, precision=B...  48.1 us
  transfers between devices with their start and end apart: 19, of which 16 were waited for; matrix products, arithmetic and copies ran while one was open for 34% of the time, Pallas kernels for 0%

commit v1 on v0

v1 whole, which is shorter than its diff:
```python
import functools
import math

import jax
import jax.numpy as jnp
from jax import lax
from jax.experimental import pallas as pl
from jax.experimental.pallas import tpu as pltpu
from jax.sharding import PartitionSpec as P

D = 8192
QUERY_HEAD_COUNT = 64
KVH = 8
HD = 128
ROWS = 512
BLK = 128
NB = ROWS // BLK
HEADS = 4
CTX = 8
CHIPS = 8
PIECE = 512
PAD = 16
SAME_CORE = [[2 * p + core for p in range(CHIPS)] for core in range(2)]

f32 = jnp.float32
bf16 = jnp.bfloat16
f16 = jnp.float16

VMEM_LIMIT = 56 * 1024 * 1024


def params():
    return pltpu.CompilerParams(vmem_limit_bytes=VMEM_LIMIT)


def split(x):
    high = x.astype(bf16)
    return high, (x - high.astype(f32)).astype(bf16)


NN = (((1,), (0,)), ((), ()))
NT = (((1,), (1,)), ((), ()))
TN = (((0,), (0,)), ((), ()))


def mm(a, b, dims):
    return lax.dot_general(a, b, dims, preferred_element_type=f32)


def mm3(a, b, dims):
    return mm(a[0], b[0], dims) + (mm(a[0], b[1], dims) + mm(a[1], b[0], dims))


def rows_of(pair, lo, hi):
    return pair[0][lo:hi], pair[1][lo:hi]


def stack(a, b):
    return jnp.concatenate([a[0], b[0]], axis=0), jnp.concatenate([a[1], b[1]], axis=0)


def unit(x):
    inverse = 1.0 / jnp.sqrt(jnp.sum(x * x, axis=-1, keepdims=True) + 1e-06)
    return x * inverse, inverse


def gate_forms(gates, writes, head):
    lane = lax.broadcasted_iota(jnp.int32, (ROWS, HEADS), 1)
    gate = jnp.sum(jnp.where(lane == head, gates, 0.0), axis=1, keepdims=True)
    write = jnp.sum(jnp.where(lane == head, writes, 0.0), axis=1, keepdims=True)
    ii = lax.broadcasted_iota(jnp.int32, (ROWS, ROWS), 0)
    jj = lax.broadcasted_iota(jnp.int32, (ROWS, ROWS), 1)
    gate_row = jnp.sum(jnp.where(ii == jj, gate, 0.0), axis=0, keepdims=True)
    column = jnp.sum(jnp.where(jj <= ii, gate_row, 0.0), axis=1, keepdims=True)
    row = jnp.sum(jnp.where(ii <= jj, gate, 0.0), axis=0, keepdims=True)
    return column, row, write


def decays(column, row, i):
    width = BLK * (i + 1)
    ii = lax.broadcasted_iota(jnp.int32, (BLK, width), 0) + BLK * i
    jj = lax.broadcasted_iota(jnp.int32, (BLK, width), 1)
    inclusive = ii >= jj
    gap = column[BLK * i : width] - row[:, :width]
    decay = jnp.where(inclusive, jnp.exp(jnp.where(inclusive, gap, 0.0)), 0.0)
    return decay, ii > jj


def inverses(blocks):
    ii = lax.broadcasted_iota(jnp.int32, (BLK, BLK), 0)
    jj = lax.broadcasted_iota(jnp.int32, (BLK, BLK), 1)
    diagonal = (ii == jj).astype(f32)
    first = ((ii >> 1) == (jj >> 1)) & (ii > jj)
    found = [diagonal - jnp.where(first, block, 0.0) for block in blocks]
    shift = 1
    while (1 << shift) < BLK:
        mask = ((ii >> (shift + 1)) == (jj >> (shift + 1))) & ((ii >> shift) > (jj >> shift))
        parts = [split(x) for x in found]
        corner = [split(jnp.where(mask, block, 0.0)) for block in blocks]
        inner = [split(mm3(c, x, NN)) for c, x in zip(corner, parts)]
        found = [x - mm3(p, y, NN) for x, p, y in zip(found, parts, inner)]
        shift += 1
    return found


def student_kernel(
    q_ref, k_ref, v_ref, gate_ref, write_ref, qmap_ref, kmap_ref,
    ah_ref, al_ref, lh_ref, ll_ref, dh_ref, dl_ref, x_ref, z_ref, message_ref,
):
    head = pl.program_id(0)
    column, row, write = gate_forms(gate_ref[...], write_ref[...], head)
    growth = jnp.exp(column)
    end = row[:, ROWS - 1 : ROWS]
    tail = jnp.exp(end - column)
    uq, _ = unit(mm(q_ref[...], qmap_ref[0], NN))
    uk, _ = unit(mm(k_ref[...], kmap_ref[0], NN))
    uqs, uks = split(uq), split(uk)
    lower, attend = [], []
    for i in range(NB):
        lo, hi = BLK * i, BLK * (i + 1)
        both = stack(rows_of(uks, lo, hi), rows_of(uqs, lo, hi))
        gram = mm3(both, rows_of(uks, 0, hi), NT)
        decay, strict = decays(column, row, i)
        lower.append(jnp.where(strict, gram[:BLK] * decay * write[lo:hi], 0.0))
        attend.append(gram[BLK:] * decay)
    inverse = [split(x) for x in inverses([lower[i][:, BLK * i :] for i in range(NB)])]
    right = jnp.concatenate([write * v_ref[...].astype(f32), (write * growth) * uk], axis=1)
    solved = None
    for i in range(NB):
        lo, hi = BLK * i, BLK * (i + 1)
        low = split(lower[i])
        lh_ref[0, lo:hi, :hi] = low[0]
        ll_ref[0, lo:hi, :hi] = low[1]
        dh_ref[0, lo:hi, :] = inverse[i][0]
        dl_ref[0, lo:hi, :] = inverse[i][1]
        rest = right[lo:hi]
        if i:
            rest = rest - mm3((low[0][:, :lo], low[1][:, :lo]), solved, NN)
        x = mm3(inverse[i], split(rest), NN)
        x_ref[0, lo:hi, :] = x
        solved = stack(solved, split(x)) if i else split(x)
    for i in range(NB):
        lo, hi = BLK * i, BLK * (i + 1)
        part = split(attend[i])
        ah_ref[0, lo:hi, :hi] = part[0]
        al_ref[0, lo:hi, :hi] = part[1]
        z = mm3(part, rows_of(solved, 0, hi), NN)
        z_ref[0, lo:hi, :HD] = z[:, :HD]
        z_ref[0, lo:hi, HD:] = growth[lo:hi] * uq[lo:hi] - z[:, HD:]
    moved = mm3(solved, split(tail * uk), TN)
    ii = lax.broadcasted_iota(jnp.int32, (HD, HD), 0)
    jj = lax.broadcasted_iota(jnp.int32, (HD, HD), 1)
    carry = jnp.where(ii == jj, jnp.exp(end), 0.0) - moved[HD:]
    half = HD // 2
    for s in range(2):
        message_ref[s, :half, :] = moved[half * s : half * (s + 1)]
        message_ref[s, half:, :] = carry


def student_local(queries, key_mine, value_mine, log_decay, write_strength, query_map, key_map):
    per_head = lambda *shape: pl.BlockSpec((1,) + shape, lambda h: (h,) + (0,) * len(shape))
    whole = lambda *shape: pl.BlockSpec(shape, lambda h: (0,) * len(shape))
    square = jax.ShapeDtypeStruct((HEADS, ROWS, ROWS), bf16)
    narrow = jax.ShapeDtypeStruct((HEADS, ROWS, BLK), bf16)
    wide = jax.ShapeDtypeStruct((HEADS, ROWS, 2 * HD), f32)
    return pl.pallas_call(
        student_kernel,
        grid=(HEADS,),
        in_specs=[
            pl.BlockSpec((ROWS, HD), lambda h: (0, h)),
            whole(ROWS, HD),
            whole(ROWS, HD),
            whole(ROWS, HEADS),
            whole(ROWS, HEADS),
            per_head(HD, HD),
            per_head(HD, HD),
        ],
        out_specs=[
            per_head(ROWS, ROWS),
            per_head(ROWS, ROWS),
            per_head(ROWS, ROWS),
            per_head(ROWS, ROWS),
            per_head(ROWS, BLK),
            per_head(ROWS, BLK),
            per_head(ROWS, 2 * HD),
            per_head(ROWS, 2 * HD),
            pl.BlockSpec((2, HD + HD // 2, HD), lambda h: (h, 0, 0)),
        ],
        out_shape=[
            square, square, square, square, narrow, narrow, wide, wide,
            jax.ShapeDtypeStruct((2 * HEADS, HD + HD // 2, HD), f32),
        ],
        compiler_params=params(),
        name="student_local",
    )(queries, key_mine, value_mine, log_decay, write_strength, query_map, key_map)


def chain_kernel(message_ref, out_ref):
    half = HD // 2
    state = jnp.zeros((half, HD), f32)
    out_ref[0] = state
    for c in range(CTX - 1):
        carry = split(message_ref[c, half:, :])
        state = mm3(split(state), carry, NN) + message_ref[c, :half, :]
        out_ref[c + 1] = state


def chain(messages):
    return pl.pallas_call(
        chain_kernel,
        out_shape=jax.ShapeDtypeStruct((CTX, HD // 2, HD), f32),
        compiler_params=params(),
        name="state_chain",
    )(messages)


def back_chain_kernel(message_ref, grad_ref, out_ref):
    half = HD // 2
    state = jnp.zeros((half, HD), f32)
    out_ref[CTX - 1] = state
    for c in range(CTX - 1, 0, -1):
        carry = split(message_ref[c, half:, :])
        state = mm3(split(state), carry, NT) + grad_ref[c]
        out_ref[c - 1] = state


def back_chain(messages, grads):
    return pl.pallas_call(
        back_chain_kernel,
        out_shape=jax.ShapeDtypeStruct((CTX, HD // 2, HD), f32),
        compiler_params=params(),
        name="state_grad_chain",
    )(messages, grads)


def teacher_kernel(ctx_ref, q_ref, kv_ref, z_ref, state_ref, high_ref, low_ref):
    mine = ctx_ref[0]
    q = q_ref[...]
    scale = 1.0 / math.sqrt(HD)

    def block(j, carry, diagonal):
        top, total, mixed = carry
        start = pl.multiple_of(j * ROWS, ROWS)
        keys = kv_ref[pl.ds(start, ROWS), :HD]
        values = kv_ref[pl.ds(start, ROWS), HD:]
        scores = mm(q, keys, NT) * scale
        if diagonal:
            ii = lax.broadcasted_iota(jnp.int32, (ROWS, ROWS), 0)
            jj = lax.broadcasted_iota(jnp.int32, (ROWS, ROWS), 1)
            scores = jnp.where(jj <= ii, scores, -jnp.inf)
        new_top = jnp.maximum(top, jnp.max(scores, axis=1, keepdims=True))
        fade = jnp.exp(top - new_top)
        weights = jnp.exp(scores - new_top)
        total = total * fade + jnp.sum(weights, axis=1, keepdims=True)
        mixed = mixed * fade + mm(weights.astype(bf16), values, NN)
        return new_top, total, mixed

    start = (
        jnp.full((ROWS, 1), -jnp.inf, f32),
        jnp.zeros((ROWS, 1), f32),
        jnp.zeros((ROWS, HD), f32),
    )
    carry = block(mine, start, True)
    _, total, mixed = lax.fori_loop(0, mine, lambda j, c: block(j, c, False), carry)
    teacher = (mixed / total).astype(bf16).astype(f32)
    student = z_ref[0, :, :HD] + mm3(split(z_ref[0, :, HD:]), split(state_ref[0]), NT)
    delta = split(student - teacher)
    high_ref[...] = delta[0]
    low_ref[...] = delta[1]


def teacher_delta(ctx, queries, kv, z, state):
    return pl.pallas_call(
        teacher_kernel,
        grid_spec=pltpu.PrefetchScalarGridSpec(
            num_scalar_prefetch=1,
            grid=(HEADS,),
            in_specs=[
                pl.BlockSpec((ROWS, HD), lambda h, c: (0, h)),
                pl.BlockSpec((CTX * ROWS, 2 * HD), lambda h, c: (0, 0)),
                pl.BlockSpec((1, ROWS, 2 * HD), lambda h, c: (h, 0, 0)),
                pl.BlockSpec((1, HD, HD), lambda h, c: (h, 0, 0)),
            ],
            out_specs=[
                pl.BlockSpec((ROWS, HD), lambda h, c: (0, h)),
                pl.BlockSpec((ROWS, HD), lambda h, c: (0, h)),
            ],
        ),
        out_shape=[jax.ShapeDtypeStruct((ROWS, HEADS * HD), bf16)] * 2,
        compiler_params=params(),
        name="teacher_delta",
    )(ctx, queries, kv, z, state)


def project_kernel(core_ref, mine_ref, other_ref, w_mine_ref, w_other_ref, out_ref):
    width = HEADS * HD
    total = mm(mine_ref[:, width:], w_mine_ref[...], NN)
    total = total + mm(other_ref[:, width:], w_other_ref[...], NN)
    total = total + mm(mine_ref[:, :width], w_mine_ref[...], NN)
    total = total + mm(other_ref[:, :width], w_other_ref[...], NN)
    out_ref[0] = total


def project(core, mine, other, w_mine, w_other):
    width = HEADS * HD
    return pl.pallas_call(
        project_kernel,
        grid_spec=pltpu.PrefetchScalarGridSpec(
            num_scalar_prefetch=1,
            grid=(CHIPS,),
            in_specs=[
                pl.BlockSpec((ROWS, 2 * width), lambda j, c: (0, 0)),
                pl.BlockSpec((ROWS, 2 * width), lambda j, c: (0, 0)),
                pl.BlockSpec((width, PIECE), lambda j, c: (0, c[0] * CHIPS + j)),
                pl.BlockSpec((width, PIECE), lambda j, c: (0, j)),
            ],
            out_specs=pl.BlockSpec((1, ROWS, PIECE), lambda j, c: (j, 0, 0)),
        ),
        out_shape=jax.ShapeDtypeStruct((CHIPS, ROWS, PIECE), f32),
        compiler_params=params(),
        name="difference_part",
    )(core, mine, other, w_mine, w_other)


def back_project_kernel(core_ref, high_ref, low_ref, w_mine_ref, w_other_ref, mine_ref, other_ref):
    mine = mm(high_ref[0], w_mine_ref[...], NT) + mm(low_ref[0], w_mine_ref[...], NT)
    other = mm(high_ref[0], w_other_ref[...], NT) + mm(low_ref[0], w_other_ref[...], NT)

    @pl.when(pl.program_id(0) == 0)
    def _():
        mine_ref[...] = mine
        other_ref[...] = other

    @pl.when(pl.program_id(0) > 0)
    def _():
        mine_ref[...] += mine
        other_ref[...] += other


def back_project(core, high, low, w_mine, w_other):
    width = HEADS * HD
    return pl.pallas_call(
        back_project_kernel,
        grid_spec=pltpu.PrefetchScalarGridSpec(
            num_scalar_prefetch=1,
            grid=(CHIPS,),
            in_specs=[
                pl.BlockSpec((1, ROWS, PIECE), lambda j, c: (j, 0, 0)),
                pl.BlockSpec((1, ROWS, PIECE), lambda j, c: (j, 0, 0)),
                pl.BlockSpec((width, PIECE), lambda j, c: (0, c[0] * CHIPS + j)),
                pl.BlockSpec((width, PIECE), lambda j, c: (0, j)),
            ],
            out_specs=[pl.BlockSpec((ROWS, width), lambda j, c: (0, 0))] * 2,
        ),
        out_shape=[jax.ShapeDtypeStruct((ROWS, width), f32)] * 2,
        compiler_params=params(),
        name="head_grad_part",
    )(core, high, low, w_mine, w_other)


def state_grad_kernel(grad_ref, z_ref, out_ref):
    out_ref[0] = mm3(split(grad_ref[...]), split(z_ref[0, :, HD:]), TN)


def state_grad_local(head_grad, z):
    return pl.pallas_call(
        state_grad_kernel,
        grid=(HEADS,),
        in_specs=[
            pl.BlockSpec((ROWS, HD), lambda h: (0, h)),
            pl.BlockSpec((1, ROWS, 2 * HD), lambda h: (h, 0, 0)),
        ],
        out_specs=pl.BlockSpec((1, HD, HD), lambda h: (h, 0, 0)),
        out_shape=jax.ShapeDtypeStruct((HEADS, HD, HD), f32),
        compiler_params=params(),
        name="state_grad_local",
    )(head_grad, z)


def backward_kernel(
    q_ref, k_ref, gate_ref, write_ref, qmap_ref, kmap_ref,
    ah_ref, al_ref, lh_ref, ll_ref, dh_ref, dl_ref, x_ref,
    state_ref, grad_ref, state_grad_ref,
    qgrad_ref, kgrad_ref,
):
    head = pl.program_id(0)
    column, row, write = gate_forms(gate_ref[...], write_ref[...], head)
    growth = jnp.exp(column)
    tail = jnp.exp(row[:, ROWS - 1 : ROWS] - column)
    uq, q_inverse = unit(mm(q_ref[...], qmap_ref[0], NN))
    uk, k_inverse = unit(mm(k_ref[...], kmap_ref[0], NN))
    uqs, uks = split(uq), split(uk)
    state = split(state_ref[0])
    state_grad = split(state_grad_ref[0])
    grad = split(grad_ref[...])
    x = x_ref[0]
    updates = split(x[:, :HD] - mm3(split(x[:, HD:]), state, NT))
    reach = mm3(split(tail * uk), state_grad, NT)
    right = [None] * NB
    for j in range(NB):
        lo, hi = BLK * j, BLK * (j + 1)
        part = (ah_ref[0, lo:, lo:hi], al_ref[0, lo:, lo:hi])
        right[j] = mm3(part, rows_of(grad, lo, ROWS), TN) + reach[lo:hi]
    solved = None
    for j in range(NB - 1, -1, -1):
        lo, hi = BLK * j, BLK * (j + 1)
        rest = right[j]
        if solved is not None:
            part = (lh_ref[0, hi:, lo:hi], ll_ref[0, hi:, lo:hi])
            rest = rest - mm3(part, solved, TN)
        y = split(mm3((dh_ref[0, lo:hi, :], dl_ref[0, lo:hi, :]), split(rest), TN))
        solved = y if solved is None else stack(y, solved)
    key_total = [None] * NB
    query_total = []
    from_state = mm3(stack(grad, solved), state, NN)
    from_next = mm3(updates, state_grad, NN)
    for i in range(NB - 1, -1, -1):
        lo, hi = BLK * i, BLK * (i + 1)
        pair = stack(rows_of(grad, lo, hi), rows_of(solved, lo, hi))
        outer = mm3(pair, rows_of(updates, 0, hi), NT)
        decay, strict = decays(column, row, i)
        through = jnp.concatenate(
            [outer[:BLK] * decay, jnp.where(strict, -outer[BLK:] * decay * write[lo:hi], 0.0)],
            axis=0,
        )
        through = split(through)
        rows = mm3(through, rows_of(uks, 0, hi), NN)
        query_total.append(growth[lo:hi] * from_state[lo:hi] + rows[:BLK])
        columns = mm3(through, stack(rows_of(uqs, lo, hi), rows_of(uks, lo, hi)), TN)
        own = rows[BLK:] + tail[lo:hi] * from_next[lo:hi]
        own = own - (write[lo:hi] * growth[lo:hi]) * from_state[ROWS + lo : ROWS + hi]
        for j in range(i + 1):
            more = columns[BLK * j : BLK * (j + 1)]
            if j == i:
                more = more + own
            key_total[j] = more if key_total[j] is None else key_total[j] + more
    query_grad = jnp.concatenate(query_total[::-1], axis=0)
    key_grad = jnp.concatenate(key_total, axis=0)
    query_grad = q_inverse * (query_grad - uq * jnp.sum(uq * query_grad, axis=1, keepdims=True))
    key_grad = k_inverse * (key_grad - uk * jnp.sum(uk * key_grad, axis=1, keepdims=True))
    query_grad, key_grad = split(query_grad), split(key_grad)
    q, k = q_ref[...], k_ref[...]
    qgrad_ref[0] = mm(q, query_grad[0], TN) + mm(q, query_grad[1], TN)
    kgrad_ref[0] = mm(k, key_grad[0], TN) + mm(k, key_grad[1], TN)


def backward_local(
    queries, key_mine, log_decay, write_strength, query_map, key_map, kept, state, head_grad, state_grad
):
    per_head = lambda *shape: pl.BlockSpec((1,) + shape, lambda h: (h,) + (0,) * len(shape))
    whole = lambda *shape: pl.BlockSpec(shape, lambda h: (0,) * len(shape))
    column = pl.BlockSpec((ROWS, HD), lambda h: (0, h))
    return pl.pallas_call(
        backward_kernel,
        grid=(HEADS,),
        in_specs=[
            column,
            whole(ROWS, HD),
            whole(ROWS, HEADS),
            whole(ROWS, HEADS),
            per_head(HD, HD),
            per_head(HD, HD),
            per_head(ROWS, ROWS),
            per_head(ROWS, ROWS),
            per_head(ROWS, ROWS),
            per_head(ROWS, ROWS),
            per_head(ROWS, BLK),
            per_head(ROWS, BLK),
            per_head(ROWS, 2 * HD),
            per_head(HD, HD),
            column,
            per_head(HD, HD),
        ],
        out_specs=[per_head(HD, HD), per_head(HD, HD)],
        out_shape=[jax.ShapeDtypeStruct((HEADS, HD, HD), f32)] * 2,
        compiler_params=params(),
        name="student_backward",
    )(
        queries, key_mine, log_decay, write_strength, query_map, key_map,
        *kept, state, head_grad, state_grad,
    )


def exponent_for(x):
    largest = jnp.maximum(jnp.max(jnp.abs(x)), 1e-30)
    return jnp.clip(14.0 - jnp.ceil(jnp.log2(largest)), -100.0, 100.0)


def packed(x):
    exponent = exponent_for(x)
    body = (x * jnp.exp2(exponent)).astype(f16)
    extra = jnp.broadcast_to(exponent.astype(f16), x.shape[:-2] + (PAD, x.shape[-1]))
    return jnp.concatenate([body, extra], axis=-2)


def unpacked(message):
    exponent = message[..., -1:, :].astype(f32)
    return message[..., :-PAD, :].astype(f32) * jnp.exp2(-exponent)


def transpose_over(x, axis, groups=None):
    return lax.all_to_all(x, axis, 0, 0, axis_index_groups=groups, tiled=True)


def shards(queries, key_heads, values, log_decay, write_strength, query_map, key_map, out_weight):
    ctx = lax.axis_index("ctx")
    head_index = lax.axis_index("head")
    core = lax.rem(head_index, 2)
    kv_column = head_index * HEADS // (QUERY_HEAD_COUNT // KVH) * HD
    key_mine = lax.dynamic_slice_in_dim(key_heads, kv_column, HD, 1)
    value_mine = lax.dynamic_slice_in_dim(values, kv_column, HD, 1)
    kv = lax.all_gather(
        jnp.concatenate([key_mine, value_mine], axis=1), "ctx", axis=0, tiled=True
    )
    partner = [(i, i ^ 1) for i in range(2 * CHIPS)]
    half = D // 2
    w_other = lax.ppermute(
        lax.dynamic_slice_in_dim(out_weight, (1 - core) * half, half, 1), "head", partner
    )
    *kept, z, message = student_local(
        queries, key_mine, value_mine, log_decay, write_strength, query_map, key_map
    )
    messages = transpose_over(message, "ctx")
    state = transpose_over(chain(messages), "ctx").reshape(HEADS, HD, HD)
    ctx_scalar = ctx.astype(jnp.int32).reshape(1)
    core_scalar = core.astype(jnp.int32).reshape(1)
    high, low = teacher_delta(ctx_scalar, queries, kv, z, state)
    delta = jnp.concatenate([high, low], axis=1)
    delta_other = lax.ppermute(delta, "head", partner)
    part = project(core_scalar, delta, delta_other, out_weight, w_other)
    pieces = transpose_over(packed(part), "head", SAME_CORE)
    difference = jnp.sum(unpacked(pieces), axis=0)
    gathered = lax.all_gather(
        packed(difference), "head", axis=0, axis_index_groups=SAME_CORE, tiled=False
    )
    columns = unpacked(gathered)
    square_mine = jnp.broadcast_to(jnp.sum(columns * columns), (8, HD))
    square_other = lax.ppermute(square_mine, "head", partner)
    columns_high, columns_low = split(columns)
    grad_mine, grad_other = back_project(
        core_scalar, columns_high, columns_low, out_weight, w_other
    )
    head_grad = grad_mine + lax.ppermute(grad_other, "head", partner)
    local = state_grad_local(head_grad, z).reshape(CTX, HD // 2, HD)
    locals_ = transpose_over(local, "ctx")
    state_grad = transpose_over(back_chain(messages, locals_), "ctx").reshape(HEADS, HD, HD)
    query_grad, key_grad = backward_local(
        queries, key_mine, log_decay, write_strength, query_map, key_map,
        kept, state, head_grad, state_grad,
    )
    grads = jnp.concatenate([query_grad, key_grad], axis=0)
    extra = jnp.broadcast_to(square_mine + square_other, (2 * HEADS, 8, HD))
    shared = transpose_over(jnp.concatenate([grads, extra], axis=1), "ctx")
    total = jnp.sum(shared, axis=0, keepdims=True)
    final = transpose_over(jnp.broadcast_to(total, (CTX,) + total.shape[1:]), "ctx")
    normalizer = CTX * ROWS * D
    return final[0, HD, 0] / normalizer, final[:HEADS, :HD], final[HEADS:, :HD]


def solution(mesh):
    placed = (
        P("ctx", "head"),
        P("ctx", None),
        P("ctx", None),
        P("ctx", "head"),
        P("ctx", "head"),
        P("head", None, None),
        P("head", None, None),
        P("head", None),
    )
    return jax.shard_map(
        shards,
        mesh=mesh,
        in_specs=placed,
        out_specs=(P(), P("head", None, None), P("head", None, None)),
        check_vma=False,
    )
```

time: 1440 us -> 354 us (0.25)
  other arithmetic: 547 us -> 21.3 us
  waiting for transfers between devices: 360 us -> 18.8 us
  matrix products: 336 us -> 0 us
  blocking collectives: 72.1 us -> 180 us
  Pallas kernels: 0 us -> 93.4 us
  starting transfers between devices: 43.8 us -> 7.13 us
  local copies, waits for them, and re-layouts: 48.2 us -> 15.2 us
    another operation x113 -> x0, other arithmetic: 485 us -> none  [the longest x88 481 us: span_step(): jax.scipy.linalg.solve_triangular(system, right_side, lower=True, unit_di...]
    dot_general x230 -> x0, matrix products: 311 us -> none  [the longest x32 51.1 us: span_step(): jnp.einsum('hcd,hdw->hcw', query_block, state, precision=BEST_PRECISION)]
    reduce_scatter x1 -> x0, waiting for transfers between devices: 158 us -> none  [shards(): lax.psum_scatter(jnp.einsum('fc,fr->cr', columns, delta_columns, precisio...]
    all_to_all x0 -> x5, blocking collectives: none -> 132 us  [transpose_over(): return lax.all_to_all(x, axis, 0, 0, axis_index_groups=groups, tiled=True)]
    all_gather x3 -> x1, waiting for transfers between devices: 111 us -> 0.01 us  [shards(): lax.all_gather(jnp.concatenate([key_mine, value_mine], axis=1), 'ctx', ax...]
    pallas_call x0 -> x8, Pallas kernels: none -> 93.4 us  [the longest x1 24.2 us: student_local(): pl.pallas_call(student_kernel, grid=(HEADS,), in_specs=[pl.BlockSpec((ROW...]
    ppermute x14 -> x4, waiting for transfers between devices: 83.7 us -> 6.66 us  [the longest x1 2.87 us: shards(): head_grad = grad_mine + lax.ppermute(grad_other, 'head', partner)]
    psum x1 -> x0, blocking collectives: 72.1 us -> none  [shards(): total_square = lax.psum(square_part, ('ctx', 'head'))]
  transfers between devices with their start and end apart: 19 -> 7, of which waited for: 16 -> 5; matrix products, arithmetic and copies ran while one was open for 34% -> 3% of each run, Pallas kernels for 0% -> 10%
where the time goes in v1:
time: 354 us; the launch traced here: 353 us
  blocking collectives  180 us (51%)
  Pallas kernels  93.4 us (26%)
  other arithmetic  21.3 us (6%)
  waiting for transfers between devices  18.8 us (5%)
  between operations  17.5 us (5%)
  local copies, waits for them, and re-layouts  15.2 us (4%)
  starting transfers between devices  7.13 us (2%)
    all_to_all x5, blocking collectives, transpose_over(): return lax.all_to_all(x, axis, 0, 0, axis_index_groups=groups, tiled=True)  132 us
    all_gather x1, blocking collectives, shards(): lax.all_gather(packed(difference), 'head', axis=0, axis_index_groups=SAME...  47.5 us
    pallas_call x1, Pallas kernels, student_local(): pl.pallas_call(student_kernel, grid=(HEADS,), in_specs=[pl.BlockSpec((ROW...  24.2 us
    pallas_call x1, Pallas kernels, backward_local(): pl.pallas_call(backward_kernel, grid=(HEADS,), in_specs=[column, whole(RO...  23.2 us
    pallas_call x1, Pallas kernels, back_project(): pl.pallas_call(back_project_kernel, grid_spec=pltpu.PrefetchScalarGridSpe...  14.8 us
    pallas_call x1, Pallas kernels, project(): pl.pallas_call(project_kernel, grid_spec=pltpu.PrefetchScalarGridSpec(num...  14.1 us
    all_to_all x2, waiting for transfers between devices, transpose_over(): return lax.all_to_all(x, axis, 0, 0, axis_index_groups=groups, tiled=True)  12.1 us
  transfers between devices with their start and end apart: 7, of which 5 were waited for; matrix products, arithmetic and copies ran while one was open for 3% of the time, Pallas kernels for 10%

profile of v1, /device:TPU:0, one launch (start us, length us, event | category | flops | bytes accessed | tf_op | source)
XLA Modules:
  0.0 352.9 jit_solution(12942180839044365222)
XLA Ops:
  7.2 0.0 all-gather.4.cloned.1.call-start
  7.2 1.0 constant_dynamic-slice_fusion.1
  8.2 0.0 copy-start.2
  8.2 0.0 copy-start.3
  8.2 0.8 pad_maximum_fusion.1
  9.0 0.0 copy-start.6
  9.0 0.0 all-gather.4.cloned.1.call-update
  9.1 0.0 copy-start.7
  9.1 4.6 %constant_dynamic-slice_fusion = bf16[512,4096]{1,0:T(8,128)(2,1)} fusion(bf16[512,8192]{1,0:T(8,128)(2,1)} %w_mine_ref.3, s32[]{:T(128)S(6)} %select_n.14), kind=kLoop, calls=%fused_computation.24 | loop fusion | bytes 8388612 | tf_op jit(solution)/shard_map/dynamic_slice | solution.py:518
  13.7 0.0 copy-done.2
  13.7 0.0 copy-done.3
  13.7 0.0 collective-permute-start.1
  13.7 0.0 copy-done.6
  13.7 0.9 copy.17.gate_ref
  14.6 0.0 copy-done.7
  14.6 0.9 copy.18.write_ref
  15.5 24.2 %student_local.1 = (bf16[4,512,512]{2,1,0:T(8,128)(2,1)}, bf16[4,512,512]{2,1,0:T(8,128)(2,1)}, bf16[4,512,512]{2,1,0:T(8,128)(2,1)}, bf16[4,512,512]{2,1,0:T(8,...) custom-call(bf16[512,512]{1,0:T(8,128)(2,1)} %q_ref.5, ...), custom_call_target="tpu_custom_call" | custom-call | tf_op jit(solution)/shard_map/student_local/pallas_call | solution.py:166
  39.7 20.4 %all_to_all.35.message_ref = f32[8,192,128]{2,1,0:T(8,128)} all-to-all(f32[8,192,128]{2,1,0:T(8,128)} %get-tuple-element.25), channel_id=1, replica_groups=mesh['ctx'=8,'head'=16] {'ctx'}, dimensions={0} | all-to-all | bytes 1572864 | tf_op jit(solution)/shard_map/all_to_all | solution.py:502
  60.1 2.9 state_chain.1
  63.0 3.5 all-to-all-start.1
  66.5 7.4 %all-to-all-done.1 = f32[8,64,128]{2,1,0:T(8,128)S(1)} async-done(((f32[8,64,128]{2,1,0:T(8,128)}), f32[8,64,128]{2,1,0:T(8,128)S(1)}, u32[]{:S(2)}, u32[]{:S(2)}) %all-to-all-start.1) | async-done | bytes 262176 | tf_op jit(solution)/shard_map/all_to_all | solution.py:502
  73.9 0.0 copy-start
  73.9 0.0 all-gather.4.cloned.1.call-done.kv_ref
  74.0 0.7 copy-done
  74.7 6.7 %teacher_delta.1 = (bf16[512,512]{1,0:T(8,128)(2,1)}, bf16[512,512]{1,0:T(8,128)(2,1)}) custom-call(s32[1]{0:T(128)} %bitcast.2.ctx_ref, bf16[512,512]{1,0:T(8,128)(2,1)} %q_ref.5, bf16[4096,256]{1,0:T(8,128)(2,1)} %all-gather.4.cloned.1.call-done.kv_ref, f32[4,512,256]{2,1,0:T(8,128)} %get-tuple-element.26.z_ref, f32[4,128,128]{2,1,0:T(8,128)} %bitcast.15), custom_call_target="tpu_custom_call" | custom-call | tf_op jit(solution)/shard_map/teacher_delta/pallas_call | solution.py:273
  81.3 1.1 constant_dynamic-update-slice_fusion.1
  82.4 1.1 constant_dynamic-update-slice_fusion.mine_ref
  83.5 0.0 copy-start.1
  83.6 0.1 collective-permute-start
  83.7 0.0 collective-permute-done.1.w_other_ref
  83.7 2.6 collective-permute-done.other_ref
  86.3 0.0 copy-done.1
  86.3 0.9 copy-done.5
  87.3 14.1 %difference_part.1 = f32[8,512,512]{2,1,0:T(8,128)} custom-call(s32[1]{0:T(128)} %bitcast.1.core_ref, bf16[512,1024]{1,0:T(8,128)(2,1)} %copy-done.1, bf16[512,1024]{1,0:T(8,128)(2,1)} %copy-done.5, bf16[512,8192]{1,0:T(8,128)(2,1)} %w_mine_ref.3, bf16[512,4096]{1,0:T(8,128)(2,1)} %collective-permute-done.1.w_other_ref), custom_call_target="tpu_custom_call" | custom-call | tf_op jit(solution)/shard_map/difference_part/pallas_call | solution.py:306
  101.4 5.0 %abs_reduce_fusion = f32[]{:T(128)} fusion(f32[8,512,512]{2,1,0:T(8,128)} %difference_part.1), kind=kLoop, calls=%fused_computation.6 | loop fusion | flops 4194303 | bytes 8388612 | tf_op jit(solution)/shard_map/reduce_max | solution.py:485
  107.1 4.6 %multiply_convert_fusion = f16[8,512,512]{2,1,0:T(8,128)(2,1)S(1)} fusion(f32[8,512,512]{2,1,0:T(8,128)} %difference_part.1, f32[]{:T(128)S(6)} %exp2.25), kind=kLoop, calls=%fused_computation.5 | loop fusion | flops 4194304 | bytes 12582916 | tf_op jit(solution)/shard_map/convert_element_type | solution.py:491
  111.7 1.1 concatenate.20
  112.8 59.0 %all_to_all.36 = f16[8,528,512]{2,1,0:T(8,128)(2,1)S(1)} all-to-all(f16[8,528,512]{2,1,0:T(8,128)(2,1)S(1)} %concatenate.20), channel_id=1, replica_groups={{0,2,4,6,8,10,12,14},{1,3,5,7,9,11,13,15},{16,18,20,22,24,26,28,30},{17..., dimensions={0} | all-to-all | bytes 8650752 | tf_op jit(solution)/shard_map/all_to_all | solution.py:502
  171.9 0.9 multiply_reduce_fusion.1
  172.8 0.7 abs_reduce_fusion.1
  174.2 0.1 multiply_convert_fusion.1
  174.3 0.1 concatenate.21
  174.4 47.5 %all-gather.5 = f16[4224,512]{1,0:T(8,128)(2,1)S(1)} all-gather(f16[528,512]{1,0:T(8,128)(2,1)S(1)} %concatenate.21), channel_id=2, replica_groups={{0,2,4,6,8,10,12,14},{1,3,5,7,9,11,13,15},{16,18,20,22,24,26,28,30},{17..., dimensions={0}, use_global_device_ids=true | all-gather | bytes 4866048 | tf_op jit(solution)/shard_map/all_gather | solution.py:533
  222.0 5.1 %subtract_convert_fusion = (bf16[8,512,512]{2,1,0:T(8,128)(2,1)}, f32[]{:T(128)}, bf16[8,512,512]{2,1,0:T(8,128)(2,1)}) fusion(f32[8,512]{1,0:T(8,128)S(1)} %bitcast.19, f16[8,528,512]{2,1,0:T(8,128)(2,1)S(1)} %bitcast.14), kind=kLoop, calls=%fused_computation.1 | loop fusion | flops 16777215 | bytes 12599300 | tf_op jit(solution)/shard_map/convert_element_type | solution.py:38
  227.0 14.8 %head_grad_part.1 = (f32[512,512]{1,0:T(8,128)}, f32[512,512]{1,0:T(8,128)}) custom-call(s32[1]{0:T(128)} %bitcast.1.core_ref, bf16[8,512,512]{2,1,0:T(8,128)(2,1)} %get-tuple-element.35.high_ref, bf16[8,512,512]{2,1,0:T(8,128)(2,1)} %get-tuple-element.33.low_ref, bf16[512,8192]{1,0:T(8,128)(2,1)} %w_mine_ref.3, ...), custom_call_target="tpu_custom_call" | custom-call | tf_op jit(solution)/shard_map/head_grad_part/pallas_call | solution.py:342
  241.9 0.0 collective-permute-start.2
  241.9 2.9 collective-permute-done.2
  244.8 2.4 add.20.grad_ref
  247.2 4.2 %state_grad_local.1 = f32[4,128,128]{2,1,0:T(8,128)} custom-call(f32[512,512]{1,0:T(8,128)} %add.20.grad_ref, f32[4,512,256]{2,1,0:T(8,128)} %get-tuple-element.26.z_ref), custom_call_target="tpu_custom_call" | custom-call | tf_op jit(solution)/shard_map/state_grad_local/pallas_call | solution.py:366
  251.3 29.4 %all_to_all.37.grad_ref = f32[8,64,128]{2,1,0:T(8,128)} all-to-all(f32[8,64,128]{2,1,0:T(8,128)} %bitcast.18), channel_id=1, replica_groups=mesh['ctx'=8,'head'=16] {'ctx'}, dimensions={0} | all-to-all | bytes 524288 | tf_op jit(solution)/shard_map/all_to_all | solution.py:502
  280.8 3.2 state_grad_chain.1
  284.0 3.4 all-to-all-start.4
  287.4 0.6 broadcast_in_dim.6
  288.1 0.1 collective-permute-start.3
  288.2 1.2 collective-permute-done.3
  289.3 0.6 broadcast_add_fusion
  289.9 4.7 %all-to-all-done.4 = f32[8,64,128]{2,1,0:T(8,128)S(1)} async-done(((f32[8,64,128]{2,1,0:T(8,128)}), f32[8,64,128]{2,1,0:T(8,128)S(1)}, u32[]{:S(2)}, u32[]{:S(2)}) %all-to-all-start.4) | async-done | bytes 262176 | tf_op jit(solution)/shard_map/all_to_all | solution.py:502
  294.6 0.7 copy-done.4
  295.3 23.2 %student_backward.1 = (f32[4,128,128]{2,1,0:T(8,128)}, f32[4,128,128]{2,1,0:T(8,128)}) custom-call(bf16[512,512]{1,0:T(8,128)(2,1)} %q_ref.5, bf16[512,128]{1,0:T(8,128)(2,1)} %copy-done.2, f32[512,4]{1,0:T(8,128)} %copy.17.gate_ref, f32[512,4]{1,0:T(8,128)} %copy.18.write_ref, bf16[4,128,128]{2,1,0:T(8,128)(2,1)} %qmap_ref.3, ...), custom_call_target="tpu_custom_call" | custom-call | tf_op jit(solution)/shard_map/student_backward/pallas_call | solution.py:453
  318.5 1.1 pad_maximum_fusion
  319.6 11.8 %all_to_all.38 = f32[8,136,128]{2,1,0:T(8,128)S(1)} all-to-all(f32[8,136,128]{2,1,0:T(8,128)S(1)} %pad_maximum_fusion), channel_id=1, replica_groups=mesh['ctx'=8,'head'=16] {'ctx'}, dimensions={0} | all-to-all | bytes 1114112 | tf_op jit(solution)/shard_map/all_to_all | solution.py:502
  331.4 11.4 %all_to_all.39 = f32[8,136,128]{2,1,0:T(8,128)S(1)} all-to-all(f32[8,136,128]{2,1,0:T(8,128)S(1)} %broadcast_in_dim.16), channel_id=1, replica_groups=mesh['ctx'=8,'head'=16] {'ctx'}, dimensions={0} | all-to-all | bytes 1114112 | tf_op jit(solution)/shard_map/all_to_all | solution.py:502
  342.9 0.5 slice.32
  344.1 0.8 fusion.7
  (9 shorter events, 0.2 us)
Async XLA Ops:
  7.2 66.8 %all-gather.4.cloned.1.call-start = ((), (), s32[]{:S(2)}) async-start(), calls=%async_computation.7 | async-start | bytes 2359296 | tf_op jit(solution)/shard_map/all_gather | solution.py:512
  8.2 5.5 %copy-start.2 = (bf16[512,128]{1,0:T(8,128)(2,1)}, bf16[512,128]{1,0:T(8,128)(2,1)S(1)}, u32[]{:S(2)}) copy-start(bf16[512,128]{1,0:T(8,128)(2,1)S(1)} %get-tuple-element.39.k_ref) | copy-start | bytes 393220
  8.2 5.5 %copy-start.3 = (bf16[512,128]{1,0:T(8,128)(2,1)}, bf16[512,128]{1,0:T(8,128)(2,1)S(1)}, u32[]{:S(2)}) copy-start(bf16[512,128]{1,0:T(8,128)(2,1)S(1)} %get-tuple-element.38.v_ref) | copy-start | bytes 393220
  9.0 4.7 %copy-start.6 = (f32[512,4]{0,1:T(4,128)S(1)}, f32[512,4]{0,1:T(4,128)}, u32[]{:S(2)}) copy-start(f32[512,4]{0,1:T(4,128)} %param.11) | copy-start | bytes 24580
  9.1 5.5 %copy-start.7 = (f32[512,4]{0,1:T(4,128)S(1)}, f32[512,4]{0,1:T(4,128)}, u32[]{:S(2)}) copy-start(f32[512,4]{0,1:T(4,128)} %param.12) | copy-start | bytes 24580
  13.7 69.9 %collective-permute-start.1 = (bf16[512,4096]{1,0:T(8,128)(2,1)}, bf16[512,4096]{1,0:T(8,128)(2,1)}, u32[]{:S(2)}, u32[]{:S(2)}) collective-permute-start(bf16[512,4096]{1,0:T(8,128)(2,1)} %constant_dynamic-slice_fusion), channel_id=1, source_target_pairs={{0,1},{1,0},{2,3},{3,2},{4,5},{5,4},{6,7},{7,6},{8,9},{9,8},{10,11... | collective-permute-start | bytes 12582920 | tf_op jit(solution)/shard_map/ppermute | solution.py:517
  63.0 10.9 %all-to-all-start.1 = ((f32[8,64,128]{2,1,0:T(8,128)}), f32[8,64,128]{2,1,0:T(8,128)S(1)}, u32[]{:S(2)}, u32[]{:S(2)}) async-start(f32[8,64,128]{2,1,0:T(8,128)} %state_chain.1), calls=%async_computation.1 | async-start | bytes 524288 | tf_op jit(solution)/shard_map/all_to_all | solution.py:502
  73.9 0.7 copy-start
  83.5 2.8 copy-start.1
  83.6 2.7 collective-permute-start
  86.3 1.0 copy-start.5
  241.9 2.9 collective-permute-start.2
  284.0 10.6 %all-to-all-start.4 = ((f32[8,64,128]{2,1,0:T(8,128)}), f32[8,64,128]{2,1,0:T(8,128)S(1)}, u32[]{:S(2)}, u32[]{:S(2)}) async-start(f32[8,64,128]{2,1,0:T(8,128)} %state_grad_chain.1), calls=%async_computation.4 | async-start | bytes 524288 | tf_op jit(solution)/shard_map/all_to_all | solution.py:502
  288.1 1.2 collective-permute-start.3
  294.6 0.7 copy-start.4
Sparse Core Ops, SparseCore 0:
  10.2 46.7 all-gather.3

commit v2 on v0

v2 whole, which is shorter than its diff:
```python
import functools
import math

import jax
import jax.numpy as jnp
from jax import lax
from jax.experimental import pallas as pl
from jax.experimental.pallas import tpu as pltpu
from jax.sharding import PartitionSpec as P

D = 8192
QUERY_HEAD_COUNT = 64
KVH = 8
HD = 128
ROWS = 512
BLK = 128
NB = ROWS // BLK
TRI = (2 * BLK, 5 * BLK)
HEADS = 4
CTX = 8
CHIPS = 8
PIECE = 512
PAD = 16
SAME_CORE = [[2 * p + core for p in range(CHIPS)] for core in range(2)]

f32 = jnp.float32
bf16 = jnp.bfloat16
f16 = jnp.float16

MIB = 1024 * 1024
FLOOR = 0
PROJECT_MIB = 24
BACK_MIB = 40
PSTEP = 2
STEP = 1
HALF = ROWS // 2
KSTEP = 4
DSTEP = 2
TEACH = 4


def params(mib):
    return pltpu.CompilerParams(vmem_limit_bytes=max(mib, FLOOR) * MIB)


def cost(micros):
    return pl.CostEstimate(flops=int(micros * 1.1e9), bytes_accessed=0, transcendentals=0)


def split(x):
    high = x.astype(bf16)
    return high, (x - high.astype(f32)).astype(bf16)


NN = (((1,), (0,)), ((), ()))
NT = (((1,), (1,)), ((), ()))
TN = (((0,), (0,)), ((), ()))


def mm(a, b, dims):
    return lax.dot_general(a, b, dims, preferred_element_type=f32)


def beside(a, b):
    return jnp.concatenate([a, b], axis=1)


def above(a, b):
    return jnp.concatenate([a, b], axis=0)


def halves(x):
    n = x.shape[1] // 2
    return x[:, :n] + x[:, n:]


def mm3(a, b, dims):
    depth_at = dims[0][0][0]
    depth = a[0].shape[depth_at]
    if depth <= 128:
        left = beside(*a) if depth_at == 1 else above(*a)
        if dims is NT:
            return halves(mm(left, above(beside(b[0], b[0]), beside(b[1], b[1])), dims))
        if b[0].shape[1] <= 128:
            wide = beside(*b)
            return halves(mm(left, above(wide, wide), dims))
        return mm(left, above(b[0], b[0]), dims) + mm(a[0], b[1], dims)
    if dims is not NT and b[0].shape[1] <= 128:
        return halves(mm(a[0], beside(*b), dims)) + mm(a[1], b[0], dims)
    return mm(a[0], b[0], dims) + (mm(a[0], b[1], dims) + mm(a[1], b[0], dims))


def rows_of(pair, lo, hi):
    return pair[0][lo:hi], pair[1][lo:hi]


def stack(a, b):
    return above(a[0], b[0]), above(a[1], b[1])


PACKED = ((0, 4 * BLK), (BLK, 3 * BLK), (BLK, 0), (0, 0))


def block(refs, n, i, j):
    at, left = PACKED[i]
    return tuple(ref[n, at : at + BLK, left + BLK * j : left + BLK * (j + 1)] for ref in refs)


def block_column(refs, n, j, first):
    parts = []
    for ref in refs:
        blocks = []
        for i in range(first, NB):
            at, left = PACKED[i]
            blocks.append(ref[n, at : at + BLK, left + BLK * j : left + BLK * (j + 1)])
        parts.append(jnp.concatenate(blocks, axis=0))
    return tuple(parts)


def store_row(refs, n, i, pair):
    at, left = PACKED[i]
    for ref, part in zip(refs, pair):
        ref[n, at : at + BLK, left : left + BLK * (i + 1)] = part


def loaded(refs, n):
    return refs[0][n], refs[1][n]


def store(refs, n, pair):
    refs[0][n] = pair[0]
    refs[1][n] = pair[1]


def unit(x):
    inverse = 1.0 / jnp.sqrt(jnp.sum(x * x, axis=-1, keepdims=True) + 1e-06)
    return x * inverse, inverse


def through_unit(grad, units, inverse):
    return inverse * (grad - units * jnp.sum(units * grad, axis=1, keepdims=True))


def gate_forms(gate_row, write_row):
    ii = lax.broadcasted_iota(jnp.int32, (ROWS, ROWS), 0)
    jj = lax.broadcasted_iota(jnp.int32, (ROWS, ROWS), 1)
    gate = jnp.sum(jnp.where(ii == jj, gate_row, 0.0), axis=1, keepdims=True)
    write = jnp.sum(jnp.where(ii == jj, write_row, 0.0), axis=1, keepdims=True)
    column = jnp.sum(jnp.where(jj <= ii, gate_row, 0.0), axis=1, keepdims=True)
    row = jnp.sum(jnp.where(ii <= jj, gate, 0.0), axis=0, keepdims=True)
    return column, row, write


def decays(column, row, i):
    width = BLK * (i + 1)
    ii = lax.broadcasted_iota(jnp.int32, (BLK, width), 0) + BLK * i
    jj = lax.broadcasted_iota(jnp.int32, (BLK, width), 1)
    inclusive = ii >= jj
    gap = column[BLK * i : width] - row[:, :width]
    return jnp.where(inclusive, jnp.exp(jnp.where(inclusive, gap, 0.0)), 0.0)


def strict(i):
    width = BLK * (i + 1)
    ii = lax.broadcasted_iota(jnp.int32, (BLK, width), 0) + BLK * i
    return ii > lax.broadcasted_iota(jnp.int32, (BLK, width), 1)


def inverses(blocks):
    ii = lax.broadcasted_iota(jnp.int32, (BLK, BLK), 0)
    jj = lax.broadcasted_iota(jnp.int32, (BLK, BLK), 1)
    diagonal = (ii == jj).astype(f32)
    first = ((ii >> 1) == (jj >> 1)) & (ii > jj)
    found = [diagonal - jnp.where(first, block, 0.0) for block in blocks]
    whole_parts = [split(block) for block in blocks]
    none = jnp.zeros((BLK, BLK), bf16)
    shift = 1
    while (1 << shift) < BLK:
        mask = ((ii >> (shift + 1)) == (jj >> (shift + 1))) & ((ii >> shift) > (jj >> shift))
        parts = [split(x) for x in found]
        corner = [tuple(jnp.where(mask, part, none) for part in pair) for pair in whole_parts]
        inner = [split(mm3(c, x, NN)) for c, x in zip(corner, parts)]
        found = [x - mm3(p, y, NN) for x, p, y in zip(found, parts, inner)]
        shift += 1
    return found


GROWTH, TAIL, WRITE, WRITE_GROWTH, INVERSE, COLUMN = range(6)


def column_of(ref, n, which):
    return ref[n, :, which : which + 1]


def per_head(*shape, step=None):
    return pl.BlockSpec((step or STEP,) + shape, lambda h, *_: (h,) + (0,) * len(shape))


def whole(*shape):
    return pl.BlockSpec(shape, lambda h, *_: (0,) * len(shape))


def columns_spec(step=None):
    return pl.BlockSpec((ROWS, (step or STEP) * HD), lambda h, *_: (0, h))


def pair_shape(*shape):
    return [jax.ShapeDtypeStruct((HEADS,) + shape, bf16)] * 2


def heads_call(kernel, name, micros, in_specs, out_specs, out_shape, mib=56, step=None):
    return pl.pallas_call(
        kernel,
        grid=(HEADS // (step or STEP),),
        in_specs=in_specs,
        out_specs=out_specs,
        out_shape=out_shape,
        compiler_params=params(mib),
        cost_estimate=cost(micros),
        name=name,
    )


def keys_kernel(
    k_ref, v_ref, gate_ref, write_ref, kmap_ref,
    cols_ref, row_ref, ukh_ref, ukl_ref, lh_ref, ll_ref, dh_ref, dl_ref, xh_ref, xl_ref, message_ref,
):
    heads = range(KSTEP)
    lower, uks, columns, rights, ends = [], [], [], [], []
    for n in heads:
        column, row, write = gate_forms(
            gate_ref[pl.ds(pl.program_id(0) * KSTEP + n, 1), :],
            write_ref[pl.ds(pl.program_id(0) * KSTEP + n, 1), :],
        )
        end = row[:, ROWS - 1 : ROWS]
        growth = jnp.exp(column)
        tail = jnp.exp(end - column)
        uk, inverse = unit(mm(k_ref[...], kmap_ref[n], NN))
        pair = split(uk)
        store((ukh_ref, ukl_ref), n, pair)
        for which, value in enumerate((growth, tail, write, write * growth, inverse, column)):
            cols_ref[n, :, which : which + 1] = value
        row_ref[n] = row
        own = []
        for i in range(NB):
            lo, hi = BLK * i, BLK * (i + 1)
            gram = mm3(rows_of(pair, lo, hi), rows_of(pair, 0, hi), NT)
            decay = decays(column, row, i)
            own.append(jnp.where(strict(i), gram * decay * write[lo:hi], 0.0))
        lower.append(own)
        uks.append(split(tail * uk))
        rights.append(beside(write * v_ref[...].astype(f32), (write * growth) * uk))
        ends.append(end)
    found = inverses([lower[n][i][:, BLK * i :] for n in heads for i in range(NB)])
    inverse = [[split(found[n * NB + i]) for i in range(NB)] for n in heads]
    solved = [None] * KSTEP
    for i in range(NB):
        lo, hi = BLK * i, BLK * (i + 1)
        for n in heads:
            low = split(lower[n][i])
            store_row((lh_ref, ll_ref), n, i, low)
            dh_ref[n, lo:hi, :] = inverse[n][i][0]
            dl_ref[n, lo:hi, :] = inverse[n][i][1]
            rest = rights[n][lo:hi]
            if i:
                rest = rest - mm3((low[0][:, :lo], low[1][:, :lo]), solved[n], NN)
            x = split(mm3(inverse[n][i], split(rest), NN))
            solved[n] = stack(solved[n], x) if i else x
    ii = lax.broadcasted_iota(jnp.int32, (HD, HD), 0)
    jj = lax.broadcasted_iota(jnp.int32, (HD, HD), 1)
    half = HD // 2
    for n in heads:
        store((xh_ref, xl_ref), n, solved[n])
        moved = mm3(solved[n], uks[n], TN)
        carry = jnp.where(ii == jj, jnp.exp(ends[n]), 0.0) - moved[HD:]
        for s in range(2):
            message_ref[2 * n + s, :half, :] = moved[half * s : half * (s + 1)]
            message_ref[2 * n + s, half:, :] = carry


def student_keys(key_mine, value_mine, log_decay, write_strength, key_map):
    return heads_call(
        keys_kernel, "student_keys", 16,
        [whole(ROWS, HD), whole(ROWS, HD), whole(HEADS, ROWS), whole(HEADS, ROWS), per_head(HD, HD, step=KSTEP)],
        [
            per_head(ROWS, 8, step=KSTEP), per_head(1, ROWS, step=KSTEP),
            per_head(ROWS, HD, step=KSTEP), per_head(ROWS, HD, step=KSTEP),
            per_head(*TRI, step=KSTEP), per_head(*TRI, step=KSTEP),
            per_head(ROWS, BLK, step=KSTEP), per_head(ROWS, BLK, step=KSTEP),
            per_head(ROWS, 2 * HD, step=KSTEP), per_head(ROWS, 2 * HD, step=KSTEP),
            pl.BlockSpec((2 * KSTEP, HD + HD // 2, HD), lambda h: (h, 0, 0)),
        ],
        [
            jax.ShapeDtypeStruct((HEADS, ROWS, 8), f32),
            jax.ShapeDtypeStruct((HEADS, 1, ROWS), f32),
            *pair_shape(ROWS, HD), *pair_shape(*TRI), *pair_shape(ROWS, BLK), *pair_shape(ROWS, 2 * HD),
            jax.ShapeDtypeStruct((2 * HEADS, HD + HD // 2, HD), f32),
        ],
        step=KSTEP,
    )(key_mine, value_mine, log_decay.T, write_strength.T, key_map)


def queries_kernel(
    q_ref, qmap_ref, cols_ref, row_ref, ukh_ref, ukl_ref, xh_ref, xl_ref,
    inverse_ref, uqh_ref, uql_ref, ah_ref, al_ref, own_ref, rh_ref, rl_ref,
):
    for n in range(STEP):
        uq, inverse = unit(mm(q_ref[:, HD * n : HD * (n + 1)], qmap_ref[n], NN))
        inverse_ref[n, :, :1] = inverse
        uqs = split(uq)
        store((uqh_ref, uql_ref), n, uqs)
        uks = loaded((ukh_ref, ukl_ref), n)
        solved = loaded((xh_ref, xl_ref), n)
        reach = column_of(cols_ref, n, GROWTH) * uq
        for i in range(NB):
            lo, hi = BLK * i, BLK * (i + 1)
            decay = decays(column_of(cols_ref, n, COLUMN), row_ref[n], i)
            attend = split(mm3(rows_of(uqs, lo, hi), rows_of(uks, 0, hi), NT) * decay)
            store_row((ah_ref, al_ref), n, i, attend)
            z = mm3(attend, rows_of(solved, 0, hi), NN)
            own_ref[n, lo:hi, :] = z[:, :HD]
            part = split(reach[lo:hi] - z[:, HD:])
            rh_ref[n, lo:hi, :] = part[0]
            rl_ref[n, lo:hi, :] = part[1]


def student_queries(queries, query_map, cols, row, uk, solved):
    return heads_call(
        queries_kernel, "student_queries", 8,
        [
            columns_spec(), per_head(HD, HD), per_head(ROWS, 8), per_head(1, ROWS),
            per_head(ROWS, HD), per_head(ROWS, HD), per_head(ROWS, 2 * HD), per_head(ROWS, 2 * HD),
        ],
        [
            per_head(ROWS, 8), per_head(ROWS, HD), per_head(ROWS, HD), per_head(*TRI),
            per_head(*TRI), per_head(ROWS, HD), per_head(ROWS, HD), per_head(ROWS, HD),
        ],
        [
            jax.ShapeDtypeStruct((HEADS, ROWS, 8), f32),
            *pair_shape(ROWS, HD), *pair_shape(*TRI),
            jax.ShapeDtypeStruct((HEADS, ROWS, HD), f32),
            *pair_shape(ROWS, HD),
        ],
    )(queries, query_map, cols, row, *uk, *solved)


def chain_kernel(message_ref, out_ref):
    half = HD // 2
    carries = [split(message_ref[c, half:, :]) for c in range(CTX - 1)]
    state = jnp.zeros((half, HD), f32)
    out_ref[0] = state
    for c in range(CTX - 1):
        state = mm3(split(state), carries[c], NN) + message_ref[c, :half, :]
        out_ref[c + 1] = state


def chain(messages):
    return pl.pallas_call(
        chain_kernel,
        out_shape=jax.ShapeDtypeStruct((CTX, HD // 2, HD), f32),
        compiler_params=params(8),
        cost_estimate=cost(3),
        name="state_chain",
    )(messages)


def back_chain_kernel(message_ref, grad_ref, out_ref):
    half = HD // 2
    carries = [split(message_ref[c, half:, :]) for c in range(CTX)]
    state = jnp.zeros((half, HD), f32)
    out_ref[CTX - 1] = state
    for c in range(CTX - 1, 0, -1):
        state = mm3(split(state), carries[c], NT) + grad_ref[c]
        out_ref[c - 1] = state


def back_chain(messages, grads):
    return pl.pallas_call(
        back_chain_kernel,
        out_shape=jax.ShapeDtypeStruct((CTX, HD // 2, HD), f32),
        compiler_params=params(8),
        cost_estimate=cost(3),
        name="state_grad_chain",
    )(messages, grads)


def teacher_kernel(half, ctx_ref, q_ref, kv_ref, out_ref):
    mine = ctx_ref[0]
    scale = math.log2(math.e) / math.sqrt(HD)

    def block(j, carry, width, diagonal):
        start = pl.multiple_of(j * ROWS, ROWS)
        keys = kv_ref[pl.ds(start, width), :HD]
        values = kv_ref[pl.ds(start, width), HD:]
        out = []
        raw = [mm(q_ref[:, HD * n : HD * (n + 1)], keys, NT) for n in range(TEACH)]
        for n in range(TEACH):
            top, total, mixed = carry[n]
            scores = raw[n]
            if diagonal:
                ii = lax.broadcasted_iota(jnp.int32, (HALF, width), 0) + HALF * half
                jj = lax.broadcasted_iota(jnp.int32, (HALF, width), 1)
                scores = jnp.where(jj <= ii, scores, -jnp.inf)
            new_top = jnp.maximum(top, jnp.max(scores, axis=1, keepdims=True))
            fade = jnp.exp2((top - new_top) * scale)
            weights = jnp.exp2((scores - new_top) * scale)
            total = total * fade + jnp.sum(weights, axis=1, keepdims=True)
            mixed = mixed * fade + mm(weights.astype(bf16), values, NN)
            out.append((new_top, total, mixed))
        return tuple(out)

    start = (
        jnp.full((HALF, 1), -jnp.inf, f32),
        jnp.zeros((HALF, 1), f32),
        jnp.zeros((HALF, HD), f32),
    )
    carry = block(mine, (start,) * TEACH, HALF * (half + 1), True)
    carry = lax.fori_loop(0, mine, lambda j, c: block(j, c, ROWS, False), carry)
    for n in range(TEACH):
        _, total, mixed = carry[n]
        out_ref[:, HD * n : HD * (n + 1)] = (mixed / total).astype(bf16)


def teacher_out(half, ctx, queries, kv):
    return pl.pallas_call(
        functools.partial(teacher_kernel, half),
        grid_spec=pltpu.PrefetchScalarGridSpec(
            num_scalar_prefetch=1,
            grid=(HEADS // TEACH,),
            in_specs=[
                pl.BlockSpec((HALF, TEACH * HD), lambda h, c: (half, h)),
                pl.BlockSpec((CTX * ROWS, 2 * HD), lambda h, c: (0, 0)),
            ],
            out_specs=pl.BlockSpec((HALF, TEACH * HD), lambda h, c: (0, h)),
        ),
        out_shape=jax.ShapeDtypeStruct((HALF, HEADS * HD), bf16),
        compiler_params=params(24),
        cost_estimate=cost(9),
        name=f"teacher_{half}",
    )(ctx, queries, kv)


def delta_kernel(own_ref, rh_ref, rl_ref, state_ref, teacher_ref, delta_ref):
    for n in range(DSTEP):
        student = own_ref[n] + mm3(loaded((rh_ref, rl_ref), n), split(state_ref[n]), NT)
        delta = split(student - teacher_ref[:, HD * n : HD * (n + 1)].astype(f32))
        delta_ref[0, :, HD * n : HD * (n + 1)] = delta[0]
        delta_ref[1, :, HD * n : HD * (n + 1)] = delta[1]


def student_delta(half, own, reach, state, teacher):
    rows = pl.BlockSpec((DSTEP, HALF, HD), lambda h: (h, half, 0))
    return heads_call(
        delta_kernel, f"delta_{half}", 2,
        [rows, rows, rows, per_head(HD, HD, step=DSTEP), pl.BlockSpec((HALF, DSTEP * HD), lambda h: (0, h))],
        pl.BlockSpec((2, HALF, DSTEP * HD), lambda h: (0, 0, h)),
        jax.ShapeDtypeStruct((2, HALF, HEADS * HD), bf16),
        step=DSTEP,
    )(own, *reach, state, teacher)


def solve_back(refs_l, refs_d, n, right):
    solved, out = None, []
    for j in range(NB - 1, -1, -1):
        lo, hi = BLK * j, BLK * (j + 1)
        rest = right[j]
        if solved is not None:
            rest = rest - mm3(block_column(refs_l, n, j, j + 1), solved, TN)
        y = mm3((refs_d[0][n, lo:hi, :], refs_d[1][n, lo:hi, :]), split(rest), TN)
        out.append(y)
        solved = split(y) if solved is None else stack(split(y), solved)
    return solved, out[::-1]


def ready_kernel(
    xh_ref, xl_ref, lh_ref, ll_ref, dh_ref, dl_ref, ukh_ref, ukl_ref, cols_ref, state_ref, ah_ref, al_ref,
    nh_ref, nl_ref, th_ref, tl_ref, bh_ref, bl_ref,
):
    for n in range(STEP):
        found = [None] * NB
        for j in range(NB - 1, -1, -1):
            rest = block_column((ah_ref, al_ref), n, j, j)
            if j < NB - 1:
                rest = rest[0].astype(f32) + rest[1].astype(f32)
                for i in range(j + 1, NB):
                    more = mm3(found[i], block((lh_ref, ll_ref), n, i, j), NN)
                    at = BLK * (i - j)
                    rest = jnp.concatenate([rest[:at], rest[at:] - more], axis=0)
                rest = split(rest)
            d = dh_ref[n, BLK * j : BLK * (j + 1), :], dl_ref[n, BLK * j : BLK * (j + 1), :]
            found[j] = split(mm3(rest, d, NN))
            for i in range(j, NB):
                at, left = PACKED[i]
                for ref, part in zip((bh_ref, bl_ref), found[j]):
                    ref[n, at : at + BLK, left + BLK * j : left + BLK * (j + 1)] = part[BLK * (i - j) : BLK * (i - j + 1)]
        x = loaded((xh_ref, xl_ref), n)
        state = split(state_ref[n])
        first = x[0][:, :HD].astype(f32) + x[1][:, :HD].astype(f32)
        store((nh_ref, nl_ref), n, split(first - mm3((x[0][:, HD:], x[1][:, HD:]), state, NT)))
        uk = ukh_ref[n].astype(f32) + ukl_ref[n].astype(f32)
        moved = column_of(cols_ref, n, TAIL) * uk
        solved, _ = solve_back(
            (lh_ref, ll_ref), (dh_ref, dl_ref), n, [moved[BLK * j : BLK * (j + 1)] for j in range(NB)]
        )
        store((th_ref, tl_ref), n, solved)


def student_ready(solved, lower, inverse, uk, cols, state, attend):
    return heads_call(
        ready_kernel, "backward_ready", 10,
        [
            per_head(ROWS, 2 * HD), per_head(ROWS, 2 * HD), per_head(*TRI), per_head(*TRI),
            per_head(ROWS, BLK), per_head(ROWS, BLK), per_head(ROWS, HD), per_head(ROWS, HD),
            per_head(ROWS, 8), per_head(HD, HD), per_head(*TRI), per_head(*TRI),
        ],
        [per_head(ROWS, HD)] * 4 + [per_head(*TRI)] * 2,
        pair_shape(ROWS, HD) + pair_shape(ROWS, HD) + pair_shape(*TRI),
    )(*solved, *lower, *inverse, *uk, cols, state, *attend)


def project_kernel(core_ref, mine_ref, other_ref, w_mine_ref, w_other_ref, out_ref):
    width = HEADS * HD
    both = mm(mine_ref[...].reshape(2 * HALF, width), w_mine_ref[...], NN)
    both = both + mm(other_ref[...].reshape(2 * HALF, width), w_other_ref[...], NN)
    total = both[:HALF] + both[HALF:]
    largest = jnp.max(jnp.max(jnp.abs(total), axis=1, keepdims=True), axis=0, keepdims=True)
    exponent = exponent_of(largest)
    scaled = total * jnp.exp2(exponent)
    for p in range(PSTEP):
        at = slice(PIECE * p, PIECE * (p + 1))
        out_ref[p, :HALF, :] = scaled[:, at]
        out_ref[p, HALF:, :] = jnp.broadcast_to(exponent, (PAD, PIECE))


def project(half, core, mine, other, w_mine, w_other):
    width = HEADS * HD
    return pl.pallas_call(
        project_kernel,
        grid_spec=pltpu.PrefetchScalarGridSpec(
            num_scalar_prefetch=1,
            grid=(CHIPS // PSTEP,),
            in_specs=[
                pl.BlockSpec((2, HALF, width), lambda j, c: (0, 0, 0)),
                pl.BlockSpec((2, HALF, width), lambda j, c: (0, 0, 0)),
                pl.BlockSpec((width, PSTEP * PIECE), lambda j, c: (0, c[0] * (CHIPS // PSTEP) + j)),
                pl.BlockSpec((width, PSTEP * PIECE), lambda j, c: (0, j)),
            ],
            out_specs=pl.BlockSpec((PSTEP, HALF + PAD, PIECE), lambda j, c: (j, 0, 0)),
        ),
        out_shape=jax.ShapeDtypeStruct((CHIPS, HALF + PAD, PIECE), f32),
        compiler_params=params(PROJECT_MIB),
        cost_estimate=cost(7),
        name=f"difference_part_{half}",
    )(core, mine, other, w_mine, w_other)


def back_project_kernel(
    core_ref, high_ref, low_ref, w_mine_ref, w_other_ref, mine_ref, other_ref, square_ref
):
    rows = (slice(0, HALF), slice(HALF + PAD, ROWS + PAD))
    both = jnp.concatenate([ref[0, at, :] for ref in (high_ref, low_ref) for at in rows], axis=0)
    mine = mm(both, w_mine_ref[...], NT)
    other = mm(both, w_other_ref[...], NT)
    mine = mine[:ROWS] + mine[ROWS:]
    other = other[:ROWS] + other[ROWS:]
    values = both[:ROWS].astype(f32) + both[ROWS:].astype(f32)
    square = jnp.sum((values * values).reshape(ROWS // 8, 8, PIECE), axis=0)

    @pl.when(pl.program_id(0) == 0)
    def _():
        mine_ref[...] = mine
        other_ref[...] = other
        square_ref[...] = square

    @pl.when(pl.program_id(0) > 0)
    def _():
        mine_ref[...] += mine
        other_ref[...] += other
        square_ref[...] += square


def back_project(core, high, low, w_mine, w_other):
    width = HEADS * HD
    columns = pl.BlockSpec((1, ROWS + 2 * PAD, PIECE), lambda j, c: (j, 0, 0))
    return pl.pallas_call(
        back_project_kernel,
        grid_spec=pltpu.PrefetchScalarGridSpec(
            num_scalar_prefetch=1,
            grid=(CHIPS,),
            in_specs=[
                columns,
                columns,
                pl.BlockSpec((width, PIECE), lambda j, c: (0, c[0] * CHIPS + j)),
                pl.BlockSpec((width, PIECE), lambda j, c: (0, j)),
            ],
            out_specs=[
                pl.BlockSpec((ROWS, width), lambda j, c: (0, 0)),
                pl.BlockSpec((ROWS, width), lambda j, c: (0, 0)),
                pl.BlockSpec((8, PIECE), lambda j, c: (0, 0)),
            ],
        ),
        out_shape=[
            jax.ShapeDtypeStruct((ROWS, width), f32),
            jax.ShapeDtypeStruct((ROWS, width), f32),
            jax.ShapeDtypeStruct((8, PIECE), f32),
        ],
        compiler_params=params(BACK_MIB),
        cost_estimate=cost(14),
        name="head_grad_part",
    )(core, high, low, w_mine, w_other)


def state_grad_kernel(mine_ref, other_ref, rh_ref, rl_ref, gh_ref, gl_ref, out_ref):
    for n in range(DSTEP):
        at = slice(HD * n, HD * (n + 1))
        grad = split(mine_ref[:, at] + other_ref[:, at])
        gh_ref[:, at] = grad[0]
        gl_ref[:, at] = grad[1]
        out_ref[n] = mm3(grad, loaded((rh_ref, rl_ref), n), TN)


def state_grad_local(mine, other, reach):
    return heads_call(
        state_grad_kernel, "state_grad_local", 4,
        [columns_spec(DSTEP), columns_spec(DSTEP), per_head(ROWS, HD, step=DSTEP), per_head(ROWS, HD, step=DSTEP)],
        [columns_spec(DSTEP), columns_spec(DSTEP), per_head(HD, HD, step=DSTEP)],
        [jax.ShapeDtypeStruct((ROWS, HEADS * HD), bf16)] * 2
        + [jax.ShapeDtypeStruct((HEADS, HD, HD), f32)],
        step=DSTEP,
    )(mine, other, *reach)


def inner_kernel(gh_ref, gl_ref, bh_ref, bl_ref, y_ref):
    for n in range(DSTEP):
        at = slice(HD * n, HD * (n + 1))
        grad = gh_ref[:, at], gl_ref[:, at]
        for j in range(NB):
            lo, hi = BLK * j, BLK * (j + 1)
            y_ref[n, lo:hi, :] = mm3(block_column((bh_ref, bl_ref), n, j, j), rows_of(grad, lo, ROWS), TN)


def inner_grad(grad, through):
    return heads_call(
        inner_kernel, "update_grad_local", 4,
        [
            columns_spec(DSTEP), columns_spec(DSTEP),
            per_head(*TRI, step=DSTEP), per_head(*TRI, step=DSTEP),
        ],
        per_head(ROWS, HD, step=DSTEP),
        jax.ShapeDtypeStruct((HEADS, ROWS, HD), f32),
        step=DSTEP,
    )(*grad, *through)


def query_grad_kernel(
    gh_ref, gl_ref, nh_ref, nl_ref, row_ref, ukh_ref, ukl_ref, uqh_ref, uql_ref,
    cols_ref, inverse_ref, state_ref, q_ref, grad_ref, key_ref,
):
    for n in range(STEP):
        at = slice(HD * n, HD * (n + 1))
        grad = gh_ref[:, at], gl_ref[:, at]
        updates = loaded((nh_ref, nl_ref), n)
        uks, uqs = loaded((ukh_ref, ukl_ref), n), loaded((uqh_ref, uql_ref), n)
        from_state = column_of(cols_ref, n, GROWTH) * mm3(grad, split(state_ref[n]), NN)
        total = [None] * NB
        query_total = []
        for i in range(NB):
            lo, hi = BLK * i, BLK * (i + 1)
            outer = mm3(rows_of(grad, lo, hi), rows_of(updates, 0, hi), NT)
            through = split(outer * decays(column_of(cols_ref, n, COLUMN), row_ref[n], i))
            query_total.append(from_state[lo:hi] + mm3(through, rows_of(uks, 0, hi), NN))
            columns = mm3(through, rows_of(uqs, lo, hi), TN)
            for j in range(i + 1):
                more = columns[BLK * j : BLK * (j + 1)]
                total[j] = more if total[j] is None else total[j] + more
        for j in range(NB):
            key_ref[n, BLK * j : BLK * (j + 1), :] = total[j]
        uq = uqs[0].astype(f32) + uqs[1].astype(f32)
        query_grad = jnp.concatenate(query_total, axis=0)
        query_grad = split(through_unit(query_grad, uq, inverse_ref[n, :, :1]))
        q = q_ref[:, at]
        grad_ref[n] = halves(mm(q, beside(*query_grad), TN))


def query_grad_local(grad, updates, row, uk, uq, cols, inverse, state, queries):
    return heads_call(
        query_grad_kernel, "query_grad", 8,
        [
            columns_spec(), columns_spec(), per_head(ROWS, HD), per_head(ROWS, HD), per_head(1, ROWS),
            per_head(ROWS, HD), per_head(ROWS, HD), per_head(ROWS, HD), per_head(ROWS, HD),
            per_head(ROWS, 8), per_head(ROWS, 8), per_head(HD, HD), columns_spec(),
        ],
        [per_head(HD, HD), per_head(ROWS, HD)],
        [
            jax.ShapeDtypeStruct((HEADS, HD, HD), f32),
            jax.ShapeDtypeStruct((HEADS, ROWS, HD), f32),
        ],
    )(*grad, *updates, row, *uk, *uq, cols, inverse, state, queries)


def key_grad_kernel(
    y_ref, th_ref, tl_ref, nh_ref, nl_ref, row_ref, ukh_ref, ukl_ref,
    cols_ref, state_ref, state_grad_ref, key_ref, k_ref, grad_ref,
):
    for n in range(STEP):
        updates, uks = loaded((nh_ref, nl_ref), n), loaded((ukh_ref, ukl_ref), n)
        state_grad = split(state_grad_ref[n])
        inner = split(y_ref[n] + mm3(loaded((th_ref, tl_ref), n), state_grad, NT))
        write = column_of(cols_ref, n, WRITE)
        base = key_ref[n] + column_of(cols_ref, n, TAIL) * mm3(updates, state_grad, NN)
        base = base - column_of(cols_ref, n, WRITE_GROWTH) * mm3(inner, split(state_ref[n]), NN)
        total = [base[BLK * j : BLK * (j + 1)] for j in range(NB)]
        for i in range(NB):
            lo, hi = BLK * i, BLK * (i + 1)
            outer = mm3(rows_of(inner, lo, hi), rows_of(updates, 0, hi), NT)
            scaled = outer * decays(column_of(cols_ref, n, COLUMN), row_ref[n], i) * write[lo:hi]
            through = split(jnp.where(strict(i), scaled, 0.0))
            total[i] = total[i] - mm3(through, rows_of(uks, 0, hi), NN)
            columns = mm3(through, rows_of(uks, lo, hi), TN)
            for j in range(i + 1):
                total[j] = total[j] - columns[BLK * j : BLK * (j + 1)]
        uk = uks[0].astype(f32) + uks[1].astype(f32)
        key_grad = jnp.concatenate(total, axis=0)
        key_grad = split(through_unit(key_grad, uk, column_of(cols_ref, n, INVERSE)))
        grad_ref[n] = halves(mm(k_ref[...], beside(*key_grad), TN))


def key_grad_local(inner, moved, updates, row, uk, cols, state, state_grad, partial, key_mine):
    return heads_call(
        key_grad_kernel, "key_grad", 9,
        [
            per_head(ROWS, HD), per_head(ROWS, HD), per_head(ROWS, HD), per_head(ROWS, HD),
            per_head(ROWS, HD), per_head(1, ROWS), per_head(ROWS, HD), per_head(ROWS, HD),
            per_head(ROWS, 8), per_head(HD, HD), per_head(HD, HD), per_head(ROWS, HD), whole(ROWS, HD),
        ],
        per_head(HD, HD),
        jax.ShapeDtypeStruct((HEADS, HD, HD), f32),
    )(inner, *moved, *updates, row, *uk, cols, state, state_grad, partial, key_mine)


def exponent_of(largest):
    return jnp.clip(14.0 - jnp.ceil(jnp.log2(jnp.maximum(largest, 1e-30))), -100.0, 100.0)


def summed(pieces):
    exponents = pieces[:, -1:, :].astype(f32)
    exponent = jnp.min(exponents, axis=0) - 3.0
    total = jnp.sum(pieces.astype(f32) * jnp.exp2(exponent[None] - exponents), axis=0)
    at = lax.broadcasted_iota(jnp.int32, total.shape, 0)
    return jnp.where(at < total.shape[0] - PAD, total, exponent).astype(f16)


def rescaled(message):
    return message.astype(f32) * jnp.exp2(-message[..., -1:, :].astype(f32))


def transpose_over(x, axis, groups=None):
    return lax.all_to_all(x, axis, 0, 0, axis_index_groups=groups, tiled=True)


def shards(queries, key_heads, values, log_decay, write_strength, query_map, key_map, out_weight):
    ctx = lax.axis_index("ctx")
    head_index = lax.axis_index("head")
    core = lax.rem(head_index, 2)
    kv_column = head_index * HEADS // (QUERY_HEAD_COUNT // KVH) * HD
    key_mine = lax.dynamic_slice_in_dim(key_heads, kv_column, HD, 1)
    value_mine = lax.dynamic_slice_in_dim(values, kv_column, HD, 1)
    kv = lax.all_gather(
        jnp.concatenate([key_mine, value_mine], axis=1), "ctx", axis=0, tiled=True
    )
    cols, row, *pairs, message = student_keys(
        key_mine, value_mine, log_decay, write_strength, key_map
    )
    uk, lower, inverse, solved = [pairs[2 * i : 2 * i + 2] for i in range(4)]
    ctx_scalar = ctx.astype(jnp.int32).reshape(1)
    core_scalar = core.astype(jnp.int32).reshape(1)
    messages = transpose_over(message, "ctx")
    partner = [(i, i ^ 1) for i in range(2 * CHIPS)]
    half = D // 2
    core_after, _ = lax.optimization_barrier((core, message))
    w_other = lax.ppermute(
        lax.dynamic_slice_in_dim(out_weight, (1 - core_after) * half, half, 1), "head", partner
    )
    cols_after, _ = lax.optimization_barrier((cols, message))
    q_inverse, *pairs = student_queries(queries, query_map, cols_after, row, uk, solved)
    uq, attend, own, reach = pairs[:2], pairs[2:4], pairs[4], pairs[5:]
    messages, own = lax.optimization_barrier((messages, own))
    states = chain(messages)
    state = transpose_over(states, "ctx").reshape(HEADS, HD, HD)
    kv, ctx_scalar, _ = lax.optimization_barrier((kv, ctx_scalar, states))
    sent, message_out = [], states
    for half in range(2):
        kv, ctx_scalar, _ = lax.optimization_barrier((kv, ctx_scalar, message_out))
        teacher = teacher_out(half, ctx_scalar, queries, kv)
        state_here, teacher = lax.optimization_barrier((state, teacher))
        delta = student_delta(half, own, reach, state_here, teacher)
        delta_other = lax.ppermute(delta, "head", partner)
        part = project(half, core_scalar, delta, delta_other, out_weight, w_other)
        message_out = part.astype(f16)
        sent.append(transpose_over(message_out, "head", SAME_CORE))
    state_after, _ = lax.optimization_barrier((state, message_out))
    *pairs, = student_ready(solved, lower, inverse, uk, cols, state_after, attend)
    sent[1], pairs = lax.optimization_barrier((sent[1], pairs))
    updates, moved, through = pairs[:2], pairs[2:4], pairs[4:]
    gathered = lax.all_gather(
        jnp.concatenate([summed(pieces) for pieces in sent], axis=0),
        "head", axis=0, axis_index_groups=SAME_CORE, tiled=False,
    )
    columns_high, columns_low = split(rescaled(gathered.reshape(CHIPS, 2, HALF + PAD, PIECE)))
    together = (CHIPS, ROWS + 2 * PAD, PIECE)
    grad_mine, grad_other, squares = back_project(
        core_scalar, columns_high.reshape(together), columns_low.reshape(together), out_weight, w_other
    )
    square_mine = jnp.broadcast_to(jnp.sum(squares), (8, HD))
    square_other = lax.ppermute(square_mine, "head", partner)
    grad_high, grad_low, local = state_grad_local(
        grad_mine, lax.ppermute(grad_other, "head", partner), reach
    )
    locals_ = transpose_over(local.reshape(CTX, HD // 2, HD), "ctx")
    (grad_high, grad_low), _ = lax.optimization_barrier(((grad_high, grad_low), local))
    head_grad = [grad_high, grad_low]
    query_grad, partial = query_grad_local(
        head_grad, updates, row, uk, uq, cols, q_inverse, state, queries
    )
    locals_, partial = lax.optimization_barrier((locals_, partial))
    states_back = back_chain(messages, locals_)
    state_grad = transpose_over(states_back, "ctx").reshape(HEADS, HD, HD)
    through_after, _ = lax.optimization_barrier((through, states_back))
    inner = inner_grad(head_grad, through_after)
    key_grad = key_grad_local(
        inner, moved, updates, row, uk, cols, state, state_grad, partial, key_mine
    )
    grads = jnp.concatenate([query_grad, key_grad], axis=0)
    extra = jnp.broadcast_to(square_mine + square_other, (2 * HEADS, 8, HD))
    shared = transpose_over(jnp.concatenate([grads, extra], axis=1), "ctx")
    total = jnp.sum(shared, axis=0, keepdims=True)
    final = transpose_over(jnp.broadcast_to(total, (CTX,) + total.shape[1:]), "ctx")
    normalizer = CTX * ROWS * D
    return final[0, HD, 0] / normalizer, final[:HEADS, :HD], final[HEADS:, :HD]


def solution(mesh):
    placed = (
        P("ctx", "head"),
        P("ctx", None),
        P("ctx", None),
        P("ctx", "head"),
        P("ctx", "head"),
        P("head", None, None),
        P("head", None, None),
        P("head", None),
    )
    return jax.shard_map(
        shards,
        mesh=mesh,
        in_specs=placed,
        out_specs=(P(), P("head", None, None), P("head", None, None)),
        check_vma=False,
    )
```

time: 1440 us -> 312 us (0.22)
  other arithmetic: 547 us -> 16.9 us
  matrix products: 336 us -> 0 us
  waiting for transfers between devices: 360 us -> 47.4 us
  Pallas kernels: 0 us -> 95.5 us
  local copies, waits for them, and re-layouts: 48.2 us -> 23 us
    another operation x113 -> x0, other arithmetic: 485 us -> none  [the longest x88 481 us: span_step(): jax.scipy.linalg.solve_triangular(system, right_side, lower=True, unit_di...]
    dot_general x230 -> x0, matrix products: 311 us -> none  [the longest x32 51.1 us: span_step(): jnp.einsum('hcd,hdw->hcw', query_block, state, precision=BEST_PRECISION)]
    reduce_scatter x1 -> x0, waiting for transfers between devices: 158 us -> none  [shards(): lax.psum_scatter(jnp.einsum('fc,fr->cr', columns, delta_columns, precisio...]
    all_gather x3 -> x1, waiting for transfers between devices: 111 us -> 1.02 us  [shards(): lax.all_gather(jnp.concatenate([key_mine, value_mine], axis=1), 'ctx', ax...]
    pallas_call x0 -> x16, Pallas kernels: none -> 95.5 us  [the longest x2 14.4 us: project(): pl.pallas_call(project_kernel, grid_spec=pltpu.PrefetchScalarGridSpec(num...]
    ppermute x14 -> x5, waiting for transfers between devices: 83.7 us -> 5.06 us  [the longest x2 4.23 us: shards(): delta_other = lax.ppermute(delta, 'head', partner)]
    psum x1 -> x0, blocking collectives: 72.1 us -> none  [shards(): total_square = lax.psum(square_part, ('ctx', 'head'))]
    all_gather x0 -> x1, blocking collectives: none -> 48.4 us  [shards(): lax.all_gather(jnp.concatenate([summed(pieces) for pieces in sent], axis=...]
  transfers between devices with their start and end apart: 19 -> 12, of which waited for: 16 -> 9; matrix products, arithmetic and copies ran while one was open for 34% -> 4% of each run, Pallas kernels for 0% -> 19%
where the time goes in v2:
time: 312 us; the launch traced here: 311 us
  Pallas kernels  95.5 us (31%)
  blocking collectives  71.6 us (23%)
  waiting for transfers between devices  47.4 us (15%)
  starting transfers between devices  39.9 us (13%)
  local copies, waits for them, and re-layouts  23 us (7%)
  other arithmetic  16.9 us (5%)
  between operations  16.1 us (5%)
    all_gather x1, blocking collectives, shards(): lax.all_gather(jnp.concatenate([summed(pieces) for pieces in sent], axis=...  48.4 us
    all_to_all x6, waiting for transfers between devices, transpose_over(): return lax.all_to_all(x, axis, 0, 0, axis_index_groups=groups, tiled=True)  41.3 us
    all_to_all x6, starting transfers between devices, transpose_over(): return lax.all_to_all(x, axis, 0, 0, axis_index_groups=groups, tiled=True)  39.3 us
    all_to_all x2, blocking collectives, transpose_over(): return lax.all_to_all(x, axis, 0, 0, axis_index_groups=groups, tiled=True)  23.3 us
    unnamed x34, local copies, waits for them, and re-layouts  15.3 us
    pallas_call x2, Pallas kernels, project(): pl.pallas_call(project_kernel, grid_spec=pltpu.PrefetchScalarGridSpec(num...  14.4 us
    pallas_call x1, Pallas kernels, student_keys(): heads_call(keys_kernel, 'student_keys', 16, [whole(ROWS, HD), whole(ROWS,...  13.8 us
    pallas_call x1, Pallas kernels, back_project(): pl.pallas_call(back_project_kernel, grid_spec=pltpu.PrefetchScalarGridSpe...  13.4 us
  transfers between devices with their start and end apart: 12, of which 9 were waited for; matrix products, arithmetic and copies ran while one was open for 4% of the time, Pallas kernels for 19%

profile of v2, /device:TPU:0, one launch (start us, length us, event | category | flops | bytes accessed | tf_op | source)
XLA Modules:
  0.0 310.5 jit_solution(12158680941024179037)
XLA Ops:
  7.2 1.0 constant_dynamic-slice_fusion.1
  8.3 0.8 pad_maximum_fusion.2
  9.1 13.8 %student_keys.1 = (f32[4,512,8]{2,1,0:T(8,128)}, f32[4,1,512]{2,1,0:T(1,128)}, bf16[4,512,128]{2,1,0:T(8,128)(2,1)}, bf16[4,512,128]{2,1,0:T(8,128)(2,1)}, bf16[...) custom-call(bf16[512,128]{1,0:T(8,128)(2,1)} %copy-done.10, ...), custom_call_target="tpu_custom_call" | custom-call | flops 17600000000 | tf_op jit(solution)/shard_map/student_keys/pallas_call | solution.py:282
  22.9 4.6 %constant_dynamic-slice_fusion = bf16[512,4096]{1,0:T(8,128)(2,1)} fusion(bf16[512,8192]{1,0:T(8,128)(2,1)} %w_mine_ref.5, s32[]{:T(128)S(6)} %select_n.21), kind=kLoop, calls=%fused_computation.23 | loop fusion | bytes 8388612 | tf_op jit(solution)/shard_map/dynamic_slice | solution.py:782
  27.5 6.4 %all-to-all-start = ((f32[8,192,128]{2,1,0:T(8,128)}), f32[8,192,128]{2,1,0:T(8,128)S(1)}, u32[]{:S(2)}, u32[]{:S(2)}) async-start(f32[8,192,128]{2,1,0:T(8,128)} %get-tuple-element.66), calls=%async_computation | async-start | bytes 1572864 | tf_op jit(solution)/shard_map/all_to_all | solution.py:758
  34.0 8.1 %student_queries.1 = (f32[4,512,8]{2,1,0:T(8,128)}, bf16[4,512,128]{2,1,0:T(8,128)(2,1)}, bf16[4,512,128]{2,1,0:T(8,128)(2,1)}, bf16[4,256,640]{2,1,0:T(8,128)(2...) custom-call(bf16[512,512]{1,0:T(8,128)(2,1)} %q_ref.7, ...), custom_call_target="tpu_custom_call" | custom-call | flops 8800000000 | tf_op jit(solution)/shard_map/student_queries/pallas_call | solution.py:328
  42.1 10.8 %all-to-all-done.message_ref = f32[8,192,128]{2,1,0:T(8,128)S(1)} async-done(((f32[8,192,128]{2,1,0:T(8,128)}), f32[8,192,128]{2,1,0:T(8,128)S(1)}, u32[]{:S(2)}, u32[]{:S(2)}) %all-to-all-start) | async-done | bytes 786464 | tf_op jit(solution)/shard_map/all_to_all | solution.py:758
  52.9 1.6 state_chain.1
  54.5 3.7 %all-to-all-start.1 = ((f32[8,64,128]{2,1,0:T(8,128)}), f32[8,64,128]{2,1,0:T(8,128)S(1)}, u32[]{:S(2)}, u32[]{:S(2)}) async-start(f32[8,64,128]{2,1,0:T(8,128)} %state_chain.1), calls=%async_computation.1 | async-start | bytes 524288 | tf_op jit(solution)/shard_map/all_to_all | solution.py:758
  58.2 1.0 all-gather.4.cloned.1.call-done.kv_ref
  59.2 1.6 copy-done.2
  60.8 0.7 teacher_0.1.teacher_ref
  61.6 0.7 copy-done.7
  62.3 3.3 %all-to-all-done.1 = f32[8,64,128]{2,1,0:T(8,128)S(1)} async-done(((f32[8,64,128]{2,1,0:T(8,128)}), f32[8,64,128]{2,1,0:T(8,128)S(1)}, u32[]{:S(2)}, u32[]{:S(2)}) %all-to-all-start.1) | async-done | bytes 262176 | tf_op jit(solution)/shard_map/all_to_all | solution.py:758
  65.6 0.7 copy-done.13
  66.3 2.4 delta_0.1.mine_ref
  68.8 2.1 collective-permute-done.other_ref
  70.9 3.4 %copy-done = bf16[512,8192]{1,0:T(8,128)(2,1)S(1)} copy-done((bf16[512,8192]{1,0:T(8,128)(2,1)S(1)}, bf16[512,8192]{1,0:T(8,128)(2,1)}, u32[]{:S(2)}) %copy-start) | copy-done | bytes 8388632
  74.3 1.0 copy-done.5
  75.3 7.2 %difference_part_0.1 = f32[8,272,512]{2,1,0:T(8,128)S(1)} custom-call(s32[1]{0:T(128)} %bitcast.core_ref, bf16[2,256,512]{2,1,0:T(8,128)(2,1)S(1)} %copy-done.5, bf16[2,256,512]{2,1,0:T(8,128)(2,1)S(1)} %collective-permute-done.other_ref, bf16[512,8192]{1,0:T(8,128)(2,1)S(1)} %copy-done, bf16[512,4096]{1,0:T(8,128)(2,1)} %collective-permute-done.1.w_other_ref), custom_call_target="tpu_custom_call" | custom-call | flops 7699999744 | tf_op jit(solution)/shard_map/difference_part_0/pallas_call | solution.py:537
  82.5 1.9 convert_element_type.45
  84.4 6.5 %all-to-all-start.2 = ((f16[8,272,512]{2,1,0:T(8,128)(2,1)}), f16[8,272,512]{2,1,0:T(8,128)(2,1)}, u32[]{:S(2)}, u32[]{:S(2)}) async-start(f16[8,272,512]{2,1,0:T(8,128)(2,1)} %convert_element_type.45), calls=%async_computation.2 | async-start | bytes 4456448 | tf_op jit(solution)/shard_map/all_to_all | solution.py:758
  91.0 1.1 teacher_1.1.teacher_ref
  92.1 0.7 copy-done.8
  92.8 2.4 delta_1.1.mine_ref
  95.2 2.1 collective-permute-done.2.other_ref
  97.3 3.4 %copy-done.1 = bf16[512,8192]{1,0:T(8,128)(2,1)S(1)} copy-done((bf16[512,8192]{1,0:T(8,128)(2,1)S(1)}, bf16[512,8192]{1,0:T(8,128)(2,1)}, u32[]{:S(2)}) %copy-start.1) | copy-done | bytes 8388632
  100.7 1.0 copy-done.6
  101.7 7.2 %difference_part_1.1 = f32[8,272,512]{2,1,0:T(8,128)S(1)} custom-call(s32[1]{0:T(128)} %bitcast.core_ref, bf16[2,256,512]{2,1,0:T(8,128)(2,1)S(1)} %copy-done.6, bf16[2,256,512]{2,1,0:T(8,128)(2,1)S(1)} %collective-permute-done.2.other_ref, bf16[512,8192]{1,0:T(8,128)(2,1)S(1)} %copy-done.1, bf16[512,4096]{1,0:T(8,128)(2,1)} %collective-permute-done.1.w_other_ref), custom_call_target="tpu_custom_call" | custom-call | flops 7699999744 | tf_op jit(solution)/shard_map/difference_part_1/pallas_call | solution.py:537
  108.9 1.9 convert_element_type.49
  110.9 10.4 %all-to-all-done.2 = f16[8,272,512]{2,1,0:T(8,128)(2,1)} async-done(((f16[8,272,512]{2,1,0:T(8,128)(2,1)}), f16[8,272,512]{2,1,0:T(8,128)(2,1)}, u32[]{:S(2)}, u32[]{:S(2)}) %all-to-all-start.2) | async-done | bytes 2228256 | tf_op jit(solution)/shard_map/all_to_all | solution.py:758
  121.2 8.0 %all-to-all-start.3 = ((f16[8,272,512]{2,1,0:T(8,128)(2,1)}), f16[8,272,512]{2,1,0:T(8,128)(2,1)S(1)}, u32[]{:S(2)}, u32[]{:S(2)}) async-start(f16[8,272,512]{2,1,0:T(8,128)(2,1)} %convert_element_type.49), calls=%async_computation.3 | async-start | bytes 4456448 | tf_op jit(solution)/shard_map/all_to_all | solution.py:758
  129.2 11.2 %backward_ready.1 = (bf16[4,512,128]{2,1,0:T(8,128)(2,1)}, bf16[4,512,128]{2,1,0:T(8,128)(2,1)}, bf16[4,512,128]{2,1,0:T(8,128)(2,1)}, bf16[4,512,128]{2,1,0:T(8...) custom-call(bf16[4,512,256]{2,1,0:T(8,128)(2,1)} %get-tuple-element.72.xh_ref, ...), custom_call_target="tpu_custom_call" | custom-call | flops 11000000512 | tf_op jit(solution)/shard_map/backward_ready/pallas_call | solution.py:509
  140.5 0.9 fusion.3
  141.4 0.9 multiply_exponential_fusion.1
  142.3 2.9 multiply_reduce_fusion.1
  145.2 13.0 %all-to-all-done.3 = f16[8,272,512]{2,1,0:T(8,128)(2,1)S(1)} async-done(((f16[8,272,512]{2,1,0:T(8,128)(2,1)}), f16[8,272,512]{2,1,0:T(8,128)(2,1)S(1)}, u32[]{:S(2)}, u32[]{:S(2)}) %all-to-all-start.3) | async-done | bytes 2228256 | tf_op jit(solution)/shard_map/all_to_all | solution.py:758
  158.3 0.5 multiply_reduce_fusion
  158.7 1.2 select_convert_fusion.1
  160.0 0.1 pad_maximum_fusion
  160.1 48.4 %all-gather.5 = f16[4352,512]{1,0:T(8,128)(2,1)S(1)} all-gather(f16[544,512]{1,0:T(8,128)(2,1)S(1)} %pad_maximum_fusion), channel_id=2, replica_groups={{0,2,4,6,8,10,12,14},{1,3,5,7,9,11,13,15},{16,18,20,22,24,26,28,30},{17..., dimensions={0}, use_global_device_ids=true | all-gather | bytes 5013504 | tf_op jit(solution)/shard_map/all_gather | solution.py:805
  208.6 3.4 %fusion.2 = (bf16[8,544,512]{2,1,0:T(8,128)(2,1)}, bf16[8,544,512]{2,1,0:T(8,128)(2,1)S(1)}) fusion(f16[8,544,512]{2,1,0:T(8,128)(2,1)S(1)} %bitcast.30, f32[8,2,512]{2,1,0:T(2,128)S(1)} %exponential_bitcast_fusion), kind=kLoop, calls=%fused_computation.3 | loop fusion | flops 13369344 | bytes 13402112 | tf_op jit(solution)/shard_map/convert_element_type | solution.py:52
  212.0 13.4 %head_grad_part.1 = (f32[512,512]{1,0:T(8,128)S(1)}, f32[512,512]{1,0:T(8,128)S(1)}, f32[8,512]{1,0:T(8,128)S(1)}) custom-call(s32[1]{0:T(128)} %bitcast.core_ref, bf16[8,544,512]{2,1,0:T(8,128)(2,1)S(1)} %get-tuple-element.128.high_ref, bf16[8,544,512]{2,1,0:T(8,128)(2,1)} %get-tuple-element.127.low_ref, bf16[512,8192]{1,0:T(8,128)(2,1)} %w_mine_ref.5, ...), custom_call_target="tpu_custom_call" | custom-call | flops 15399999488 | tf_op jit(solution)/shard_map/head_grad_part/pallas_call | solution.py:585
  225.3 1.0 copy-done.9
  226.3 0.6 reduce_sum.38
  226.9 0.6 broadcast_in_dim.29
  227.6 0.6 collective-permute-start.4
  228.2 0.8 collective-permute-done.4
  229.0 0.6 broadcast_add_fusion
  229.7 1.1 copy-done.15
  230.7 2.8 state_grad_local.1
  233.5 8.9 %all-to-all-start.4 = ((f32[8,64,128]{2,1,0:T(8,128)}), f32[8,64,128]{2,1,0:T(8,128)S(1)}, u32[]{:S(2)}, u32[]{:S(2)}) async-start(f32[8,64,128]{2,1,0:T(8,128)} %bitcast.37), calls=%async_computation.4 | async-start | bytes 524288 | tf_op jit(solution)/shard_map/all_to_all | solution.py:758
  242.5 8.4 %query_grad.1 = (f32[4,128,128]{2,1,0:T(8,128)}, f32[4,512,128]{2,1,0:T(8,128)}) custom-call(bf16[512,512]{1,0:T(8,128)(2,1)} %get-tuple-element.108.gh_ref, bf16[512,512]{1,0:T(8,128)(2,1)} %get-tuple-element.109.gl_ref, bf16[4,512,128]{2,1,0:T(8,128)(2,1)} %get-tuple-element.110.nh_ref, bf16[4,512,128]{2,1,0:T(8,128)(2,1)} %get-tuple-element.111.nl_ref, ...), custom_call_target="tpu_custom_call" | custom-call | flops 8800000000 | tf_op jit(solution)/shard_map/query_grad/pallas_call | solution.py:686
  250.9 1.6 state_grad_chain.1
  252.5 5.7 %all-to-all-start.5 = ((f32[8,64,128]{2,1,0:T(8,128)}), f32[8,64,128]{2,1,0:T(8,128)S(1)}, u32[]{:S(2)}, u32[]{:S(2)}) async-start(f32[8,64,128]{2,1,0:T(8,128)} %state_grad_chain.1), calls=%async_computation.5 | async-start | bytes 524288 | tf_op jit(solution)/shard_map/all_to_all | solution.py:758
  258.2 3.4 %update_grad_local.1.y_ref = f32[4,512,128]{2,1,0:T(8,128)} custom-call(bf16[512,512]{1,0:T(8,128)(2,1)} %get-tuple-element.108.gh_ref, bf16[512,512]{1,0:T(8,128)(2,1)} %get-tuple-element.109.gl_ref, bf16[4,256,640]{2,1,0:T(8,128)(2,1)} %get-tuple-element.121.bh_ref, bf16[4,256,640]{2,1,0:T(8,128)(2,1)} %get-tuple-element.122.bl_ref), custom_call_target="tpu_custom_call" | custom-call | flops 4400000000 | tf_op jit(solution)/shard_map/update_grad_local/pallas_call | solution.py:643
  261.6 3.8 %all-to-all-done.5 = f32[8,64,128]{2,1,0:T(8,128)S(1)} async-done(((f32[8,64,128]{2,1,0:T(8,128)}), f32[8,64,128]{2,1,0:T(8,128)S(1)}, u32[]{:S(2)}, u32[]{:S(2)}) %all-to-all-start.5) | async-done | bytes 262176 | tf_op jit(solution)/shard_map/all_to_all | solution.py:758
  265.4 0.7 copy-done.14
  266.1 10.0 %key_grad.1 = f32[4,128,128]{2,1,0:T(8,128)} custom-call(f32[4,512,128]{2,1,0:T(8,128)} %update_grad_local.1.y_ref, bf16[4,512,128]{2,1,0:T(8,128)(2,1)} %get-tuple-element.123.th_ref, bf16[4,512,128]{2,1,0:T(8,128)(2,1)} %get-tuple-element.124.tl_ref, bf16[4,512,128]{2,1,0:T(8,128)(2,1)} %get-tuple-element.110.nh_ref, ...), custom_call_target="tpu_custom_call" | custom-call | flops 9900000256 | tf_op jit(solution)/shard_map/key_grad/pallas_call | solution.py:729
  276.2 1.0 pad_maximum_fusion.1
  277.2 11.8 %all_to_all.40 = f32[8,136,128]{2,1,0:T(8,128)S(1)} all-to-all(f32[8,136,128]{2,1,0:T(8,128)S(1)} %pad_maximum_fusion.1), channel_id=1, replica_groups=mesh['ctx'=8,'head'=16] {'ctx'}, dimensions={0} | all-to-all | bytes 1114112 | tf_op jit(solution)/shard_map/all_to_all | solution.py:758
  289.1 11.4 %all_to_all.41 = f32[8,136,128]{2,1,0:T(8,128)S(1)} all-to-all(f32[8,136,128]{2,1,0:T(8,128)S(1)} %broadcast_in_dim.31), channel_id=1, replica_groups=mesh['ctx'=8,'head'=16] {'ctx'}, dimensions={0} | all-to-all | bytes 1114112 | tf_op jit(solution)/shard_map/all_to_all | solution.py:758
  300.5 0.5 slice.26
  301.7 0.8 fusion.4
  (42 shorter events, 0.4 us)
Async XLA Ops:
  7.2 52.1 %all-gather.4.cloned.1.call-start = ((), (), s32[]{:S(2)}) async-start(), calls=%async_computation.8 | async-start | bytes 2359296 | tf_op jit(solution)/shard_map/all_gather | solution.py:768
  8.2 0.8 copy-start.10
  8.2 0.8 copy-start.11
  27.5 41.2 %collective-permute-start.1 = (bf16[512,4096]{1,0:T(8,128)(2,1)}, bf16[512,4096]{1,0:T(8,128)(2,1)}, u32[]{:S(2)}, u32[]{:S(2)}) collective-permute-start(bf16[512,4096]{1,0:T(8,128)(2,1)} %constant_dynamic-slice_fusion), channel_id=1, source_target_pairs={{0,1},{1,0},{2,3},{3,2},{4,5},{5,4},{6,7},{7,6},{8,9},{9,8},{10,11... | collective-permute-start | bytes 12582920 | tf_op jit(solution)/shard_map/ppermute | solution.py:781
  27.5 25.4 %all-to-all-start = ((f32[8,192,128]{2,1,0:T(8,128)}), f32[8,192,128]{2,1,0:T(8,128)S(1)}, u32[]{:S(2)}, u32[]{:S(2)}) async-start(f32[8,192,128]{2,1,0:T(8,128)} %get-tuple-element.66), calls=%async_computation | async-start | bytes 1572864 | tf_op jit(solution)/shard_map/all_to_all | solution.py:758
  52.9 6.3 %copy-start.4 = (bf16[512,512]{1,0:T(8,128)(2,1)S(1)}, bf16[512,512]{1,0:T(8,128)(2,1)}, u32[]{:S(2)}) copy-start(bf16[512,512]{1,0:T(8,128)(2,1)} %q_ref.7) | copy-start | bytes 1572868
  54.5 11.1 %all-to-all-start.1 = ((f32[8,64,128]{2,1,0:T(8,128)}), f32[8,64,128]{2,1,0:T(8,128)S(1)}, u32[]{:S(2)}, u32[]{:S(2)}) async-start(f32[8,64,128]{2,1,0:T(8,128)} %state_chain.1), calls=%async_computation.1 | async-start | bytes 524288 | tf_op jit(solution)/shard_map/all_to_all | solution.py:758
  59.2 1.6 copy-start.2
  61.6 0.7 copy-start.7
  65.6 0.7 copy-start.13
  68.7 2.1 collective-permute-start
  70.9 3.4 %copy-start = (bf16[512,8192]{1,0:T(8,128)(2,1)S(1)}, bf16[512,8192]{1,0:T(8,128)(2,1)}, u32[]{:S(2)}) copy-start(bf16[512,8192]{1,0:T(8,128)(2,1)} %w_mine_ref.5) | copy-start | bytes 25165828
  74.2 1.0 copy-start.5
  82.5 8.5 %copy-start.3 = (bf16[4096,256]{1,0:T(8,128)(2,1)S(1)}, bf16[4096,256]{1,0:T(8,128)(2,1)}, u32[]{:S(2)}) copy-start(bf16[4096,256]{1,0:T(8,128)(2,1)} %all-gather.4.cloned.1.call-done.kv_ref) | copy-start | bytes 6291460
  84.4 36.8 %all-to-all-start.2 = ((f16[8,272,512]{2,1,0:T(8,128)(2,1)}), f16[8,272,512]{2,1,0:T(8,128)(2,1)}, u32[]{:S(2)}, u32[]{:S(2)}) async-start(f16[8,272,512]{2,1,0:T(8,128)(2,1)} %convert_element_type.45), calls=%async_computation.2 | async-start | bytes 4456448 | tf_op jit(solution)/shard_map/all_to_all | solution.py:758
  92.1 0.7 copy-start.8
  95.2 2.1 collective-permute-start.2
  97.3 3.4 %copy-start.1 = (bf16[512,8192]{1,0:T(8,128)(2,1)S(1)}, bf16[512,8192]{1,0:T(8,128)(2,1)}, u32[]{:S(2)}) copy-start(bf16[512,8192]{1,0:T(8,128)(2,1)} %w_mine_ref.5) | copy-start | bytes 25165828
  100.7 1.0 copy-start.6
  121.2 36.9 %all-to-all-start.3 = ((f16[8,272,512]{2,1,0:T(8,128)(2,1)}), f16[8,272,512]{2,1,0:T(8,128)(2,1)S(1)}, u32[]{:S(2)}, u32[]{:S(2)}) async-start(f16[8,272,512]{2,1,0:T(8,128)(2,1)} %convert_element_type.49), calls=%async_computation.3 | async-start | bytes 4456448 | tf_op jit(solution)/shard_map/all_to_all | solution.py:758
  225.3 1.0 copy-start.9
  226.3 3.3 %collective-permute-start.3 = (f32[512,512]{1,0:T(8,128)S(1)}, f32[512,512]{1,0:T(8,128)S(1)}, u32[]{:S(2)}, u32[]{:S(2)}) collective-permute-start(f32[512,512]{1,0:T(8,128)S(1)} %get-tuple-element.105), channel_id=1, source_target_pairs={{0,1},{1,0},{2,3},{3,2},{4,5},{5,4},{6,7},{7,6},{8,9},{9,8},{10,11... | collective-permute-start | bytes 3145736 | tf_op jit(solution)/shard_map/ppermute | solution.py:817
  227.6 1.4 collective-permute-start.4
  229.6 1.1 copy-start.15
  233.5 17.3 %all-to-all-start.4 = ((f32[8,64,128]{2,1,0:T(8,128)}), f32[8,64,128]{2,1,0:T(8,128)S(1)}, u32[]{:S(2)}, u32[]{:S(2)}) async-start(f32[8,64,128]{2,1,0:T(8,128)} %bitcast.37), calls=%async_computation.4 | async-start | bytes 524288 | tf_op jit(solution)/shard_map/all_to_all | solution.py:758
  252.5 12.9 %all-to-all-start.5 = ((f32[8,64,128]{2,1,0:T(8,128)}), f32[8,64,128]{2,1,0:T(8,128)S(1)}, u32[]{:S(2)}, u32[]{:S(2)}) async-start(f32[8,64,128]{2,1,0:T(8,128)} %state_grad_chain.1), calls=%async_computation.5 | async-start | bytes 524288 | tf_op jit(solution)/shard_map/all_to_all | solution.py:758
  265.4 0.7 copy-start.14
  266.1 10.0 %copy-start.12 = (f32[4,128,128]{2,1,0:T(8,128)S(1)}, f32[4,128,128]{2,1,0:T(8,128)}, u32[]{:S(2)}) copy-start(f32[4,128,128]{2,1,0:T(8,128)} %get-tuple-element.115) | copy-start | bytes 786436
Sparse Core Ops, SparseCore 0:
  10.2 48.9 all-gather.3

commit v3 on v2

--- a/solution.py
+++ b/solution.py
@@ -20,7 +20,7 @@
 CTX = 8
 CHIPS = 8
 PIECE = 512
-PAD = 16
+PAD = 8
 SAME_CORE = [[2 * p + core for p in range(CHIPS)] for core in range(2)]
 
 f32 = jnp.float32
@@ -29,8 +29,8 @@
 
 MIB = 1024 * 1024
 FLOOR = 0
-PROJECT_MIB = 24
-BACK_MIB = 40
+PROJECT_MIB = 45
+BACK_MIB = 44
 PSTEP = 2
 STEP = 1
 HALF = ROWS // 2
@@ -123,6 +123,13 @@
         ref[n, at : at + BLK, left : left + BLK * (i + 1)] = part
 
 
+def joined(blocks):
+    return tuple(
+        jnp.concatenate([jnp.concatenate([b[p] for b in line], axis=1) for line in blocks], axis=0)
+        for p in range(2)
+    )
+
+
 def loaded(refs, n):
     return refs[0][n], refs[1][n]
 
@@ -171,16 +178,16 @@
     jj = lax.broadcasted_iota(jnp.int32, (BLK, BLK), 1)
     diagonal = (ii == jj).astype(f32)
     first = ((ii >> 1) == (jj >> 1)) & (ii > jj)
-    found = [diagonal - jnp.where(first, block, 0.0) for block in blocks]
-    whole_parts = [split(block) for block in blocks]
+    found = [split(diagonal - jnp.where(first, block, 0.0)) for block in blocks]
+    whole_parts = [split(-block) for block in blocks]
     none = jnp.zeros((BLK, BLK), bf16)
     shift = 1
     while (1 << shift) < BLK:
         mask = ((ii >> (shift + 1)) == (jj >> (shift + 1))) & ((ii >> shift) > (jj >> shift))
-        parts = [split(x) for x in found]
         corner = [tuple(jnp.where(mask, part, none) for part in pair) for pair in whole_parts]
-        inner = [split(mm3(c, x, NN)) for c, x in zip(corner, parts)]
-        found = [x - mm3(p, y, NN) for x, p, y in zip(found, parts, inner)]
+        inner = [split(mm3(c, x, NN)) for c, x in zip(corner, found)]
+        more = [split(mm3(x, y, NN)) for x, y in zip(found, inner)]
+        found = [(x[0] + y[0], x[1] + y[1]) for x, y in zip(found, more)]
         shift += 1
     return found
 
@@ -252,7 +259,7 @@
         rights.append(beside(write * v_ref[...].astype(f32), (write * growth) * uk))
         ends.append(end)
     found = inverses([lower[n][i][:, BLK * i :] for n in heads for i in range(NB)])
-    inverse = [[split(found[n * NB + i]) for i in range(NB)] for n in heads]
+    inverse = [[found[n * NB + i] for i in range(NB)] for n in heads]
     solved = [None] * KSTEP
     for i in range(NB):
         lo, hi = BLK * i, BLK * (i + 1)
@@ -455,6 +462,7 @@
         [rows, rows, rows, per_head(HD, HD, step=DSTEP), pl.BlockSpec((HALF, DSTEP * HD), lambda h: (0, h))],
         pl.BlockSpec((2, HALF, DSTEP * HD), lambda h: (0, 0, h)),
         jax.ShapeDtypeStruct((2, HALF, HEADS * HD), bf16),
+        mib=24,
         step=DSTEP,
     )(own, *reach, state, teacher)
 
@@ -543,7 +551,7 @@
                 pl.BlockSpec((2, HALF, width), lambda j, c: (0, 0, 0)),
                 pl.BlockSpec((2, HALF, width), lambda j, c: (0, 0, 0)),
                 pl.BlockSpec((width, PSTEP * PIECE), lambda j, c: (0, c[0] * (CHIPS // PSTEP) + j)),
-                pl.BlockSpec((width, PSTEP * PIECE), lambda j, c: (0, j)),
+                pl.BlockSpec((width, PSTEP * PIECE), lambda j, c: (0, c[0] * (CHIPS // PSTEP) + j)),
             ],
             out_specs=pl.BlockSpec((PSTEP, HALF + PAD, PIECE), lambda j, c: (j, 0, 0)),
         ),
@@ -557,8 +565,7 @@
 def back_project_kernel(
     core_ref, high_ref, low_ref, w_mine_ref, w_other_ref, mine_ref, other_ref, square_ref
 ):
-    rows = (slice(0, HALF), slice(HALF + PAD, ROWS + PAD))
-    both = jnp.concatenate([ref[0, at, :] for ref in (high_ref, low_ref) for at in rows], axis=0)
+    both = jnp.concatenate([high_ref[0, :ROWS, :], low_ref[0, :ROWS, :]], axis=0)
     mine = mm(both, w_mine_ref[...], NT)
     other = mm(both, w_other_ref[...], NT)
     mine = mine[:ROWS] + mine[ROWS:]
@@ -569,13 +576,15 @@
     @pl.when(pl.program_id(0) == 0)
     def _():
         mine_ref[...] = mine
-        other_ref[...] = other
+        other_ref[:ROWS, :] = other
+        other_ref[ROWS:, :] = square
         square_ref[...] = square
 
     @pl.when(pl.program_id(0) > 0)
     def _():
         mine_ref[...] += mine
-        other_ref[...] += other
+        other_ref[:ROWS, :] += other
+        other_ref[ROWS:, :] += square
         square_ref[...] += square
 
 
@@ -591,17 +600,17 @@
                 columns,
                 columns,
                 pl.BlockSpec((width, PIECE), lambda j, c: (0, c[0] * CHIPS + j)),
-                pl.BlockSpec((width, PIECE), lambda j, c: (0, j)),
+                pl.BlockSpec((width, PIECE), lambda j, c: (0, c[0] * CHIPS + j)),
             ],
             out_specs=[
                 pl.BlockSpec((ROWS, width), lambda j, c: (0, 0)),
-                pl.BlockSpec((ROWS, width), lambda j, c: (0, 0)),
+                pl.BlockSpec((ROWS + 8, width), lambda j, c: (0, 0)),
                 pl.BlockSpec((8, PIECE), lambda j, c: (0, 0)),
             ],
         ),
         out_shape=[
             jax.ShapeDtypeStruct((ROWS, width), f32),
-            jax.ShapeDtypeStruct((ROWS, width), f32),
+            jax.ShapeDtypeStruct((ROWS + 8, width), f32),
             jax.ShapeDtypeStruct((8, PIECE), f32),
         ],
         compiler_params=params(BACK_MIB),
@@ -610,24 +619,36 @@
     )(core, high, low, w_mine, w_other)
 
 
-def state_grad_kernel(mine_ref, other_ref, rh_ref, rl_ref, gh_ref, gl_ref, out_ref):
+def state_grad_kernel(
+    mine_ref, other_ref, square_ref, rh_ref, rl_ref, gh_ref, gl_ref, out_ref, total_ref
+):
     for n in range(DSTEP):
         at = slice(HD * n, HD * (n + 1))
-        grad = split(mine_ref[:, at] + other_ref[:, at])
+        grad = split(mine_ref[:, at] + other_ref[:ROWS, at])
         gh_ref[:, at] = grad[0]
         gl_ref[:, at] = grad[1]
         out_ref[n] = mm3(grad, loaded((rh_ref, rl_ref), n), TN)
-
-
-def state_grad_local(mine, other, reach):
+        total_ref[n] = square_ref[:, at] + other_ref[ROWS:, at]
+
+
+def state_grad_local(mine, other, squares, reach):
     return heads_call(
-        state_grad_kernel, "state_grad_local", 4,
-        [columns_spec(DSTEP), columns_spec(DSTEP), per_head(ROWS, HD, step=DSTEP), per_head(ROWS, HD, step=DSTEP)],
-        [columns_spec(DSTEP), columns_spec(DSTEP), per_head(HD, HD, step=DSTEP)],
+        state_grad_kernel, "state_grad_local", 2,
+        [
+            columns_spec(DSTEP),
+            pl.BlockSpec((ROWS + 8, DSTEP * HD), lambda h: (0, h)),
+            pl.BlockSpec((8, DSTEP * HD), lambda h: (0, h)),
+            per_head(ROWS, HD, step=DSTEP), per_head(ROWS, HD, step=DSTEP),
+        ],
+        [
+            columns_spec(DSTEP), columns_spec(DSTEP),
+            per_head(HD, HD, step=DSTEP), per_head(8, HD, step=DSTEP),
+        ],
         [jax.ShapeDtypeStruct((ROWS, HEADS * HD), bf16)] * 2
-        + [jax.ShapeDtypeStruct((HEADS, HD, HD), f32)],
+        + [jax.ShapeDtypeStruct((HEADS, HD, HD), f32), jax.ShapeDtypeStruct((HEADS, 8, HD), f32)],
+        mib=24,
         step=DSTEP,
-    )(mine, other, *reach)
+    )(mine, other, squares, *reach)
 
 
 def inner_kernel(gh_ref, gl_ref, bh_ref, bl_ref, y_ref):
@@ -662,21 +683,18 @@
         updates = loaded((nh_ref, nl_ref), n)
         uks, uqs = loaded((ukh_ref, ukl_ref), n), loaded((uqh_ref, uql_ref), n)
         from_state = column_of(cols_ref, n, GROWTH) * mm3(grad, split(state_ref[n]), NN)
-        total = [None] * NB
-        query_total = []
+        none = (jnp.zeros((BLK, BLK), bf16),) * 2
+        blocks = [[none] * NB for _ in range(NB)]
         for i in range(NB):
             lo, hi = BLK * i, BLK * (i + 1)
             outer = mm3(rows_of(grad, lo, hi), rows_of(updates, 0, hi), NT)
-            through = split(outer * decays(column_of(cols_ref, n, COLUMN), row_ref[n], i))
-            query_total.append(from_state[lo:hi] + mm3(through, rows_of(uks, 0, hi), NN))
-            columns = mm3(through, rows_of(uqs, lo, hi), TN)
+            scaled = outer * decays(column_of(cols_ref, n, COLUMN), row_ref[n], i)
             for j in range(i + 1):
-                more = columns[BLK * j : BLK * (j + 1)]
-                total[j] = more if total[j] is None else total[j] + more
-        for j in range(NB):
-            key_ref[n, BLK * j : BLK * (j + 1), :] = total[j]
+                blocks[i][j] = split(scaled[:, BLK * j : BLK * (j + 1)])
+        through = joined(blocks)
+        key_ref[n] = mm3(through, uqs, TN)
         uq = uqs[0].astype(f32) + uqs[1].astype(f32)
-        query_grad = jnp.concatenate(query_total, axis=0)
+        query_grad = from_state + mm3(through, uks, NN)
         query_grad = split(through_unit(query_grad, uq, inverse_ref[n, :, :1]))
         q = q_ref[:, at]
         grad_ref[n] = halves(mm(q, beside(*query_grad), TN))
@@ -709,18 +727,19 @@
         write = column_of(cols_ref, n, WRITE)
         base = key_ref[n] + column_of(cols_ref, n, TAIL) * mm3(updates, state_grad, NN)
         base = base - column_of(cols_ref, n, WRITE_GROWTH) * mm3(inner, split(state_ref[n]), NN)
-        total = [base[BLK * j : BLK * (j + 1)] for j in range(NB)]
+        both = [[None] * NB for _ in range(NB)]
         for i in range(NB):
             lo, hi = BLK * i, BLK * (i + 1)
             outer = mm3(rows_of(inner, lo, hi), rows_of(updates, 0, hi), NT)
             scaled = outer * decays(column_of(cols_ref, n, COLUMN), row_ref[n], i) * write[lo:hi]
-            through = split(jnp.where(strict(i), scaled, 0.0))
-            total[i] = total[i] - mm3(through, rows_of(uks, 0, hi), NN)
-            columns = mm3(through, rows_of(uks, lo, hi), TN)
-            for j in range(i + 1):
-                total[j] = total[j] - columns[BLK * j : BLK * (j + 1)]
+            through = jnp.where(strict(i), scaled, 0.0)
+            for j in range(i):
+                part = through[:, BLK * j : BLK * (j + 1)]
+                both[i][j], both[j][i] = split(part), split(part.T)
+            part = through[:, lo:hi]
+            both[i][i] = split(part + part.T)
+        key_grad = base - mm3(joined(both), uks, NN)
         uk = uks[0].astype(f32) + uks[1].astype(f32)
-        key_grad = jnp.concatenate(total, axis=0)
         key_grad = split(through_unit(key_grad, uk, column_of(cols_ref, n, INVERSE)))
         grad_ref[n] = halves(mm(k_ref[...], beside(*key_grad), TN))
 
@@ -746,12 +765,14 @@
     exponents = pieces[:, -1:, :].astype(f32)
     exponent = jnp.min(exponents, axis=0) - 3.0
     total = jnp.sum(pieces.astype(f32) * jnp.exp2(exponent[None] - exponents), axis=0)
-    at = lax.broadcasted_iota(jnp.int32, total.shape, 0)
-    return jnp.where(at < total.shape[0] - PAD, total, exponent).astype(f16)
+    return total[:-PAD].astype(f16), jnp.broadcast_to(exponent, (PAD, PIECE)).astype(f16)
 
 
 def rescaled(message):
-    return message.astype(f32) * jnp.exp2(-message[..., -1:, :].astype(f32))
+    exponent = message[:, -2 * PAD :: PAD, :].astype(f32)
+    at = lax.broadcasted_iota(jnp.int32, message.shape, 1)
+    scale = jnp.exp2(-exponent)
+    return message.astype(f32) * jnp.where(at < HALF, scale[:, :1], scale[:, 1:])
 
 
 def transpose_over(x, axis, groups=None):
@@ -768,6 +789,8 @@
     kv = lax.all_gather(
         jnp.concatenate([key_mine, value_mine], axis=1), "ctx", axis=0, tiled=True
     )
+    partner = [(i, i ^ 1) for i in range(2 * CHIPS)]
+    w_other = lax.ppermute(out_weight, "head", partner)
     cols, row, *pairs, message = student_keys(
         key_mine, value_mine, log_decay, write_strength, key_map
     )
@@ -775,12 +798,6 @@
     ctx_scalar = ctx.astype(jnp.int32).reshape(1)
     core_scalar = core.astype(jnp.int32).reshape(1)
     messages = transpose_over(message, "ctx")
-    partner = [(i, i ^ 1) for i in range(2 * CHIPS)]
-    half = D // 2
-    core_after, _ = lax.optimization_barrier((core, message))
-    w_other = lax.ppermute(
-        lax.dynamic_slice_in_dim(out_weight, (1 - core_after) * half, half, 1), "head", partner
-    )
     cols_after, _ = lax.optimization_barrier((cols, message))
     q_inverse, *pairs = student_queries(queries, query_map, cols_after, row, uk, solved)
     uq, attend, own, reach = pairs[:2], pairs[2:4], pairs[4], pairs[5:]
@@ -802,19 +819,17 @@
     *pairs, = student_ready(solved, lower, inverse, uk, cols, state_after, attend)
     sent[1], pairs = lax.optimization_barrier((sent[1], pairs))
     updates, moved, through = pairs[:2], pairs[2:4], pairs[4:]
+    first, second = [summed(pieces) for pieces in sent]
     gathered = lax.all_gather(
-        jnp.concatenate([summed(pieces) for pieces in sent], axis=0),
+        jnp.concatenate([first[0], second[0], first[1], second[1]], axis=0),
         "head", axis=0, axis_index_groups=SAME_CORE, tiled=False,
     )
-    columns_high, columns_low = split(rescaled(gathered.reshape(CHIPS, 2, HALF + PAD, PIECE)))
-    together = (CHIPS, ROWS + 2 * PAD, PIECE)
+    columns_high, columns_low = split(rescaled(gathered))
     grad_mine, grad_other, squares = back_project(
-        core_scalar, columns_high.reshape(together), columns_low.reshape(together), out_weight, w_other
-    )
-    square_mine = jnp.broadcast_to(jnp.sum(squares), (8, HD))
-    square_other = lax.ppermute(square_mine, "head", partner)
-    grad_high, grad_low, local = state_grad_local(
-        grad_mine, lax.ppermute(grad_other, "head", partner), reach
+        core_scalar, columns_high, columns_low, out_weight, w_other
+    )
+    grad_high, grad_low, local, squares = state_grad_local(
+        grad_mine, lax.ppermute(grad_other, "head", partner), squares, reach
     )
     locals_ = transpose_over(local.reshape(CTX, HD // 2, HD), "ctx")
     (grad_high, grad_low), _ = lax.optimization_barrier(((grad_high, grad_low), local))
@@ -831,12 +846,12 @@
         inner, moved, updates, row, uk, cols, state, state_grad, partial, key_mine
     )
     grads = jnp.concatenate([query_grad, key_grad], axis=0)
-    extra = jnp.broadcast_to(square_mine + square_other, (2 * HEADS, 8, HD))
+    extra = jnp.concatenate([squares, squares], axis=0)
     shared = transpose_over(jnp.concatenate([grads, extra], axis=1), "ctx")
     total = jnp.sum(shared, axis=0, keepdims=True)
     final = transpose_over(jnp.broadcast_to(total, (CTX,) + total.shape[1:]), "ctx")
     normalizer = CTX * ROWS * D
-    return final[0, HD, 0] / normalizer, final[:HEADS, :HD], final[HEADS:, :HD]
+    return jnp.sum(final[:HEADS, HD:]) / normalizer, final[:HEADS, :HD], final[HEADS:, :HD]
 
 
 def solution(mesh):

time: 312 us -> 302 us (0.968)
  local copies, waits for them, and re-layouts: 23 us -> 9.86 us
  waiting for transfers between devices: 47.4 us -> 56 us
  Pallas kernels: 95.5 us -> 88.7 us
    unnamed x34 -> x42, local copies, waits for them, and re-layouts: 15.3 us -> 7.02 us
    all_gather x1, waiting for transfers between devices: 1.02 us -> 6.51 us  [shards(): lax.all_gather(jnp.concatenate([key_mine, value_mine], axis=1), 'ctx', ax...]
    dynamic_slice x1 -> x0, local copies, waits for them, and re-layouts: 4.63 us -> none  [shards(): lax.dynamic_slice_in_dim(out_weight, (1 - core_after) * half, half, 1)]
    pallas_call x2, Pallas kernels: 4.85 us -> 1.46 us  [student_delta(): heads_call(delta_kernel, f'delta_{half}', 2, [rows, rows, rows, per_head(...]
  transfers between devices with their start and end apart: 12 -> 11, of which waited for: 9 -> 8; matrix products, arithmetic and copies ran while one was open for 4% -> 3% of each run, Pallas kernels for 19% -> 19%
where the time goes in v3:
time: 302 us; the launch traced here: 300 us
  Pallas kernels  88.7 us (29%)
  blocking collectives  72.2 us (24%)
  waiting for transfers between devices  56 us (19%)
  starting transfers between devices  41.4 us (14%)
  between operations  16.2 us (5%)
  other arithmetic  15.7 us (5%)
  local copies, waits for them, and re-layouts  9.86 us (3%)
    all_gather x1, blocking collectives, shards(): lax.all_gather(jnp.concatenate([first[0], second[0], first[1], second[1]]...  49.1 us
    all_to_all x6, waiting for transfers between devices, transpose_over(): return lax.all_to_all(x, axis, 0, 0, axis_index_groups=groups, tiled=True)  43.1 us
    all_to_all x6, starting transfers between devices, transpose_over(): return lax.all_to_all(x, axis, 0, 0, axis_index_groups=groups, tiled=True)  41.1 us
    all_to_all x2, blocking collectives, transpose_over(): return lax.all_to_all(x, axis, 0, 0, axis_index_groups=groups, tiled=True)  23.1 us
    pallas_call x2, Pallas kernels, project(): pl.pallas_call(project_kernel, grid_spec=pltpu.PrefetchScalarGridSpec(num...  14.9 us
    pallas_call x1, Pallas kernels, student_keys(): heads_call(keys_kernel, 'student_keys', 16, [whole(ROWS, HD), whole(ROWS,...  13.8 us
    pallas_call x1, Pallas kernels, back_project(): pl.pallas_call(back_project_kernel, grid_spec=pltpu.PrefetchScalarGridSpe...  13.4 us
    pallas_call x1, Pallas kernels, student_ready(): heads_call(ready_kernel, 'backward_ready', 10, [per_head(ROWS, 2 * HD), p...  11.2 us
  transfers between devices with their start and end apart: 11, of which 8 were waited for; matrix products, arithmetic and copies ran while one was open for 3% of the time, Pallas kernels for 19%

profile of v3, /device:TPU:0, one launch (start us, length us, event | category | flops | bytes accessed | tf_op | source)
XLA Modules:
  0.0 300.1 jit_solution(8688229563599830429)
XLA Ops:
  7.2 0.0 all-gather.4.cloned.1.call-start
  7.2 0.1 collective-permute-start.1
  7.3 1.0 constant_dynamic-slice_fusion
  8.3 0.8 pad_maximum_fusion.1
  9.1 0.0 all-gather.4.cloned.1.call-update
  9.2 13.8 %student_keys.1 = (f32[4,512,8]{2,1,0:T(8,128)}, f32[4,1,512]{2,1,0:T(1,128)}, bf16[4,512,128]{2,1,0:T(8,128)(2,1)}, bf16[4,512,128]{2,1,0:T(8,128)(2,1)}, bf16[...) custom-call(bf16[512,128]{1,0:T(8,128)(2,1)} %copy-done.15, ...), custom_call_target="tpu_custom_call" | custom-call | flops 17600000000 | tf_op jit(solution)/shard_map/student_keys/pallas_call | solution.py:289
  23.0 6.4 %all-to-all-start = ((f32[8,192,128]{2,1,0:T(8,128)}), f32[8,192,128]{2,1,0:T(8,128)S(1)}, u32[]{:S(2)}, u32[]{:S(2)}) async-start(f32[8,192,128]{2,1,0:T(8,128)} %get-tuple-element.64), calls=%async_computation | async-start | bytes 1572864 | tf_op jit(solution)/shard_map/all_to_all | solution.py:779
  29.4 8.1 %student_queries.1 = (f32[4,512,8]{2,1,0:T(8,128)}, bf16[4,512,128]{2,1,0:T(8,128)(2,1)}, bf16[4,512,128]{2,1,0:T(8,128)(2,1)}, bf16[4,256,640]{2,1,0:T(8,128)(2...) custom-call(bf16[512,512]{1,0:T(8,128)(2,1)} %q_ref.7, ...), custom_call_target="tpu_custom_call" | custom-call | flops 8800000000 | tf_op jit(solution)/shard_map/student_queries/pallas_call | solution.py:335
  37.4 11.3 %all-to-all-done.message_ref = f32[8,192,128]{2,1,0:T(8,128)S(1)} async-done(((f32[8,192,128]{2,1,0:T(8,128)}), f32[8,192,128]{2,1,0:T(8,128)S(1)}, u32[]{:S(2)}, u32[]{:S(2)}) %all-to-all-start) | async-done | bytes 786464 | tf_op jit(solution)/shard_map/all_to_all | solution.py:779
  48.7 1.6 state_chain.1
  50.3 3.5 %all-to-all-start.1 = ((f32[8,64,128]{2,1,0:T(8,128)}), f32[8,64,128]{2,1,0:T(8,128)S(1)}, u32[]{:S(2)}, u32[]{:S(2)}) async-start(f32[8,64,128]{2,1,0:T(8,128)} %state_chain.1), calls=%async_computation.1 | async-start | bytes 524288 | tf_op jit(solution)/shard_map/all_to_all | solution.py:779
  53.8 6.5 %all-gather.4.cloned.1.call-done.kv_ref = bf16[4096,256]{1,0:T(8,128)(2,1)} async-done(((bf16[512,256]{1,0:T(8,128)(2,1)}), bf16[4096,256]{1,0:T(8,128)(2,1)}) %all-gather.4.cloned.1.call-update) | async-done | bytes 2097168 | tf_op jit(solution)/shard_map/all_gather | solution.py:789
  60.3 1.6 copy-done.1
  61.9 0.8 teacher_0.1.teacher_ref
  62.7 0.4 copy-done.5
  63.1 0.1 copy-done.7
  63.2 1.0 copy-done.10
  64.3 0.7 delta_0.1.mine_ref
  65.0 0.1 collective-permute-start
  65.1 1.9 collective-permute-done.other_ref
  67.0 7.4 %difference_part_0.1 = f32[8,264,512]{2,1,0:T(8,128)S(1)} custom-call(s32[1]{0:T(128)} %bitcast.core_ref, bf16[2,256,512]{2,1,0:T(8,128)(2,1)S(1)} %delta_0.1.mine_ref, bf16[2,256,512]{2,1,0:T(8,128)(2,1)S(1)} %collective-permute-done.other_ref, bf16[512,8192]{1,0:T(8,128)(2,1)} %w_mine_ref.5, bf16[512,8192]{1,0:T(8,128)(2,1)} %collective-permute-done.1.w_other_ref), custom_call_target="tpu_custom_call" | custom-call | flops 7699999744 | tf_op jit(solution)/shard_map/difference_part_0/pallas_call | solution.py:545
  74.5 1.9 convert_element_type.43
  76.3 7.0 %all-to-all-start.2 = ((f16[8,264,512]{2,1,0:T(8,128)(2,1)}), f16[8,264,512]{2,1,0:T(8,128)(2,1)}, u32[]{:S(2)}, u32[]{:S(2)}) async-start(f16[8,264,512]{2,1,0:T(8,128)(2,1)} %convert_element_type.43), calls=%async_computation.2 | async-start | bytes 4325376 | tf_op jit(solution)/shard_map/all_to_all | solution.py:779
  83.3 1.0 copy-done.4
  84.3 1.1 teacher_1.1.teacher_ref
  85.4 0.1 copy-done.6
  85.6 0.1 copy-done.8
  85.7 0.2 copy-done.11
  85.8 0.7 delta_1.1.mine_ref
  86.6 0.1 collective-permute-start.2
  86.7 1.9 collective-permute-done.2.other_ref
  88.6 7.4 %difference_part_1.1 = f32[8,264,512]{2,1,0:T(8,128)S(1)} custom-call(s32[1]{0:T(128)} %bitcast.core_ref, bf16[2,256,512]{2,1,0:T(8,128)(2,1)S(1)} %delta_1.1.mine_ref, bf16[2,256,512]{2,1,0:T(8,128)(2,1)S(1)} %collective-permute-done.2.other_ref, bf16[512,8192]{1,0:T(8,128)(2,1)} %w_mine_ref.5, bf16[512,8192]{1,0:T(8,128)(2,1)} %collective-permute-done.1.w_other_ref), custom_call_target="tpu_custom_call" | custom-call | flops 7699999744 | tf_op jit(solution)/shard_map/difference_part_1/pallas_call | solution.py:545
  96.0 1.9 convert_element_type.46
  97.9 14.9 %all-to-all-done.2 = f16[8,264,512]{2,1,0:T(8,128)(2,1)} async-done(((f16[8,264,512]{2,1,0:T(8,128)(2,1)}), f16[8,264,512]{2,1,0:T(8,128)(2,1)}, u32[]{:S(2)}, u32[]{:S(2)}) %all-to-all-start.2) | async-done | bytes 2162720 | tf_op jit(solution)/shard_map/all_to_all | solution.py:779
  112.8 7.6 %all-to-all-start.3 = ((f16[8,264,512]{2,1,0:T(8,128)(2,1)}), f16[8,264,512]{2,1,0:T(8,128)(2,1)S(1)}, u32[]{:S(2)}, u32[]{:S(2)}) async-start(f16[8,264,512]{2,1,0:T(8,128)(2,1)} %convert_element_type.46), calls=%async_computation.3 | async-start | bytes 4325376 | tf_op jit(solution)/shard_map/all_to_all | solution.py:779
  120.4 11.2 %backward_ready.1 = (bf16[4,512,128]{2,1,0:T(8,128)(2,1)}, bf16[4,512,128]{2,1,0:T(8,128)(2,1)}, bf16[4,512,128]{2,1,0:T(8,128)(2,1)}, bf16[4,512,128]{2,1,0:T(8...) custom-call(bf16[4,512,256]{2,1,0:T(8,128)(2,1)} %get-tuple-element.70.xh_ref, ...), custom_call_target="tpu_custom_call" | custom-call | flops 11000000512 | tf_op jit(solution)/shard_map/backward_ready/pallas_call | solution.py:517
  131.6 0.9 fusion.1
  132.5 0.9 multiply_exponential_fusion.2
  133.4 2.1 multiply_reduce_fusion.1
  135.6 13.1 %all-to-all-done.3 = f16[8,264,512]{2,1,0:T(8,128)(2,1)S(1)} async-done(((f16[8,264,512]{2,1,0:T(8,128)(2,1)}), f16[8,264,512]{2,1,0:T(8,128)(2,1)S(1)}, u32[]{:S(2)}, u32[]{:S(2)}) %all-to-all-start.3) | async-done | bytes 2162720 | tf_op jit(solution)/shard_map/all_to_all | solution.py:779
  148.8 0.4 multiply_reduce_fusion
  149.3 0.2 pad_maximum_fusion
  149.5 49.1 %all-gather.5 = f16[4224,512]{1,0:T(8,128)(2,1)} all-gather(f16[528,512]{1,0:T(8,128)(2,1)S(1)} %pad_maximum_fusion), channel_id=2, replica_groups={{0,2,4,6,8,10,12,14},{1,3,5,7,9,11,13,15},{16,18,20,22,24,26,28,30},{17..., dimensions={0}, use_global_device_ids=true | all-gather | bytes 4866048 | tf_op jit(solution)/shard_map/all_gather | solution.py:823
  198.6 0.9 slice.36
  199.6 4.8 %subtract_convert_fusion = (bf16[8,528,512]{2,1,0:T(8,128)(2,1)}, bf16[8,528,512]{2,1,0:T(8,128)(2,1)S(1)}) fusion(f16[8,528,512]{2,1,0:T(8,128)(2,1)} %bitcast.26, f32[8,512]{1,0:T(8,128)S(1)} %bitcast.28, f32[8,512]{1,0:T(8,128)S(1)} %bitcast.29, pred[528]{0:T(1024)(128)(4,1)S(1)} %iota_compare_fusion), kind=kLoop, calls=%fused_computation | loop fusion | flops 15138816 | bytes 13009424 | tf_op jit(solution)/shard_map/convert_element_type | solution.py:52
  204.4 13.4 %head_grad_part.1 = (f32[512,512]{1,0:T(8,128)S(1)}, f32[520,512]{1,0:T(8,128)S(1)}, f32[8,512]{1,0:T(8,128)S(1)}) custom-call(s32[1]{0:T(128)} %bitcast.core_ref, bf16[8,528,512]{2,1,0:T(8,128)(2,1)S(1)} %get-tuple-element.126.high_ref, bf16[8,528,512]{2,1,0:T(8,128)(2,1)} %get-tuple-element.125.low_ref, bf16[512,8192]{1,0:T(8,128)(2,1)} %w_mine_ref.5, ...), custom_call_target="tpu_custom_call" | custom-call | flops 15399999488 | tf_op jit(solution)/shard_map/head_grad_part/pallas_call | solution.py:594
  217.9 0.1 collective-permute-start.3
  218.0 2.7 collective-permute-done.3.other_ref
  220.7 1.6 state_grad_local.1
  222.3 0.8 copy-done.13
  223.0 0.8 copy-done.14
  223.9 10.9 %all-to-all-start.4 = ((f32[8,64,128]{2,1,0:T(8,128)}), f32[8,64,128]{2,1,0:T(8,128)S(1)}, u32[]{:S(2)}, u32[]{:S(2)}) async-start(f32[8,64,128]{2,1,0:T(8,128)} %bitcast.6), calls=%async_computation.4 | async-start | bytes 524288 | tf_op jit(solution)/shard_map/all_to_all | solution.py:779
  234.8 7.9 %query_grad.1 = (f32[4,128,128]{2,1,0:T(8,128)}, f32[4,512,128]{2,1,0:T(8,128)}) custom-call(bf16[512,512]{1,0:T(8,128)(2,1)} %copy-done.13, bf16[512,512]{1,0:T(8,128)(2,1)} %copy-done.14, bf16[4,512,128]{2,1,0:T(8,128)(2,1)} %get-tuple-element.109.nh_ref, bf16[4,512,128]{2,1,0:T(8,128)(2,1)} %get-tuple-element.110.nl_ref, ...), custom_call_target="tpu_custom_call" | custom-call | flops 8800000000 | tf_op jit(solution)/shard_map/query_grad/pallas_call | solution.py:704
  242.7 1.6 state_grad_chain.1
  244.3 5.7 %all-to-all-start.5 = ((f32[8,64,128]{2,1,0:T(8,128)}), f32[8,64,128]{2,1,0:T(8,128)S(1)}, u32[]{:S(2)}, u32[]{:S(2)}) async-start(f32[8,64,128]{2,1,0:T(8,128)} %state_grad_chain.1), calls=%async_computation.5 | async-start | bytes 524288 | tf_op jit(solution)/shard_map/all_to_all | solution.py:779
  250.0 3.4 %update_grad_local.1.y_ref = f32[4,512,128]{2,1,0:T(8,128)} custom-call(bf16[512,512]{1,0:T(8,128)(2,1)} %copy-done.13, bf16[512,512]{1,0:T(8,128)(2,1)} %copy-done.14, bf16[4,256,640]{2,1,0:T(8,128)(2,1)} %get-tuple-element.119.bh_ref, bf16[4,256,640]{2,1,0:T(8,128)(2,1)} %get-tuple-element.120.bl_ref), custom_call_target="tpu_custom_call" | custom-call | flops 4400000000 | tf_op jit(solution)/shard_map/update_grad_local/pallas_call | solution.py:664
  253.5 3.8 %all-to-all-done.5 = f32[8,64,128]{2,1,0:T(8,128)S(1)} async-done(((f32[8,64,128]{2,1,0:T(8,128)}), f32[8,64,128]{2,1,0:T(8,128)S(1)}, u32[]{:S(2)}, u32[]{:S(2)}) %all-to-all-start.5) | async-done | bytes 262176 | tf_op jit(solution)/shard_map/all_to_all | solution.py:779
  257.3 0.7 copy-done.17
  258.0 7.9 %key_grad.1 = f32[4,128,128]{2,1,0:T(8,128)} custom-call(f32[4,512,128]{2,1,0:T(8,128)} %update_grad_local.1.y_ref, bf16[4,512,128]{2,1,0:T(8,128)(2,1)} %get-tuple-element.121.th_ref, bf16[4,512,128]{2,1,0:T(8,128)(2,1)} %get-tuple-element.122.tl_ref, bf16[4,512,128]{2,1,0:T(8,128)(2,1)} %get-tuple-element.109.nh_ref, ...), custom_call_target="tpu_custom_call" | custom-call | flops 9900000256 | tf_op jit(solution)/shard_map/key_grad/pallas_call | solution.py:748
  265.9 1.0 maximum_maximum_fusion
  266.8 11.7 %all_to_all.40 = f32[8,136,128]{2,1,0:T(8,128)S(1)} all-to-all(f32[8,136,128]{2,1,0:T(8,128)S(1)} %maximum_maximum_fusion), channel_id=1, replica_groups=mesh['ctx'=8,'head'=16] {'ctx'}, dimensions={0} | all-to-all | bytes 1114112 | tf_op jit(solution)/shard_map/all_to_all | solution.py:779
  278.6 11.4 %all_to_all.41 = f32[8,136,128]{2,1,0:T(8,128)S(1)} all-to-all(f32[8,136,128]{2,1,0:T(8,128)S(1)} %broadcast_in_dim.44), channel_id=1, replica_groups=mesh['ctx'=8,'head'=16] {'ctx'}, dimensions={0} | all-to-all | bytes 1114112 | tf_op jit(solution)/shard_map/all_to_all | solution.py:779
  290.0 0.6 slice_reduce_fusion
  291.3 0.8 fusion.4
  (47 shorter events, 0.4 us)
Async XLA Ops:
  7.2 53.1 %all-gather.4.cloned.1.call-start = ((), (), s32[]{:S(2)}) async-start(), calls=%async_computation.8 | async-start | bytes 2359296 | tf_op jit(solution)/shard_map/all_gather | solution.py:789
  7.2 59.8 %collective-permute-start.1 = (bf16[512,8192]{1,0:T(8,128)(2,1)}, bf16[512,8192]{1,0:T(8,128)(2,1)}, u32[]{:S(2)}, u32[]{:S(2)}) collective-permute-start(bf16[512,8192]{1,0:T(8,128)(2,1)} %w_mine_ref.5), channel_id=1, source_target_pairs={{0,1},{1,0},{2,3},{3,2},{4,5},{5,4},{6,7},{7,6},{8,9},{9,8},{10,11... | collective-permute-start | bytes 25165832 | tf_op jit(solution)/shard_map/ppermute | solution.py:793
  8.3 0.8 copy-start.15
  8.3 0.8 copy-start.16
  23.0 25.8 %all-to-all-start = ((f32[8,192,128]{2,1,0:T(8,128)}), f32[8,192,128]{2,1,0:T(8,128)S(1)}, u32[]{:S(2)}, u32[]{:S(2)}) async-start(f32[8,192,128]{2,1,0:T(8,128)} %get-tuple-element.64), calls=%async_computation | async-start | bytes 1572864 | tf_op jit(solution)/shard_map/all_to_all | solution.py:779
  48.7 11.6 %copy-start.3 = (bf16[512,512]{1,0:T(8,128)(2,1)S(1)}, bf16[512,512]{1,0:T(8,128)(2,1)}, u32[]{:S(2)}) copy-start(bf16[512,512]{1,0:T(8,128)(2,1)} %q_ref.7) | copy-start | bytes 1572868
  50.3 12.3 %all-to-all-start.1 = ((f32[8,64,128]{2,1,0:T(8,128)}), f32[8,64,128]{2,1,0:T(8,128)S(1)}, u32[]{:S(2)}, u32[]{:S(2)}) async-start(f32[8,64,128]{2,1,0:T(8,128)} %state_chain.1), calls=%async_computation.1 | async-start | bytes 524288 | tf_op jit(solution)/shard_map/all_to_all | solution.py:779
  60.3 1.6 copy-start.1
  61.9 1.2 copy-start.5
  61.9 1.4 copy-start.7
  62.7 22.7 %copy-start = (f32[8,64,128]{2,1,0:T(8,128)}, f32[8,64,128]{2,1,0:T(8,128)S(1)}, u32[]{:S(2)}) copy-start(f32[8,64,128]{2,1,0:T(8,128)S(1)} %all-to-all-done.1) | copy-start | bytes 786436
  63.2 1.0 copy-start.10
  65.0 2.0 collective-permute-start
  74.5 8.8 %copy-start.2 = (bf16[4096,256]{1,0:T(8,128)(2,1)S(1)}, bf16[4096,256]{1,0:T(8,128)(2,1)}, u32[]{:S(2)}) copy-start(bf16[4096,256]{1,0:T(8,128)(2,1)} %all-gather.4.cloned.1.call-done.kv_ref) | copy-start | bytes 6291460
  76.3 36.5 %all-to-all-start.2 = ((f16[8,264,512]{2,1,0:T(8,128)(2,1)}), f16[8,264,512]{2,1,0:T(8,128)(2,1)}, u32[]{:S(2)}, u32[]{:S(2)}) async-start(f16[8,264,512]{2,1,0:T(8,128)(2,1)} %convert_element_type.43), calls=%async_computation.2 | async-start | bytes 4325376 | tf_op jit(solution)/shard_map/all_to_all | solution.py:779
  83.3 1.0 copy-start.4
  84.3 1.2 copy-start.6
  84.3 1.4 copy-start.8
  84.3 1.5 copy-start.11
  86.6 2.0 collective-permute-start.2
  112.8 35.8 %all-to-all-start.3 = ((f16[8,264,512]{2,1,0:T(8,128)(2,1)}), f16[8,264,512]{2,1,0:T(8,128)(2,1)S(1)}, u32[]{:S(2)}, u32[]{:S(2)}) async-start(f16[8,264,512]{2,1,0:T(8,128)(2,1)} %convert_element_type.46), calls=%async_computation.3 | async-start | bytes 4325376 | tf_op jit(solution)/shard_map/all_to_all | solution.py:779
  204.4 16.2 %copy-start.9 = (bf16[4,512,128]{2,1,0:T(8,128)(2,1)S(1)}, bf16[4,512,128]{2,1,0:T(8,128)(2,1)}, u32[]{:S(2)}) copy-start(bf16[4,512,128]{2,1,0:T(8,128)(2,1)} %get-tuple-element.74.rh_ref) | copy-start | bytes 1572868
  204.4 16.2 %copy-start.12 = (bf16[4,512,128]{2,1,0:T(8,128)(2,1)S(1)}, bf16[4,512,128]{2,1,0:T(8,128)(2,1)}, u32[]{:S(2)}) copy-start(bf16[4,512,128]{2,1,0:T(8,128)(2,1)} %get-tuple-element.75.rl_ref) | copy-start | bytes 1572868
  217.9 2.8 collective-permute-start.3
  222.3 0.8 copy-start.13
  223.0 0.8 copy-start.14
  223.9 18.8 %all-to-all-start.4 = ((f32[8,64,128]{2,1,0:T(8,128)}), f32[8,64,128]{2,1,0:T(8,128)S(1)}, u32[]{:S(2)}, u32[]{:S(2)}) async-start(f32[8,64,128]{2,1,0:T(8,128)} %bitcast.6), calls=%async_computation.4 | async-start | bytes 524288 | tf_op jit(solution)/shard_map/all_to_all | solution.py:779
  244.3 12.9 %all-to-all-start.5 = ((f32[8,64,128]{2,1,0:T(8,128)}), f32[8,64,128]{2,1,0:T(8,128)S(1)}, u32[]{:S(2)}, u32[]{:S(2)}) async-start(f32[8,64,128]{2,1,0:T(8,128)} %state_grad_chain.1), calls=%async_computation.5 | async-start | bytes 524288 | tf_op jit(solution)/shard_map/all_to_all | solution.py:779
  257.3 0.7 copy-start.17
  258.0 7.9 %copy-start.18 = (f32[4,128,128]{2,1,0:T(8,128)S(1)}, f32[4,128,128]{2,1,0:T(8,128)}, u32[]{:S(2)}) copy-start(f32[4,128,128]{2,1,0:T(8,128)} %get-tuple-element.114) | copy-start | bytes 786436
Sparse Core Ops, SparseCore 0:
  10.2 50.0 all-gather.3

commit v4 on v3

--- a/solution.py
+++ b/solution.py
@@ -565,13 +565,16 @@
 def back_project_kernel(
     core_ref, high_ref, low_ref, w_mine_ref, w_other_ref, mine_ref, other_ref, square_ref
 ):
-    both = jnp.concatenate([high_ref[0, :ROWS, :], low_ref[0, :ROWS, :]], axis=0)
-    mine = mm(both, w_mine_ref[...], NT)
-    other = mm(both, w_other_ref[...], NT)
+    mine = other = square = 0.0
+    for p in range(PSTEP):
+        at = slice(PIECE * p, PIECE * (p + 1))
+        both = jnp.concatenate([high_ref[p, :ROWS, :], low_ref[p, :ROWS, :]], axis=0)
+        mine = mine + mm(both, w_mine_ref[:, at], NT)
+        other = other + mm(both, w_other_ref[:, at], NT)
+        values = both[:ROWS].astype(f32) + both[ROWS:].astype(f32)
+        square = square + jnp.sum((values * values).reshape(ROWS // 8, 8, PIECE), axis=0)
     mine = mine[:ROWS] + mine[ROWS:]
     other = other[:ROWS] + other[ROWS:]
-    values = both[:ROWS].astype(f32) + both[ROWS:].astype(f32)
-    square = jnp.sum((values * values).reshape(ROWS // 8, 8, PIECE), axis=0)
 
     @pl.when(pl.program_id(0) == 0)
     def _():
@@ -590,17 +593,17 @@
 
 def back_project(core, high, low, w_mine, w_other):
     width = HEADS * HD
-    columns = pl.BlockSpec((1, ROWS + 2 * PAD, PIECE), lambda j, c: (j, 0, 0))
+    columns = pl.BlockSpec((PSTEP, ROWS + 2 * PAD, PIECE), lambda j, c: (j, 0, 0))
     return pl.pallas_call(
         back_project_kernel,
         grid_spec=pltpu.PrefetchScalarGridSpec(
             num_scalar_prefetch=1,
-            grid=(CHIPS,),
+            grid=(CHIPS // PSTEP,),
             in_specs=[
                 columns,
                 columns,
-                pl.BlockSpec((width, PIECE), lambda j, c: (0, c[0] * CHIPS + j)),
-                pl.BlockSpec((width, PIECE), lambda j, c: (0, c[0] * CHIPS + j)),
+                pl.BlockSpec((width, PSTEP * PIECE), lambda j, c: (0, c[0] * (CHIPS // PSTEP) + j)),
+                pl.BlockSpec((width, PSTEP * PIECE), lambda j, c: (0, c[0] * (CHIPS // PSTEP) + j)),
             ],
             out_specs=[
                 pl.BlockSpec((ROWS, width), lambda j, c: (0, 0)),
@@ -769,10 +772,10 @@
 
 
 def rescaled(message):
-    exponent = message[:, -2 * PAD :: PAD, :].astype(f32)
     at = lax.broadcasted_iota(jnp.int32, message.shape, 1)
-    scale = jnp.exp2(-exponent)
-    return message.astype(f32) * jnp.where(at < HALF, scale[:, :1], scale[:, 1:])
+    first, second = message[:, ROWS : ROWS + 1, :], message[:, ROWS + PAD : ROWS + PAD + 1, :]
+    exponent = jnp.where(at < HALF, first, second).astype(f32)
+    return message.astype(f32) * jnp.exp2(-exponent)
 
 
 def transpose_over(x, axis, groups=None):

time: 302 us -> 297 us (0.983)
  no operation moved by 1% of the time
where the time goes in v4:
time: 297 us; the launch traced here: 295 us
  Pallas kernels  87.6 us (29%)
  blocking collectives  70.4 us (24%)
  waiting for transfers between devices  55.8 us (19%)
  starting transfers between devices  41.5 us (14%)
  between operations  16.2 us (5%)
  other arithmetic  14.9 us (5%)
  local copies, waits for them, and re-layouts  8.96 us (3%)
    all_gather x1, blocking collectives, shards(): lax.all_gather(jnp.concatenate([first[0], second[0], first[1], second[1]]...  47.3 us
    all_to_all x6, waiting for transfers between devices, transpose_over(): return lax.all_to_all(x, axis, 0, 0, axis_index_groups=groups, tiled=True)  43.2 us
    all_to_all x6, starting transfers between devices, transpose_over(): return lax.all_to_all(x, axis, 0, 0, axis_index_groups=groups, tiled=True)  41.1 us
    all_to_all x2, blocking collectives, transpose_over(): return lax.all_to_all(x, axis, 0, 0, axis_index_groups=groups, tiled=True)  23.1 us
    pallas_call x2, Pallas kernels, project(): pl.pallas_call(project_kernel, grid_spec=pltpu.PrefetchScalarGridSpec(num...  14.9 us
    pallas_call x1, Pallas kernels, student_keys(): heads_call(keys_kernel, 'student_keys', 16, [whole(ROWS, HD), whole(ROWS,...  13.9 us
    pallas_call x1, Pallas kernels, back_project(): pl.pallas_call(back_project_kernel, grid_spec=pltpu.PrefetchScalarGridSpe...  12.2 us
    pallas_call x1, Pallas kernels, student_ready(): heads_call(ready_kernel, 'backward_ready', 10, [per_head(ROWS, 2 * HD), p...  11.2 us
  transfers between devices with their start and end apart: 11, of which 8 were waited for; matrix products, arithmetic and copies ran while one was open for 3% of the time, Pallas kernels for 19%

profile of v4, /device:TPU:0, one launch (start us, length us, event | category | flops | bytes accessed | tf_op | source)
XLA Modules:
  0.0 295.5 jit_solution(12882675487872341253)
XLA Ops:
  7.2 0.0 all-gather.4.cloned.1.call-start
  7.2 0.1 collective-permute-start.1
  7.3 1.0 constant_dynamic-slice_fusion
  8.3 0.0 copy-start.16
  8.3 0.8 pad_maximum_fusion.1
  9.1 0.0 all-gather.4.cloned.1.call-update
  9.2 13.9 %student_keys.1 = (f32[4,512,8]{2,1,0:T(8,128)}, f32[4,1,512]{2,1,0:T(1,128)}, bf16[4,512,128]{2,1,0:T(8,128)(2,1)}, bf16[4,512,128]{2,1,0:T(8,128)(2,1)}, bf16[...) custom-call(bf16[512,128]{1,0:T(8,128)(2,1)} %copy-done.15, ...), custom_call_target="tpu_custom_call" | custom-call | flops 17600000000 | tf_op jit(solution)/shard_map/student_keys/pallas_call | solution.py:289
  23.1 6.4 %all-to-all-start = ((f32[8,192,128]{2,1,0:T(8,128)}), f32[8,192,128]{2,1,0:T(8,128)S(1)}, u32[]{:S(2)}, u32[]{:S(2)}) async-start(f32[8,192,128]{2,1,0:T(8,128)} %get-tuple-element.64), calls=%async_computation | async-start | bytes 1572864 | tf_op jit(solution)/shard_map/all_to_all | solution.py:782
  29.5 8.1 %student_queries.1 = (f32[4,512,8]{2,1,0:T(8,128)}, bf16[4,512,128]{2,1,0:T(8,128)(2,1)}, bf16[4,512,128]{2,1,0:T(8,128)(2,1)}, bf16[4,256,640]{2,1,0:T(8,128)(2...) custom-call(bf16[512,512]{1,0:T(8,128)(2,1)} %q_ref.7, ...), custom_call_target="tpu_custom_call" | custom-call | flops 8800000000 | tf_op jit(solution)/shard_map/student_queries/pallas_call | solution.py:335
  37.7 11.4 %all-to-all-done.message_ref = f32[8,192,128]{2,1,0:T(8,128)S(1)} async-done(((f32[8,192,128]{2,1,0:T(8,128)}), f32[8,192,128]{2,1,0:T(8,128)S(1)}, u32[]{:S(2)}, u32[]{:S(2)}) %all-to-all-start) | async-done | bytes 786464 | tf_op jit(solution)/shard_map/all_to_all | solution.py:782
  49.0 1.6 state_chain.1
  50.6 3.4 %all-to-all-start.1 = ((f32[8,64,128]{2,1,0:T(8,128)}), f32[8,64,128]{2,1,0:T(8,128)S(1)}, u32[]{:S(2)}, u32[]{:S(2)}) async-start(f32[8,64,128]{2,1,0:T(8,128)} %state_chain.1), calls=%async_computation.1 | async-start | bytes 524288 | tf_op jit(solution)/shard_map/all_to_all | solution.py:782
  54.1 6.2 %all-gather.4.cloned.1.call-done.kv_ref = bf16[4096,256]{1,0:T(8,128)(2,1)} async-done(((bf16[512,256]{1,0:T(8,128)(2,1)}), bf16[4096,256]{1,0:T(8,128)(2,1)}) %all-gather.4.cloned.1.call-update) | async-done | bytes 2097168 | tf_op jit(solution)/shard_map/all_gather | solution.py:792
  60.2 1.6 copy-done.1
  61.8 0.8 teacher_0.1.teacher_ref
  62.6 0.4 copy-done.5
  63.1 0.1 copy-done.7
  63.2 1.0 copy-done.10
  64.2 0.7 delta_0.1.mine_ref
  65.0 0.1 collective-permute-start
  65.1 1.9 collective-permute-done.other_ref
  67.0 7.4 %difference_part_0.1 = f32[8,264,512]{2,1,0:T(8,128)S(1)} custom-call(s32[1]{0:T(128)} %bitcast.core_ref, bf16[2,256,512]{2,1,0:T(8,128)(2,1)S(1)} %delta_0.1.mine_ref, bf16[2,256,512]{2,1,0:T(8,128)(2,1)S(1)} %collective-permute-done.other_ref, bf16[512,8192]{1,0:T(8,128)(2,1)} %w_mine_ref.5, bf16[512,8192]{1,0:T(8,128)(2,1)} %collective-permute-done.1.w_other_ref), custom_call_target="tpu_custom_call" | custom-call | flops 7699999744 | tf_op jit(solution)/shard_map/difference_part_0/pallas_call | solution.py:545
  74.4 1.9 convert_element_type.43
  76.3 7.0 %all-to-all-start.2 = ((f16[8,264,512]{2,1,0:T(8,128)(2,1)}), f16[8,264,512]{2,1,0:T(8,128)(2,1)}, u32[]{:S(2)}, u32[]{:S(2)}) async-start(f16[8,264,512]{2,1,0:T(8,128)(2,1)} %convert_element_type.43), calls=%async_computation.2 | async-start | bytes 4325376 | tf_op jit(solution)/shard_map/all_to_all | solution.py:782
  83.3 1.0 copy-done.4
  84.4 1.1 teacher_1.1.teacher_ref
  85.4 0.1 copy-done.6
  85.6 0.1 copy-done.8
  85.7 0.2 copy-done.11
  85.9 0.7 delta_1.1.mine_ref
  86.6 0.1 collective-permute-start.2
  86.7 1.9 collective-permute-done.2.other_ref
  88.6 7.4 %difference_part_1.1 = f32[8,264,512]{2,1,0:T(8,128)S(1)} custom-call(s32[1]{0:T(128)} %bitcast.core_ref, bf16[2,256,512]{2,1,0:T(8,128)(2,1)S(1)} %delta_1.1.mine_ref, bf16[2,256,512]{2,1,0:T(8,128)(2,1)S(1)} %collective-permute-done.2.other_ref, bf16[512,8192]{1,0:T(8,128)(2,1)} %w_mine_ref.5, bf16[512,8192]{1,0:T(8,128)(2,1)} %collective-permute-done.1.w_other_ref), custom_call_target="tpu_custom_call" | custom-call | flops 7699999744 | tf_op jit(solution)/shard_map/difference_part_1/pallas_call | solution.py:545
  96.0 1.9 convert_element_type.46
  98.0 14.9 %all-to-all-done.2 = f16[8,264,512]{2,1,0:T(8,128)(2,1)} async-done(((f16[8,264,512]{2,1,0:T(8,128)(2,1)}), f16[8,264,512]{2,1,0:T(8,128)(2,1)}, u32[]{:S(2)}, u32[]{:S(2)}) %all-to-all-start.2) | async-done | bytes 2162720 | tf_op jit(solution)/shard_map/all_to_all | solution.py:782
  112.9 7.6 %all-to-all-start.3 = ((f16[8,264,512]{2,1,0:T(8,128)(2,1)}), f16[8,264,512]{2,1,0:T(8,128)(2,1)S(1)}, u32[]{:S(2)}, u32[]{:S(2)}) async-start(f16[8,264,512]{2,1,0:T(8,128)(2,1)} %convert_element_type.46), calls=%async_computation.3 | async-start | bytes 4325376 | tf_op jit(solution)/shard_map/all_to_all | solution.py:782
  120.5 11.2 %backward_ready.1 = (bf16[4,512,128]{2,1,0:T(8,128)(2,1)}, bf16[4,512,128]{2,1,0:T(8,128)(2,1)}, bf16[4,512,128]{2,1,0:T(8,128)(2,1)}, bf16[4,512,128]{2,1,0:T(8...) custom-call(bf16[4,512,256]{2,1,0:T(8,128)(2,1)} %get-tuple-element.70.xh_ref, ...), custom_call_target="tpu_custom_call" | custom-call | flops 11000000512 | tf_op jit(solution)/shard_map/backward_ready/pallas_call | solution.py:517
  131.7 0.9 fusion.1
  132.6 0.9 multiply_exponential_fusion.1
  133.5 2.1 multiply_reduce_fusion.1
  135.7 13.0 %all-to-all-done.3 = f16[8,264,512]{2,1,0:T(8,128)(2,1)S(1)} async-done(((f16[8,264,512]{2,1,0:T(8,128)(2,1)}), f16[8,264,512]{2,1,0:T(8,128)(2,1)S(1)}, u32[]{:S(2)}, u32[]{:S(2)}) %all-to-all-start.3) | async-done | bytes 2162720 | tf_op jit(solution)/shard_map/all_to_all | solution.py:782
  148.8 0.4 multiply_reduce_fusion
  149.4 0.2 pad_maximum_fusion
  149.6 47.3 %all-gather.5 = f16[4224,512]{1,0:T(8,128)(2,1)S(1)} all-gather(f16[528,512]{1,0:T(8,128)(2,1)S(1)} %pad_maximum_fusion), channel_id=2, replica_groups={{0,2,4,6,8,10,12,14},{1,3,5,7,9,11,13,15},{16,18,20,22,24,26,28,30},{17..., dimensions={0}, use_global_device_ids=true | all-gather | bytes 4866048 | tf_op jit(solution)/shard_map/all_gather | solution.py:826
  196.9 4.0 %subtract_convert_fusion = (bf16[8,528,512]{2,1,0:T(8,128)(2,1)}, bf16[8,528,512]{2,1,0:T(8,128)(2,1)S(1)}) fusion(f16[8,528,512]{2,1,0:T(8,128)(2,1)S(1)} %bitcast.26, pred[528]{0:T(1024)(128)(4,1)S(1)} %iota_compare_fusion, f16[8,512]{1,0:T(8,128)(2,1)S(1)} %bitcast.30, f16[8,512]{1,0:T(8,128)(2,1)S(1)} %bitcast.31), kind=kLoop, calls=%fused_computation | loop fusion | flops 21626880 | bytes 12993040 | tf_op jit(solution)/shard_map/convert_element_type | solution.py:52
  201.0 12.2 %head_grad_part.1 = (f32[512,512]{1,0:T(8,128)S(1)}, f32[520,512]{1,0:T(8,128)S(1)}, f32[8,512]{1,0:T(8,128)S(1)}) custom-call(s32[1]{0:T(128)} %bitcast.core_ref, bf16[8,528,512]{2,1,0:T(8,128)(2,1)S(1)} %get-tuple-element.126.high_ref, bf16[8,528,512]{2,1,0:T(8,128)(2,1)} %get-tuple-element.125.low_ref, bf16[512,8192]{1,0:T(8,128)(2,1)} %w_mine_ref.5, ...), custom_call_target="tpu_custom_call" | custom-call | flops 15399999488 | tf_op jit(solution)/shard_map/head_grad_part/pallas_call | solution.py:597
  213.2 0.1 collective-permute-start.3
  213.3 2.7 collective-permute-done.3.other_ref
  216.0 1.6 state_grad_local.1
  217.6 0.8 copy-done.13
  218.4 0.8 copy-done.14
  219.2 10.9 %all-to-all-start.4 = ((f32[8,64,128]{2,1,0:T(8,128)}), f32[8,64,128]{2,1,0:T(8,128)S(1)}, u32[]{:S(2)}, u32[]{:S(2)}) async-start(f32[8,64,128]{2,1,0:T(8,128)} %bitcast.6), calls=%async_computation.4 | async-start | bytes 524288 | tf_op jit(solution)/shard_map/all_to_all | solution.py:782
  230.2 7.9 %query_grad.1 = (f32[4,128,128]{2,1,0:T(8,128)}, f32[4,512,128]{2,1,0:T(8,128)}) custom-call(bf16[512,512]{1,0:T(8,128)(2,1)} %copy-done.13, bf16[512,512]{1,0:T(8,128)(2,1)} %copy-done.14, bf16[4,512,128]{2,1,0:T(8,128)(2,1)} %get-tuple-element.109.nh_ref, bf16[4,512,128]{2,1,0:T(8,128)(2,1)} %get-tuple-element.110.nl_ref, ...), custom_call_target="tpu_custom_call" | custom-call | flops 8800000000 | tf_op jit(solution)/shard_map/query_grad/pallas_call | solution.py:707
  238.1 1.6 state_grad_chain.1
  239.7 5.7 %all-to-all-start.5 = ((f32[8,64,128]{2,1,0:T(8,128)}), f32[8,64,128]{2,1,0:T(8,128)S(1)}, u32[]{:S(2)}, u32[]{:S(2)}) async-start(f32[8,64,128]{2,1,0:T(8,128)} %state_grad_chain.1), calls=%async_computation.5 | async-start | bytes 524288 | tf_op jit(solution)/shard_map/all_to_all | solution.py:782
  245.4 3.4 %update_grad_local.1.y_ref = f32[4,512,128]{2,1,0:T(8,128)} custom-call(bf16[512,512]{1,0:T(8,128)(2,1)} %copy-done.13, bf16[512,512]{1,0:T(8,128)(2,1)} %copy-done.14, bf16[4,256,640]{2,1,0:T(8,128)(2,1)} %get-tuple-element.119.bh_ref, bf16[4,256,640]{2,1,0:T(8,128)(2,1)} %get-tuple-element.120.bl_ref), custom_call_target="tpu_custom_call" | custom-call | flops 4400000000 | tf_op jit(solution)/shard_map/update_grad_local/pallas_call | solution.py:667
  248.8 3.8 %all-to-all-done.5 = f32[8,64,128]{2,1,0:T(8,128)S(1)} async-done(((f32[8,64,128]{2,1,0:T(8,128)}), f32[8,64,128]{2,1,0:T(8,128)S(1)}, u32[]{:S(2)}, u32[]{:S(2)}) %all-to-all-start.5) | async-done | bytes 262176 | tf_op jit(solution)/shard_map/all_to_all | solution.py:782
  252.6 0.7 copy-done.17
  253.3 7.9 %key_grad.1 = f32[4,128,128]{2,1,0:T(8,128)} custom-call(f32[4,512,128]{2,1,0:T(8,128)} %update_grad_local.1.y_ref, bf16[4,512,128]{2,1,0:T(8,128)(2,1)} %get-tuple-element.121.th_ref, bf16[4,512,128]{2,1,0:T(8,128)(2,1)} %get-tuple-element.122.tl_ref, bf16[4,512,128]{2,1,0:T(8,128)(2,1)} %get-tuple-element.109.nh_ref, ...), custom_call_target="tpu_custom_call" | custom-call | flops 9900000256 | tf_op jit(solution)/shard_map/key_grad/pallas_call | solution.py:751
  261.2 1.0 maximum_maximum_fusion
  262.2 11.7 %all_to_all.40 = f32[8,136,128]{2,1,0:T(8,128)S(1)} all-to-all(f32[8,136,128]{2,1,0:T(8,128)S(1)} %maximum_maximum_fusion), channel_id=1, replica_groups=mesh['ctx'=8,'head'=16] {'ctx'}, dimensions={0} | all-to-all | bytes 1114112 | tf_op jit(solution)/shard_map/all_to_all | solution.py:782
  273.9 11.4 %all_to_all.41 = f32[8,136,128]{2,1,0:T(8,128)S(1)} all-to-all(f32[8,136,128]{2,1,0:T(8,128)S(1)} %broadcast_in_dim.44), channel_id=1, replica_groups=mesh['ctx'=8,'head'=16] {'ctx'}, dimensions={0} | all-to-all | bytes 1114112 | tf_op jit(solution)/shard_map/all_to_all | solution.py:782
  285.4 0.6 slice_reduce_fusion
  286.6 0.8 fusion.5
  (45 shorter events, 0.4 us)
Async XLA Ops:
  7.2 53.1 %all-gather.4.cloned.1.call-start = ((), (), s32[]{:S(2)}) async-start(), calls=%async_computation.8 | async-start | bytes 2359296 | tf_op jit(solution)/shard_map/all_gather | solution.py:792
  7.2 59.8 %collective-permute-start.1 = (bf16[512,8192]{1,0:T(8,128)(2,1)}, bf16[512,8192]{1,0:T(8,128)(2,1)}, u32[]{:S(2)}, u32[]{:S(2)}) collective-permute-start(bf16[512,8192]{1,0:T(8,128)(2,1)} %w_mine_ref.5), channel_id=1, source_target_pairs={{0,1},{1,0},{2,3},{3,2},{4,5},{5,4},{6,7},{7,6},{8,9},{9,8},{10,11... | collective-permute-start | bytes 25165832 | tf_op jit(solution)/shard_map/ppermute | solution.py:796
  8.3 0.8 copy-start.15
  8.3 0.8 copy-start.16
  23.1 25.9 %all-to-all-start = ((f32[8,192,128]{2,1,0:T(8,128)}), f32[8,192,128]{2,1,0:T(8,128)S(1)}, u32[]{:S(2)}, u32[]{:S(2)}) async-start(f32[8,192,128]{2,1,0:T(8,128)} %get-tuple-element.64), calls=%async_computation | async-start | bytes 1572864 | tf_op jit(solution)/shard_map/all_to_all | solution.py:782
  49.0 11.2 %copy-start.3 = (bf16[512,512]{1,0:T(8,128)(2,1)S(1)}, bf16[512,512]{1,0:T(8,128)(2,1)}, u32[]{:S(2)}) copy-start(bf16[512,512]{1,0:T(8,128)(2,1)} %q_ref.7) | copy-start | bytes 1572868
  50.6 12.0 %all-to-all-start.1 = ((f32[8,64,128]{2,1,0:T(8,128)}), f32[8,64,128]{2,1,0:T(8,128)S(1)}, u32[]{:S(2)}, u32[]{:S(2)}) async-start(f32[8,64,128]{2,1,0:T(8,128)} %state_chain.1), calls=%async_computation.1 | async-start | bytes 524288 | tf_op jit(solution)/shard_map/all_to_all | solution.py:782
  60.2 1.6 copy-start.1
  61.8 1.2 copy-start.5
  61.8 1.4 copy-start.7
  62.6 22.8 %copy-start = (f32[8,64,128]{2,1,0:T(8,128)}, f32[8,64,128]{2,1,0:T(8,128)S(1)}, u32[]{:S(2)}) copy-start(f32[8,64,128]{2,1,0:T(8,128)S(1)} %all-to-all-done.1) | copy-start | bytes 786436
  63.2 1.0 copy-start.10
  65.0 2.0 collective-permute-start
  74.4 8.9 %copy-start.2 = (bf16[4096,256]{1,0:T(8,128)(2,1)S(1)}, bf16[4096,256]{1,0:T(8,128)(2,1)}, u32[]{:S(2)}) copy-start(bf16[4096,256]{1,0:T(8,128)(2,1)} %all-gather.4.cloned.1.call-done.kv_ref) | copy-start | bytes 6291460
  76.3 36.6 %all-to-all-start.2 = ((f16[8,264,512]{2,1,0:T(8,128)(2,1)}), f16[8,264,512]{2,1,0:T(8,128)(2,1)}, u32[]{:S(2)}, u32[]{:S(2)}) async-start(f16[8,264,512]{2,1,0:T(8,128)(2,1)} %convert_element_type.43), calls=%async_computation.2 | async-start | bytes 4325376 | tf_op jit(solution)/shard_map/all_to_all | solution.py:782
  83.3 1.0 copy-start.4
  84.4 1.2 copy-start.6
  84.4 1.4 copy-start.8
  84.4 1.5 copy-start.11
  86.6 2.0 collective-permute-start.2
  112.9 35.9 %all-to-all-start.3 = ((f16[8,264,512]{2,1,0:T(8,128)(2,1)}), f16[8,264,512]{2,1,0:T(8,128)(2,1)S(1)}, u32[]{:S(2)}, u32[]{:S(2)}) async-start(f16[8,264,512]{2,1,0:T(8,128)(2,1)} %convert_element_type.46), calls=%async_computation.3 | async-start | bytes 4325376 | tf_op jit(solution)/shard_map/all_to_all | solution.py:782
  201.0 15.0 %copy-start.9 = (bf16[4,512,128]{2,1,0:T(8,128)(2,1)S(1)}, bf16[4,512,128]{2,1,0:T(8,128)(2,1)}, u32[]{:S(2)}) copy-start(bf16[4,512,128]{2,1,0:T(8,128)(2,1)} %get-tuple-element.74.rh_ref) | copy-start | bytes 1572868
  201.0 15.0 %copy-start.12 = (bf16[4,512,128]{2,1,0:T(8,128)(2,1)S(1)}, bf16[4,512,128]{2,1,0:T(8,128)(2,1)}, u32[]{:S(2)}) copy-start(bf16[4,512,128]{2,1,0:T(8,128)(2,1)} %get-tuple-element.75.rl_ref) | copy-start | bytes 1572868
  213.2 2.8 collective-permute-start.3
  217.6 0.8 copy-start.13
  218.4 0.8 copy-start.14
  219.2 18.8 %all-to-all-start.4 = ((f32[8,64,128]{2,1,0:T(8,128)}), f32[8,64,128]{2,1,0:T(8,128)S(1)}, u32[]{:S(2)}, u32[]{:S(2)}) async-start(f32[8,64,128]{2,1,0:T(8,128)} %bitcast.6), calls=%async_computation.4 | async-start | bytes 524288 | tf_op jit(solution)/shard_map/all_to_all | solution.py:782
  239.7 12.9 %all-to-all-start.5 = ((f32[8,64,128]{2,1,0:T(8,128)}), f32[8,64,128]{2,1,0:T(8,128)S(1)}, u32[]{:S(2)}, u32[]{:S(2)}) async-start(f32[8,64,128]{2,1,0:T(8,128)} %state_grad_chain.1), calls=%async_computation.5 | async-start | bytes 524288 | tf_op jit(solution)/shard_map/all_to_all | solution.py:782
  252.6 0.7 copy-start.17
  253.3 7.9 %copy-start.18 = (f32[4,128,128]{2,1,0:T(8,128)S(1)}, f32[4,128,128]{2,1,0:T(8,128)}, u32[]{:S(2)}) copy-start(f32[4,128,128]{2,1,0:T(8,128)} %get-tuple-element.114) | copy-start | bytes 786436
Sparse Core Ops, SparseCore 0:
  10.2 49.9 all-gather.3
